TPU v7x, 128 devices: a whole 4x4x4 slice. The times are simulated.
128 devices in a mesh: dp: 16 (over z, y), tensor: 8 (over x, core).
Axes of the slice: x: 4, y: 4, z: 4, core: 2. Of those that a mesh axis runs over, the one named last changes fastest.
Arguments:
- query: bfloat16 [32, 128, 8192], P('dp', None, 'tensor'), may hold values from -6 to 6
- image: bfloat16 [32, 512, 8192], P('dp', None, 'tensor'), may hold values from -6 to 6
- tiles: int32 [32], replicated, may hold values from 0 to 4, as said below
- image_slot: int32 [32], replicated, may hold values from 0 to 31, as said below
- key_weight_matrix: bfloat16 [8192, 1024], P('dp', 'tensor'), may hold values from -0.0625 to 0.0625
- value_weight_matrix: bfloat16 [8192, 1024], P('dp', 'tensor'), may hold values from -0.0625 to 0.0625
- query_gain: float32 [128], replicated, may hold values from 0.5 to 2
- key_gain: float32 [128], replicated, may hold values from 0.5 to 2
- gate: float32 [1], replicated, may hold values from 0.3 to 1.5
- cotangent: bfloat16 [32, 128, 8192], P('dp', None, 'tensor'), may hold values from -6 to 6
Outputs:
- context: bfloat16 [32, 128, 8192], P('dp', None, 'tensor')
- d_query: bfloat16 [32, 128, 8192], P('dp', None, 'tensor')
- d_w_key: float32 [8192, 1024], P('dp', 'tensor')
- d_w_value: float32 [8192, 1024], P('dp', 'tensor')
Inputs may be any that keep to these rules, and one draw needn't show every extreme that they name: Some sample has 4 tiles and some has none. image_slot is a permutation of the samples. Sample s sits at dp index s // 2; the image rows image_slot[s] sit at the same dp index or at the one that differs from it by half the dp axis, and of the two samples at one dp index at most one has its image at the other index.
All inputs are finite; a program needn't handle non-finite values.
Results may differ from a plain program's by a relative error of at most 0.02.
Values may be sent and summed in bfloat16 or wider, within the bound.
No kernel may reach another device: no remote copies, remote signals or barrier semaphores. Data moves between devices by JAX's collectives and lax.ppermute only.
A program may use at most 128 MiB of HBM per device.

v0:
```python
import jax
import jax.numpy as jnp
from jax import lax
from jax.sharding import PartitionSpec as P

TILE = 128


EPS = 1e-06


def swapped(shard, axis, distance):
    return lax.ppermute(shard, axis, [(i, i ^ 1 << distance) for i in range(lax.axis_size(axis))])


def rms_factor(values):
    return lax.rsqrt(jnp.mean(values * values, axis=-1, keepdims=True) + EPS)


def norm_back(values, norm_multiplier, gain, grad):
    weighted = grad * gain
    inner = jnp.sum(weighted * values, axis=-1, keepdims=True)
    return (
        norm_multiplier * weighted
        - values * (norm_multiplier * norm_multiplier * norm_multiplier) * inner / values.shape[-1]
    )


def choose(flag, local, remote, index):
    mine = lax.dynamic_index_in_dim(local, index, 0, keepdims=False)
    theirs = lax.dynamic_index_in_dim(remote, index, 0, keepdims=False)
    return jnp.where(flag, mine, theirs)


def attend(q_norm, keys, vals, cot, count, ratio):
    text_rows, kv_local, group, head_dim = q_norm.shape
    scale = head_dim ** (-0.5)

    def tile_scores(index):
        key_tile = lax.dynamic_slice_in_dim(keys, index * TILE, TILE, 0)
        val_tile = lax.dynamic_slice_in_dim(vals, index * TILE, TILE, 0)
        raw = (
            jnp.einsum("tkgd,skd->kgts", q_norm, key_tile, preferred_element_type=jnp.float32)
            * scale
        )
        return (jnp.exp(raw), key_tile, val_tile)

    def forward(index, carry):
        total, accum = carry
        expo, key_tile, val_tile = tile_scores(index)
        total = total + jnp.sum(expo, axis=-1, keepdims=True)
        accum = accum + jnp.einsum(
            "kgts,skd->tkgd",
            expo.astype(jnp.bfloat16),
            val_tile,
            preferred_element_type=jnp.float32,
        )
        return (total, accum)

    start = (
        jnp.zeros((kv_local, group, text_rows, 1), jnp.float32),
        jnp.zeros((text_rows, kv_local, group, head_dim), jnp.float32),
    )
    total, accum = lax.fori_loop(0, count, forward, start)
    total = total + (count == 0).astype(jnp.float32)
    total_rows = jnp.transpose(total[..., 0], (2, 0, 1))[..., None]
    attended = accum / total_rows
    d_att = ratio * cot.astype(jnp.float32)
    d_att_b = d_att.astype(jnp.bfloat16)
    scaled_b = (d_att / total_rows).astype(jnp.bfloat16)
    delta = jnp.transpose(jnp.sum(d_att * attended, axis=-1), (1, 2, 0))[..., None]

    def backward(index, carry):
        d_qn, d_keys, d_vals = carry
        expo, key_tile, val_tile = tile_scores(index)
        d_prob = jnp.einsum("tkgd,skd->kgts", d_att_b, val_tile, preferred_element_type=jnp.float32)
        d_score = (expo / total * (d_prob - delta)).astype(jnp.bfloat16)
        d_qn = d_qn + scale * jnp.einsum(
            "kgts,skd->tkgd", d_score, key_tile, preferred_element_type=jnp.float32
        )
        key_part = scale * jnp.einsum(
            "kgts,tkgd->skd", d_score, q_norm, preferred_element_type=jnp.float32
        )
        val_part = jnp.einsum(
            "kgts,tkgd->skd",
            expo.astype(jnp.bfloat16),
            scaled_b,
            preferred_element_type=jnp.float32,
        )
        d_keys = lax.dynamic_update_slice_in_dim(d_keys, key_part, index * TILE, 0)
        d_vals = lax.dynamic_update_slice_in_dim(d_vals, val_part, index * TILE, 0)
        return (d_qn, d_keys, d_vals)

    start = (
        jnp.zeros((text_rows, kv_local, group, head_dim), jnp.float32),
        jnp.zeros(keys.shape, jnp.float32),
        jnp.zeros(vals.shape, jnp.float32),
    )
    d_qn, d_keys, d_vals = lax.fori_loop(0, count, backward, start)
    return (ratio * attended, d_qn, d_keys, d_vals)


def per_device(
    query,
    image,
    tiles,
    image_slot,
    key_weight_matrix,
    value_weight_matrix,
    query_gain,
    key_gain,
    gate,
    cotangent,
):
    head_dim = query_gain.shape[0]
    samp_local = query.shape[0]
    text_rows = query.shape[1]
    kv_cols = key_weight_matrix.shape[1]
    kv_local = kv_cols // head_dim
    group = query.shape[2] // kv_cols
    img_rows = image.shape[1]
    tile_total = img_rows // TILE
    ratio = jnp.tanh(gate[0])
    top_bit = (lax.axis_size("dp") // 2).bit_length() - 1
    rank = lax.axis_index("dp")
    first = rank * samp_local
    local_ids = first + jnp.arange(samp_local, dtype=jnp.int32)
    every = jnp.arange(tiles.shape[0], dtype=jnp.int32)
    match = image_slot[None, :] == local_ids[:, None]
    slot_sample = jnp.sum(jnp.where(match, every[None, :], 0), axis=1)
    home_tiles = lax.dynamic_slice_in_dim(tiles, first, samp_local)
    home_slot = lax.dynamic_slice_in_dim(image_slot, first, samp_local)
    key_rows, value_rows = (
        lax.all_gather(key_weight_matrix, "dp", axis=0, tiled=True),
        lax.all_gather(value_weight_matrix, "dp", axis=0, tiled=True),
    )
    w_both = jnp.concatenate([key_rows, value_rows], axis=1)
    width = w_both.shape[0]
    projected = []
    kept = []
    for slot in range(samp_local):
        proj_parts = []
        feat_parts = []
        for index in range(tile_total):
            part = image[slot, index * TILE : (index + 1) * TILE]
            full = lax.all_gather(part, "tensor", axis=1, tiled=True)
            proj_parts.append(jnp.dot(full, w_both, preferred_element_type=jnp.float32))
            feat_parts.append(full)
        projected.append(jnp.concatenate(proj_parts, axis=0))
        kept.append(feat_parts)
    projected = jnp.stack(projected)
    kraw = projected[..., :kv_cols].reshape(samp_local, img_rows, kv_local, head_dim)
    key_factor = rms_factor(kraw)
    keys = (kraw * key_factor * key_gain).astype(jnp.bfloat16)
    vals = (
        projected[..., kv_cols:]
        .astype(jnp.bfloat16)
        .reshape(samp_local, img_rows, kv_local, head_dim)
    )
    q_raw = query.astype(jnp.float32).reshape(samp_local, text_rows, kv_local, group, head_dim)
    q_factor = rms_factor(q_raw)
    q_norm = (q_raw * q_factor * query_gain).astype(jnp.bfloat16)
    cot = cotangent.reshape(samp_local, text_rows, kv_local, group, head_dim)
    far_keys, far_vals = swapped((keys, vals), "dp", top_bit)
    gated_rows, d_qn_rows, home_dk, home_dv = ([], [], [], [])
    for own in range(samp_local):
        slot = home_slot[own]
        near = slot // samp_local == rank
        index = slot % samp_local
        result = attend(
            q_norm[own],
            choose(near, keys, far_keys, index),
            choose(near, vals, far_vals, index),
            cot[own],
            home_tiles[own],
            ratio,
        )
        gated_rows.append(result[0])
        d_qn_rows.append(result[1])
        home_dk.append(result[2])
        home_dv.append(result[3])
    home_dk = jnp.stack(home_dk)
    home_dv = jnp.stack(home_dv)
    far_dk, far_dv = (
        swapped(home_dk.astype(jnp.bfloat16), "dp", top_bit).astype(home_dk.dtype),
        swapped(home_dv.astype(jnp.bfloat16), "dp", top_bit).astype(home_dv.dtype),
    )
    slot_dk, slot_dv = ([], [])
    for slot in range(samp_local):
        sample = slot_sample[slot]
        near = sample // samp_local == rank
        index = sample % samp_local
        slot_dk.append(choose(near, home_dk, far_dk, index))
        slot_dv.append(choose(near, home_dv, far_dv, index))
    gated_rows = jnp.stack(gated_rows)
    d_qn_rows = jnp.stack(d_qn_rows)
    slot_dk = jnp.stack(slot_dk)
    slot_dv = jnp.stack(slot_dv)
    context = gated_rows.astype(jnp.bfloat16).reshape(query.shape)
    d_query = (
        norm_back(q_raw, q_factor, query_gain, d_qn_rows).astype(jnp.bfloat16).reshape(query.shape)
    )
    grad_key_unnormed = norm_back(kraw, key_factor, key_gain, slot_dk).astype(jnp.bfloat16)
    grad_key_unnormed = grad_key_unnormed.reshape(samp_local, img_rows, kv_cols)
    d_vals = slot_dv.astype(jnp.bfloat16).reshape(samp_local, img_rows, kv_cols)
    d_both = jnp.concatenate([grad_key_unnormed, d_vals], axis=2)
    dims = (((0,), (0,)), ((), ()))
    grads = jnp.zeros((width, 2 * kv_cols), jnp.float32)
    for slot in range(samp_local):
        for index in range(tile_total):
            grad_tile = d_both[slot, index * TILE : (index + 1) * TILE]
            grads = grads + lax.dot_general(
                kept[slot][index], grad_tile, dims, preferred_element_type=jnp.float32
            )
    shares = lax.psum_scatter(
        grads.astype(jnp.bfloat16), "dp", scatter_dimension=0, tiled=True
    ).astype(jnp.float32)
    return (context, d_query, shares[:, :kv_cols], shares[:, kv_cols:])


def solution(mesh):
    placed = (
        P("dp", None, "tensor"),
        P("dp", None, "tensor"),
        P(),
        P(),
        P("dp", "tensor"),
        P("dp", "tensor"),
        P(),
        P(),
        P(),
        P("dp", None, "tensor"),
    )
    return jax.shard_map(
        per_device,
        mesh=mesh,
        in_specs=placed,
        out_specs=(
            P("dp", None, "tensor"),
            P("dp", None, "tensor"),
            P("dp", "tensor"),
            P("dp", "tensor"),
        ),
        check_vma=False,
    )
```

profile of v0, /device:TPU:4, one launch (start us, length us, event | category | flops | bytes accessed | tf_op | source)
XLA Modules:
  0.0 517.6 jit_solution(14088600843013296658)
XLA Ops:
  32.1 25.8 %all-gather.19.cloned.1.call-done = bf16[8192,128]{1,0:T(8,128)(2,1)} async-done(((bf16[512,128]{1,0:T(8,128)(2,1)}), bf16[8192,128]{1,0:T(8,128)(2,1)}) %all-gather.19.cloned.1.call-update) | async-done | bytes 2097168 | tf_op jit(solution)/shard_map/all_gather | solution.py:134
  61.0 43.5 %all-gather.21.cloned.1.call-done = bf16[8192,128]{1,0:T(8,128)(2,1)} async-done(((bf16[512,128]{1,0:T(8,128)(2,1)}), bf16[8192,128]{1,0:T(8,128)(2,1)}) %all-gather.21.cloned.1.call-update) | async-done | bytes 2097168 | tf_op jit(solution)/shard_map/all_gather | solution.py:135
  107.6 22.0 %all-gather.37.cloned.1.call-done = bf16[1,128,8192]{2,1,0:T(8,128)(2,1)} async-done(((bf16[1,128,1024]{2,1,0:T(8,128)(2,1)}), bf16[1,128,8192]{2,1,0:T(8,128)(2,1)}) %all-gather.37.cloned.1.call-update) | async-done | bytes 2097168 | tf_op jit(solution)/shard_map/all_gather | solution.py:146
  129.7 3.5 fusion.131
  133.2 23.5 %all-gather.35.cloned.1.call-done = bf16[1,128,8192]{2,1,0:T(8,128)(2,1)} async-done(((bf16[1,128,1024]{2,1,0:T(8,128)(2,1)}), bf16[1,128,8192]{2,1,0:T(8,128)(2,1)}) %all-gather.35.cloned.1.call-update) | async-done | bytes 2097168 | tf_op jit(solution)/shard_map/all_gather | solution.py:146
  156.7 3.5 fusion.128
  160.2 24.0 %all-gather.33.cloned.1.call-done = bf16[1,128,8192]{2,1,0:T(8,128)(2,1)} async-done(((bf16[1,128,1024]{2,1,0:T(8,128)(2,1)}), bf16[1,128,8192]{2,1,0:T(8,128)(2,1)}) %all-gather.33.cloned.1.call-update) | async-done | bytes 2097168 | tf_op jit(solution)/shard_map/all_gather | solution.py:146
  184.3 3.5 fusion.125
  187.8 23.5 %all-gather.31.cloned.1.call-done = bf16[1,128,8192]{2,1,0:T(8,128)(2,1)} async-done(((bf16[1,128,1024]{2,1,0:T(8,128)(2,1)}), bf16[1,128,8192]{2,1,0:T(8,128)(2,1)}) %all-gather.31.cloned.1.call-update) | async-done | bytes 2097168 | tf_op jit(solution)/shard_map/all_gather | solution.py:146
  211.3 3.5 fusion.122
  214.9 23.6 %all-gather.29.cloned.1.call-done = bf16[1,128,8192]{2,1,0:T(8,128)(2,1)} async-done(((bf16[1,128,1024]{2,1,0:T(8,128)(2,1)}), bf16[1,128,8192]{2,1,0:T(8,128)(2,1)}) %all-gather.29.cloned.1.call-update) | async-done | bytes 2097168 | tf_op jit(solution)/shard_map/all_gather | solution.py:146
  238.5 3.5 fusion.119
  242.0 23.6 %all-gather.27.cloned.1.call-done = bf16[1,128,8192]{2,1,0:T(8,128)(2,1)} async-done(((bf16[1,128,1024]{2,1,0:T(8,128)(2,1)}), bf16[1,128,8192]{2,1,0:T(8,128)(2,1)}) %all-gather.27.cloned.1.call-update) | async-done | bytes 2097168 | tf_op jit(solution)/shard_map/all_gather | solution.py:146
  265.6 3.5 fusion.116
  269.2 23.6 %all-gather.25.cloned.1.call-done = bf16[1,128,8192]{2,1,0:T(8,128)(2,1)} async-done(((bf16[1,128,1024]{2,1,0:T(8,128)(2,1)}), bf16[1,128,8192]{2,1,0:T(8,128)(2,1)}) %all-gather.25.cloned.1.call-update) | async-done | bytes 2097168 | tf_op jit(solution)/shard_map/all_gather | solution.py:146
  292.8 3.5 fusion.113
  296.4 24.0 %all-gather.23.cloned.1.call-done = bf16[1,128,8192]{2,1,0:T(8,128)(2,1)} async-done(((bf16[1,128,1024]{2,1,0:T(8,128)(2,1)}), bf16[1,128,8192]{2,1,0:T(8,128)(2,1)}) %all-gather.23.cloned.1.call-update) | async-done | bytes 2097168 | tf_op jit(solution)/shard_map/all_gather | solution.py:146
  320.4 3.5 fusion.110
  328.9 6.9 %collective-permute-done = bf16[2,512,1,128]{3,1,0,2:T(8,128)(2,1)S(1)} collective-permute-done((bf16[2,512,1,128]{3,1,0,2:T(8,128)(2,1)S(1)}, bf16[2,512,1,128]{3,1,0,2:T(8,128)(2,1)S(1)}, u32[]{:S(2)}, u32[]{:S(2)}) %collective-permute-start) | collective-permute-done | bytes 262176 | tf_op jit(solution)/shard_map/ppermute | solution.py:13
  336.5 4.2 collective-permute-done.1
  350.3 5.3 %while.55 = (s32[]{:T(128)}, f32[128,1,8,128]{0,3,2,1:T(8,128)S(1)}, f32[512,1,128]{2,0,1:T(8,128)S(1)}, bf16[512,1,128]{2,0,1:T(8,128)(2,1)S(1)}, s32[]{:T(128)...) while((s32[]{:T(128)}, ...), condition=%wide.region_13.14_spmd, body=%wide.region_12.13_spmd.sunk | while | flops 168837120 | bytes 4694239 | solution.py:99
  359.0 28.1 %collective-permute-start.2 = (bf16[2,512,1,128]{3,1,2,0:T(8,128)(2,1)}, bf16[2,512,1,128]{3,1,2,0:T(8,128)(2,1)}, u32[]{:S(2)}, u32[]{:S(2)}) collective-permute-start(bf16[2,512,1,128]{3,1,2,0:T(8,128)(2,1)} %fusion.140), channel_id=1, source_target_pairs={{0,64},{8,72},{16,80},{24,88},{32,96},{40,104},{48,112},{56,120},{... | collective-permute-start | bytes 786440 | tf_op jit(solution)/shard_map/ppermute | solution.py:13
  397.5 5.7 %collective-permute-done.3 = bf16[2,512,1,128]{3,1,2,0:T(8,128)(2,1)S(1)} collective-permute-done((bf16[2,512,1,128]{3,1,2,0:T(8,128)(2,1)S(1)}, bf16[2,512,1,128]{3,1,2,0:T(8,128)(2,1)S(1)}, u32[]{:S(2)}, u32[]{:S(2)}) %collective-permute-start.3) | collective-permute-done | bytes 262176 | tf_op jit(solution)/shard_map/ppermute | solution.py:13
  431.9 76.5 %reduce-scatter.2.cloned.1.call-done = bf16[512,256]{0,1:T(8,128)(2,1)} async-done(((bf16[8192,256]{0,1:T(8,128)(2,1)}), bf16[512,256]{0,1:T(8,128)(2,1)}) %reduce-scatter.2.cloned.1.call-update) | async-done | bytes 262160 | tf_op jit(solution)/shard_map/reduce_scatter | solution.py:215
  (183 shorter events, 83.0 us)
Async XLA Ops:
  7.2 50.7 %all-gather.19.cloned.1.call-start = ((), (), s32[]{:S(2)}) async-start(), calls=%async_computation.1 | async-start | bytes 2228224 | tf_op jit(solution)/shard_map/all_gather | solution.py:134
  7.9 96.6 %all-gather.21.cloned.1.call-start = ((), (), s32[]{:S(2)}) async-start(), calls=%async_computation.2 | async-start | bytes 2228224 | tf_op jit(solution)/shard_map/all_gather | solution.py:135
  8.6 121.0 %all-gather.37.cloned.1.call-start = ((), (), s32[]{:S(2)}) async-start(), calls=%async_computation.11 | async-start | bytes 2359296 | tf_op jit(solution)/shard_map/all_gather | solution.py:146
  11.5 10.5 %copy-start.13 = (bf16[2,128,1024]{2,1,0:T(8,128)(2,1)S(1)}, bf16[2,128,1024]{2,1,0:T(8,128)(2,1)}, u32[]{:S(2)}) copy-start(bf16[2,128,1024]{2,1,0:T(8,128)(2,1)} %param.18) | copy-start | bytes 1572868
  11.6 145.1 %all-gather.35.cloned.1.call-start = ((), (), s32[]{:S(2)}) async-start(), calls=%async_computation.10 | async-start | bytes 2359296 | tf_op jit(solution)/shard_map/all_gather | solution.py:146
  12.1 172.1 %all-gather.33.cloned.1.call-start = ((), (), s32[]{:S(2)}) async-start(), calls=%async_computation.9 | async-start | bytes 2359296 | tf_op jit(solution)/shard_map/all_gather | solution.py:146
  12.7 198.6 %all-gather.31.cloned.1.call-start = ((), (), s32[]{:S(2)}) async-start(), calls=%async_computation.8 | async-start | bytes 2359296 | tf_op jit(solution)/shard_map/all_gather | solution.py:146
  13.3 225.2 %all-gather.29.cloned.1.call-start = ((), (), s32[]{:S(2)}) async-start(), calls=%async_computation.7 | async-start | bytes 2359296 | tf_op jit(solution)/shard_map/all_gather | solution.py:146
  14.0 251.6 %all-gather.27.cloned.1.call-start = ((), (), s32[]{:S(2)}) async-start(), calls=%async_computation.6 | async-start | bytes 2359296 | tf_op jit(solution)/shard_map/all_gather | solution.py:146
  14.8 278.0 %all-gather.25.cloned.1.call-start = ((), (), s32[]{:S(2)}) async-start(), calls=%async_computation.5 | async-start | bytes 2359296 | tf_op jit(solution)/shard_map/all_gather | solution.py:146
  15.5 304.9 %all-gather.23.cloned.1.call-start = ((), (), s32[]{:S(2)}) async-start(), calls=%async_computation.4 | async-start | bytes 2359296 | tf_op jit(solution)/shard_map/all_gather | solution.py:146
  16.1 492.2 %reduce-scatter.2.cloned.1.call-start = ((), (), s32[]{:S(2)}) async-start(), calls=%async_computation.3 | async-start | bytes 4456448 | tf_op jit(solution)/shard_map/reduce_scatter | solution.py:215
  28.6 32.4 %copy-start.12 = (bf16[1,128,1024]{1,2,0:T(8,128)(2,1)}, bf16[1,128,1024]{1,2,0:T(8,128)(2,1)S(1)}, u32[]{:S(2)}) copy-start(bf16[1,128,1024]{1,2,0:T(8,128)(2,1)S(1)} %copy.174) | copy-start | bytes 786436
  325.1 10.7 %collective-permute-start = (bf16[2,512,1,128]{3,1,0,2:T(8,128)(2,1)S(1)}, bf16[2,512,1,128]{3,1,0,2:T(8,128)(2,1)S(1)}, u32[]{:S(2)}, u32[]{:S(2)}) collective-permute-start(bf16[2,512,1,128]{3,1,0,2:T(8,128)(2,1)S(1)} %fusion.188), channel_id=1, source_target_pairs={{0,64},{8,72},{16,80},{24,88},{32,96},{40,104},{48,112},{56,120},{... | collective-permute-start | bytes 786440 | tf_op jit(solution)/shard_map/ppermute | solution.py:13
  328.3 12.4 %collective-permute-start.1 = (bf16[2,512,1,128]{3,1,0,2:T(8,128)(2,1)S(1)}, bf16[2,512,1,128]{3,1,0,2:T(8,128)(2,1)S(1)}, u32[]{:S(2)}, u32[]{:S(2)}) collective-permute-start(bf16[2,512,1,128]{3,1,0,2:T(8,128)(2,1)S(1)} %fusion.187), channel_id=1, source_target_pairs={{0,64},{8,72},{16,80},{24,88},{32,96},{40,104},{48,112},{56,120},{... | collective-permute-start | bytes 786440 | tf_op jit(solution)/shard_map/ppermute | solution.py:13
  350.3 6.1 %copy-start.19 = (bf16[128,1,8,128]{0,3,2,1:T(8,128)(2,1)S(1)}, bf16[128,1,8,128]{0,3,2,1:T(8,128)(2,1)}, u32[]{:S(2)}) copy-start(bf16[128,1,8,128]{0,3,2,1:T(8,128)(2,1)} %get-tuple-element.558) | copy-start | bytes 786436
  350.3 6.3 %copy-start.26 = (f32[1,8,128,1]{2,1,3,0:T(8,128)S(1)}, f32[1,8,128,1]{2,1,3,0:T(8,128)}, u32[]{:S(2)}) copy-start(f32[1,8,128,1]{2,1,3,0:T(8,128)} %broadcast_add_fusion.1) | copy-start | bytes 12292
  357.2 38.1 %copy-start.11 = (f32[512,1,128]{2,0,1:T(8,128)S(1)}, f32[512,1,128]{2,0,1:T(8,128)}, u32[]{:S(2)}) copy-start(f32[512,1,128]{2,0,1:T(8,128)} %copy-done.10) | copy-start | bytes 786436
  357.3 38.3 %copy-start.25 = (f32[2,512]{1,0:T(2,128)S(1)}, f32[2,512]{1,0:T(2,128)}, u32[]{:S(2)}) copy-start(f32[2,512]{1,0:T(2,128)} %get-tuple-element.548) | copy-start | bytes 12292
  357.3 38.3 %copy-start.28 = (f32[128]{0:T(128)S(1)}, f32[128]{0:T(128)}, u32[]{:S(2)}) copy-start(f32[128]{0:T(128)} %param.25) | copy-start | bytes 1540
  359.0 35.4 %collective-permute-start.2 = (bf16[2,512,1,128]{3,1,2,0:T(8,128)(2,1)}, bf16[2,512,1,128]{3,1,2,0:T(8,128)(2,1)}, u32[]{:S(2)}, u32[]{:S(2)}) collective-permute-start(bf16[2,512,1,128]{3,1,2,0:T(8,128)(2,1)} %fusion.140), channel_id=1, source_target_pairs={{0,64},{8,72},{16,80},{24,88},{32,96},{40,104},{48,112},{56,120},{... | collective-permute-start | bytes 786440 | tf_op jit(solution)/shard_map/ppermute | solution.py:13
  394.3 8.9 %copy-start.17 = (bf16[512,1,128]{2,0,1:T(8,128)(2,1)S(1)}, bf16[512,1,128]{2,0,1:T(8,128)(2,1)}, u32[]{:S(2)}) copy-start(bf16[512,1,128]{2,0,1:T(8,128)(2,1)} %get-tuple-element.220) | copy-start | bytes 393220
  394.3 8.9 %collective-permute-start.3 = (bf16[2,512,1,128]{3,1,2,0:T(8,128)(2,1)S(1)}, bf16[2,512,1,128]{3,1,2,0:T(8,128)(2,1)S(1)}, u32[]{:S(2)}, u32[]{:S(2)}) collective-permute-start(bf16[2,512,1,128]{3,1,2,0:T(8,128)(2,1)S(1)} %fusion.139), channel_id=1, source_target_pairs={{0,64},{8,72},{16,80},{24,88},{32,96},{40,104},{48,112},{56,120},{... | collective-permute-start | bytes 786440 | tf_op jit(solution)/shard_map/ppermute | solution.py:13
  395.5 7.9 %copy-start.7 = (bf16[1,128,8192]{2,1,0:T(8,128)(2,1)S(1)}, bf16[1,128,8192]{2,1,0:T(8,128)(2,1)}, u32[]{:S(2)}) copy-start(bf16[1,128,8192]{2,1,0:T(8,128)(2,1)} %all-gather.23.cloned.1.call-done) | copy-start | bytes 6291460
  (20 other events, 40.7 us)
Sparse Core Ops, SparseCore 0:
  10.1 47.6 all-gather.18
  60.0 44.5 all-gather.20
  106.2 23.3 all-gather.36
  131.2 25.4 all-gather.34
  158.8 25.4 all-gather.32
  185.8 25.4 all-gather.30
  213.0 25.4 all-gather.28
  240.2 25.4 all-gather.26
  267.3 25.4 all-gather.24
  294.9 25.4 all-gather.22
  418.0 90.3 reduce-scatter.1
where the time goes:
time: 522 us; the launch traced here: 518 us
  waiting for transfers between devices  356 us (68%)
  matrix products  44.8 us (9%)
  starting transfers between devices  32.2 us (6%)
  local copies, waits for them, and re-layouts  30.7 us (6%)
  between operations  26.7 us (5%)
  other arithmetic  22.8 us (4%)
    all_gather x8, waiting for transfers between devices, per_device(): full = lax.all_gather(part, 'tensor', axis=1, tiled=True)  188 us
    reduce_scatter x1, waiting for transfers between devices, per_device(): lax.psum_scatter(grads.astype(jnp.bfloat16), 'dp', scatter_dimension=0, t...  76.5 us
    all_gather x1, waiting for transfers between devices, per_device(): lax.all_gather(value_weight_matrix, 'dp', axis=0, tiled=True)  43.5 us
    ppermute x4, starting transfers between devices, swapped(): lax.ppermute(shard, axis, [(i, i ^ 1 << distance) for i in range(lax.axis...  31.7 us
    dot_general x8, matrix products, per_device(): proj_parts.append(jnp.dot(full, w_both, preferred_element_type=jnp.float32))  28.3 us
    all_gather x1, waiting for transfers between devices, per_device(): lax.all_gather(key_weight_matrix, 'dp', axis=0, tiled=True)  25.8 us
    ppermute x4, waiting for transfers between devices, swapped(): lax.ppermute(shard, axis, [(i, i ^ 1 << distance) for i in range(lax.axis...  16.8 us
    dot_general x8, matrix products, per_device(): lax.dot_general(kept[slot][index], grad_tile, dims, preferred_element_typ...  12.3 us
  transfers between devices with their start and end apart: 15, of which 14 were waited for; matrix products, arithmetic and copies ran while one was open for 12% of the time, Pallas kernels for 0%

commit v1 on v0

v1 whole, which is shorter than its diff:
```python
import functools

import jax
import jax.numpy as jnp
from jax import lax
from jax.experimental import pallas as pl
from jax.experimental.pallas import tpu as pltpu
from jax.sharding import PartitionSpec as P

TILE = 128
RING = 4
EPS = 1e-06


def along_z(x, step):
    pairs = [(z * RING + y, (z + step) % RING * RING + y) for z in range(RING) for y in range(RING)]
    return lax.ppermute(x, "dp", pairs)


def along_y(x, step):
    pairs = [(z * RING + y, z * RING + (y + step) % RING) for z in range(RING) for y in range(RING)]
    return lax.ppermute(x, "dp", pairs)


def along_x(x, step):
    pairs = [(i * 2 + c, (i + step) % RING * 2 + c) for i in range(RING) for c in range(2)]
    return lax.ppermute(x, "tensor", pairs)


def other_core(x):
    return lax.ppermute(x, "tensor", [(i, i ^ 1) for i in range(2 * RING)])


def exchange_xz(x):
    pairs = []
    for z in range(RING):
        for y in range(RING):
            for i in range(RING):
                for c in range(2):
                    source = (z * RING + y) * 2 * RING + i * 2 + c
                    target = (i * RING + y) * 2 * RING + z * 2 + c
                    pairs.append((source, target))
    return lax.ppermute(x, ("dp", "tensor"), pairs)


def gathered(x, move):
    return [x] + [move(x, step) for step in range(1, RING)]


def scattered(blocks, move):
    arrived = [move(blocks[step], step) for step in range(1, RING)]
    total = blocks[0].astype(jnp.float32)
    for block in arrived:
        total = total + block.astype(jnp.float32)
    return total


def rms_factor(values):
    return lax.rsqrt(jnp.mean(values * values, axis=-1, keepdims=True) + EPS)


def norm_back(values, norm_multiplier, gain, grad):
    weighted = grad * gain
    inner = jnp.sum(weighted * values, axis=-1, keepdims=True)
    return (
        norm_multiplier * weighted
        - values * (norm_multiplier * norm_multiplier * norm_multiplier) * inner / values.shape[-1]
    )


def matmul(a, b, contract):
    return lax.dot_general(a, b, (contract, ((), ())), preferred_element_type=jnp.float32)


def attend_kernel(heads, index, ratio_ref, q_ref, cot_ref, kv_ref, gain_ref, *refs):
    context_ref, d_query_ref, d_kv_ref, d_key_sum, d_value_sum = refs[-5:]
    step = pl.program_id(0)
    head_dim = gain_ref.shape[1]
    scale = head_dim ** (-0.5)
    count = index[1]
    ratio = ratio_ref[0]
    gain = gain_ref[...]
    keys = kv_ref[:, :head_dim]
    vals = kv_ref[:, head_dim:]

    def stacked(ref):
        parts = [ref[0, :, h * head_dim : (h + 1) * head_dim] for h in range(heads)]
        return jnp.concatenate(parts, axis=0).astype(jnp.float32)

    def unstacked(ref, rows):
        text = rows.shape[0] // heads
        for h in range(heads):
            part = rows[h * text : (h + 1) * text]
            ref[0, :, h * head_dim : (h + 1) * head_dim] = part.astype(ref.dtype)

    @pl.when(step == 0)
    def _():
        d_key_sum[...] = jnp.zeros_like(d_key_sum)
        d_value_sum[...] = jnp.zeros_like(d_value_sum)

    q_raw = stacked(q_ref)
    q_factor = rms_factor(q_raw)
    q_norm = (q_raw * q_factor * gain).astype(jnp.bfloat16)
    raw = matmul(q_norm, keys, ((1,), (1,))) * scale
    place = lax.broadcasted_iota(jnp.int32, raw.shape, 1)
    expo = jnp.where(place < count * TILE, jnp.exp(raw), 0.0)
    total = jnp.sum(expo, axis=1, keepdims=True) + (count == 0).astype(jnp.float32)
    inverse = 1.0 / total
    weights_b = expo.astype(jnp.bfloat16)
    attended = matmul(weights_b, vals, ((1,), (0,))) * inverse
    unstacked(context_ref, ratio * attended)
    d_att = ratio * stacked(cot_ref)
    d_att_b = d_att.astype(jnp.bfloat16)
    scaled_b = (d_att * inverse).astype(jnp.bfloat16)
    delta = jnp.sum(d_att * attended, axis=1, keepdims=True)
    d_prob = matmul(d_att_b, vals, ((1,), (1,)))
    d_score = (expo * inverse * (d_prob - delta)).astype(jnp.bfloat16)
    d_qn = scale * matmul(d_score, keys, ((1,), (0,)))
    unstacked(d_query_ref, norm_back(q_raw, q_factor, gain, d_qn))
    d_key_sum[...] += matmul(d_score, q_norm, ((0,), (0,)))
    d_value_sum[...] += matmul(weights_b, scaled_b, ((0,), (0,)))

    @pl.when(step == pl.num_programs(0) - 1)
    def _():
        d_kv_ref[:, :head_dim] = (scale * d_key_sum[...]).astype(d_kv_ref.dtype)
        d_kv_ref[:, head_dim:] = d_value_sum[...].astype(d_kv_ref.dtype)


def attend(own, count, ratio, query, cot, key_value, gain, earlier, heads=2):
    rows, both = key_value.shape
    head_dim = both // 2
    text = query.shape[1]
    width = heads * head_dim
    block = pl.BlockSpec((1, text, width), lambda h, index: (index[0], 0, h))
    whole = lambda shape: pl.BlockSpec(shape, lambda h, index: (0, 0))
    in_specs = [
        pl.BlockSpec(memory_space=pltpu.SMEM),
        block,
        block,
        whole((rows, both)),
        whole((1, head_dim)),
    ]
    aliases = {}
    if earlier:
        in_specs += [pl.BlockSpec(memory_space=pl.ANY)] * 2
        aliases = {6: 0, 7: 1}
    steps = query.shape[2] // width
    return pl.pallas_call(
        functools.partial(attend_kernel, heads),
        grid_spec=pltpu.PrefetchScalarGridSpec(
            num_scalar_prefetch=1,
            grid=(steps,),
            in_specs=in_specs,
            out_specs=[block, block, whole((rows, both))],
            scratch_shapes=[pltpu.VMEM((rows, head_dim), jnp.float32)] * 2,
        ),
        out_shape=[
            jax.ShapeDtypeStruct(query.shape, jnp.bfloat16),
            jax.ShapeDtypeStruct(query.shape, jnp.bfloat16),
            jax.ShapeDtypeStruct((rows, both), jnp.bfloat16),
        ],
        input_output_aliases=aliases,
        compiler_params=pltpu.CompilerParams(
            dimension_semantics=("arbitrary",), vmem_limit_bytes=24 * 1024 * 1024
        ),
        cost_estimate=pl.CostEstimate(
            flops=14 * steps * heads * text * rows * head_dim,
            bytes_accessed=8 * text * steps * width + 6 * rows * head_dim,
            transcendentals=steps * heads * text * rows,
        ),
    )(
        jnp.stack([own, count]).astype(jnp.int32),
        ratio,
        query,
        cot,
        key_value,
        gain[None, :],
        *earlier,
    )


def per_device(
    query,
    image,
    tiles,
    image_slot,
    key_weight_matrix,
    value_weight_matrix,
    query_gain,
    key_gain,
    gate,
    cotangent,
):
    head_dim = query_gain.shape[0]
    samp_local, img_rows, depth = image.shape
    ratio = jnp.tanh(gate)
    rank = lax.axis_index("dp")
    place = lax.axis_index("tensor")
    z, y = rank // RING, rank % RING
    x, core = place // 2, place % 2

    shard = jnp.concatenate([key_weight_matrix, value_weight_matrix], axis=1)
    shard = exchange_xz(shard)
    half = shard.shape[0] // 2
    both = shard.shape[1]
    upper = jnp.concatenate(gathered(shard[:half], along_z), axis=1)
    lower = jnp.concatenate(gathered(shard[half:], along_y), axis=0)
    upper = jnp.concatenate(gathered(upper, along_y), axis=0)
    lower = jnp.concatenate(gathered(lower, along_z), axis=1)

    first = rank * samp_local
    every = jnp.arange(tiles.shape[0], dtype=jnp.int32)
    local_ids = first + jnp.arange(samp_local, dtype=jnp.int32)
    match = image_slot[None, :] == local_ids[:, None]
    slot_sample = jnp.sum(jnp.where(match, every[None, :], 0), axis=1)
    slot_away = slot_sample // samp_local != rank
    swaps = jnp.any(slot_away)
    far_slot = jnp.where(slot_away[1], 1, 0)
    home_slot = lax.dynamic_slice_in_dim(image_slot, first, samp_local)
    own_away = home_slot // samp_local != rank
    own_of_slot = (home_slot[1] == first + far_slot).astype(jnp.int32)
    far_own = jnp.where(swaps, jnp.where(own_away[1], 1, 0), own_of_slot)
    home_tiles = lax.dynamic_slice_in_dim(tiles, first, samp_local)

    columns = jnp.concatenate([image, other_core(image)], axis=2)
    feats = []
    for slot in (far_slot, 1 - far_slot):
        parts = []
        for h in range(2):
            for o in range(RING):
                block = ((y - o) % RING) ^ (2 * core)
                start = (slot, 0, block * 2 * half + h * half)
                parts.append(lax.dynamic_slice(columns, start, (1, img_rows, half))[0])
        feats.append(jnp.concatenate(parts, axis=1))

    raw_rows, key_values = [], []
    for rows in feats:
        blocks = []
        for d in range(RING):
            group = (z - x - d) % RING * both
            weights = jnp.concatenate(
                [
                    lax.dynamic_slice_in_dim(upper, group, both, 1),
                    lax.dynamic_slice_in_dim(lower, group, both, 1),
                ],
                axis=0,
            )
            block = matmul(rows, weights, ((1,), (0,)))
            blocks.append(block if d == 0 else block.astype(jnp.bfloat16))
        projected = scattered(blocks, along_x)
        raw = projected[:, :head_dim]
        keys = (raw * rms_factor(raw) * key_gain).astype(jnp.bfloat16)
        raw_rows.append(raw)
        key_values.append(
            jnp.concatenate([keys, projected[:, head_dim:].astype(jnp.bfloat16)], axis=1)
        )

    away = along_z(key_values[0], RING // 2)
    away = jnp.where(swaps, away, key_values[0])
    near_own = 1 - far_own
    earlier = ()
    grads = [None, None]
    order = ((0, far_own, away), (1, near_own, key_values[1]))
    for slot, own, key_value in order:
        result = attend(
            own, home_tiles[own], ratio, query, cotangent, key_value, query_gain, earlier
        )
        earlier = result[:2]
        grads[slot] = result[2]
    context, d_query = earlier
    back = along_z(grads[0], RING // 2)
    grads[0] = jnp.where(swaps, back, grads[0])

    d_rows = [[], []]
    for slot in (1, 0):
        raw = raw_rows[slot]
        grad = grads[slot].astype(jnp.float32)
        d_raw = norm_back(raw, rms_factor(raw), key_gain, grad[:, :head_dim])
        own = jnp.concatenate([d_raw.astype(jnp.bfloat16), grads[slot][:, head_dim:]], axis=1)
        d_rows[slot] = gathered(own, along_x)
    by_source = jnp.stack([jnp.concatenate([d_rows[0][o], d_rows[1][o]], axis=0) for o in range(RING)])
    groups = [
        lax.dynamic_index_in_dim(by_source, (x - z - d) % RING, 0, keepdims=False)
        for d in range(RING)
    ]
    all_groups = jnp.concatenate(groups, axis=1)
    all_feats = jnp.concatenate(feats, axis=0)

    def sent(block, d):
        return block if d == 0 else block.astype(jnp.bfloat16)

    upper_blocks, lower_blocks = [], []
    wide = RING * half
    for d in range(RING):
        o = -d % RING
        rows = all_feats[:, o * half : (o + 1) * half]
        upper_blocks.append(sent(matmul(rows, all_groups, ((0,), (0,))), d))
        lower_blocks.append(sent(matmul(all_feats[:, wide:], groups[d], ((0,), (0,))), d))
    upper_sum = scattered(upper_blocks, along_y)
    lower_sum = scattered(lower_blocks, along_z)
    upper_parts = [sent(upper_sum[:, d * both : (d + 1) * both], d) for d in range(RING)]
    lower_parts = [
        sent(lower_sum[-d % RING * half : (-d % RING + 1) * half], d) for d in range(RING)
    ]
    upper_sum = scattered(upper_parts, along_z)
    lower_sum = scattered(lower_parts, along_y)
    share = jnp.concatenate([upper_sum, lower_sum], axis=0).astype(jnp.bfloat16)
    share = exchange_xz(share).astype(jnp.float32)
    return (context, d_query, share[:, :head_dim], share[:, head_dim:])


def solution(mesh):
    placed = (
        P("dp", None, "tensor"),
        P("dp", None, "tensor"),
        P(),
        P(),
        P("dp", "tensor"),
        P("dp", "tensor"),
        P(),
        P(),
        P(),
        P("dp", None, "tensor"),
    )
    return jax.shard_map(
        per_device,
        mesh=mesh,
        in_specs=placed,
        out_specs=(
            P("dp", None, "tensor"),
            P("dp", None, "tensor"),
            P("dp", "tensor"),
            P("dp", "tensor"),
        ),
        check_vma=False,
    )
```

time: 522 us -> 252 us (0.48)
  waiting for transfers between devices: 356 us -> 110 us
  starting transfers between devices: 32.2 us -> 80.5 us
  matrix products: 44.8 us -> 11.9 us
  between operations: 26.7 us -> 4.93 us
  local copies, waits for them, and re-layouts: 30.7 us -> 13.1 us
  Pallas kernels: 0 us -> 10.6 us
    all_gather x10 -> x0, waiting for transfers between devices: 257 us -> none  [the longest x8 188 us: per_device(): full = lax.all_gather(part, 'tensor', axis=1, tiled=True)]
    ppermute x4 -> x41, waiting for transfers between devices: 16.8 us -> 110 us  [the longest x14 41 us: along_z(): return lax.ppermute(x, 'dp', pairs)]
    reduce_scatter x1 -> x0, waiting for transfers between devices: 76.5 us -> none  [per_device(): lax.psum_scatter(grads.astype(jnp.bfloat16), 'dp', scatter_dimension=0, t...]
    ppermute x4 -> x41, starting transfers between devices: 31.7 us -> 80.5 us  [the longest x12 34.6 us: along_x(): return lax.ppermute(x, 'tensor', pairs)]
    dot_general x23 -> x16, matrix products: 44.8 us -> 11.9 us  [matmul(): lax.dot_general(a, b, (contract, ((), ())), preferred_element_type=jnp.fl...]
    pallas_call x0 -> x2, Pallas kernels: none -> 10.6 us  [attend(): pl.pallas_call(functools.partial(attend_kernel, heads), grid_spec=pltpu.P...]
    concatenate x1 -> x11, other arithmetic: 0.06 us -> 9.67 us  [the longest x1 3.98 us: per_device(): upper = jnp.concatenate(gathered(upper, along_y), axis=0)]
    convert_element_type x7 -> x2, other arithmetic: 7.22 us -> 0.68 us  [the longest x1 0.48 us: per_device(): d_raw.astype(jnp.bfloat16)]
  transfers between devices with their start and end apart: 15 -> 41, of which waited for: 14 -> 22; matrix products, arithmetic and copies ran while one was open for 12% -> 11% of each run, Pallas kernels for 0% -> 2%
where the time goes in v1:
time: 252 us; the launch traced here: 250 us
  waiting for transfers between devices  110 us (44%)
  starting transfers between devices  80.5 us (32%)
  other arithmetic  19.1 us (8%)
  local copies, waits for them, and re-layouts  13.1 us (5%)
  matrix products  11.9 us (5%)
  Pallas kernels  10.6 us (4%)
  between operations  4.93 us (2%)
    ppermute x14, waiting for transfers between devices, along_z(): return lax.ppermute(x, 'dp', pairs)  41 us
    ppermute x12, starting transfers between devices, along_x(): return lax.ppermute(x, 'tensor', pairs)  34.6 us
    ppermute x12, waiting for transfers between devices, along_y(): return lax.ppermute(x, 'dp', pairs)  29.3 us
    ppermute x12, waiting for transfers between devices, along_x(): return lax.ppermute(x, 'tensor', pairs)  20.5 us
    ppermute x14, starting transfers between devices, along_z(): return lax.ppermute(x, 'dp', pairs)  20.2 us
    ppermute x2, waiting for transfers between devices, exchange_xz(): return lax.ppermute(x, ('dp', 'tensor'), pairs)  19 us
    ppermute x12, starting transfers between devices, along_y(): return lax.ppermute(x, 'dp', pairs)  14.3 us
    dot_general x16, matrix products, matmul(): lax.dot_general(a, b, (contract, ((), ())), preferred_element_type=jnp.fl...  11.9 us
  transfers between devices with their start and end apart: 41, of which 22 were waited for; matrix products, arithmetic and copies ran while one was open for 11% of the time, Pallas kernels for 2%

profile of v1, /device:TPU:4, one launch (start us, length us, event | category | flops | bytes accessed | tf_op | source)
XLA Modules:
  0.0 249.9 jit_solution(6144244619438336569)
XLA Ops:
  1.8 5.7 %collective-permute-start.1 = (bf16[512,256]{1,0:T(8,128)(2,1)S(1)}, bf16[512,256]{1,0:T(8,128)(2,1)S(1)}, u32[]{:S(2)}, u32[]{:S(2)}) collective-permute-start(bf16[512,256]{1,0:T(8,128)(2,1)S(1)} %pad_maximum_fusion.19), channel_id=1, source_target_pairs={{0,0},{1,1},{2,32},{3,33},{4,64},{5,65},{6,96},{7,97},{8,8},{9,9},... | collective-permute-start | bytes 786440 | tf_op jit(solution)/shard_map/ppermute | solution.py:43
  7.6 12.5 %collective-permute-done.1 = bf16[512,256]{1,0:T(8,128)(2,1)S(1)} collective-permute-done((bf16[512,256]{1,0:T(8,128)(2,1)S(1)}, bf16[512,256]{1,0:T(8,128)(2,1)S(1)}, u32[]{:S(2)}, u32[]{:S(2)}) %collective-permute-start.1) | collective-permute-done | bytes 262176 | tf_op jit(solution)/shard_map/ppermute | solution.py:43
  38.5 10.3 %collective-permute-done.2 = bf16[256,256]{1,0:T(8,128)(2,1)S(1)} collective-permute-done((bf16[256,256]{1,0:T(8,128)(2,1)S(1)}, bf16[256,256]{1,0:T(8,128)(2,1)S(1)}, u32[]{:S(2)}, u32[]{:S(2)}) %collective-permute-start.2) | collective-permute-done | bytes 131104 | tf_op jit(solution)/shard_map/ppermute | solution.py:17
  63.3 11.2 %collective-permute-done.7 = bf16[256,1024]{1,0:T(8,128)(2,1)} collective-permute-done((bf16[256,1024]{1,0:T(8,128)(2,1)S(1)}, bf16[256,1024]{1,0:T(8,128)(2,1)}, u32[]{:S(2)}, u32[]{:S(2)}) %collective-permute-start.7) | collective-permute-done | bytes 524320 | tf_op jit(solution)/shard_map/ppermute | solution.py:22
  74.4 3.6 %collective-permute-done.5 = bf16[256,1024]{1,0:T(8,128)(2,1)} collective-permute-done((bf16[256,1024]{1,0:T(8,128)(2,1)S(1)}, bf16[256,1024]{1,0:T(8,128)(2,1)}, u32[]{:S(2)}, u32[]{:S(2)}) %collective-permute-start.5) | collective-permute-done | bytes 524320 | tf_op jit(solution)/shard_map/ppermute | solution.py:22
  78.1 4.0 %pad_maximum_fusion.1 = bf16[1024,1024]{1,0:T(8,128)(2,1)S(1)} fusion(bf16[256,1024]{1,0:T(8,128)(2,1)} %collective-permute-done.7, bf16[256,1024]{1,0:T(8,128)(2,1)} %collective-permute-done.6, bf16[256,1024]{1,0:T(8,128)(2,1)} %collective-permute-done.5, bf16[256,256]{1,0:T(8,128)(2,1)S(1)} %collective-permute-done.4, bf16[256,256]{1,0:T(8,128)(2,1)S(1)} %copy-done.14, ...), kind=kLoop, calls=%fused_computation.1 | loop fusion | flops 14680064 | bytes 4194304 | tf_op jit(solution)/shard_map/concatenate | solution.py:208
  92.1 5.9 %collective-permute-start.15 = (bf16[512,256]{1,0:T(8,128)(2,1)S(1)}, bf16[512,256]{1,0:T(8,128)(2,1)S(1)}, u32[]{:S(2)}, u32[]{:S(2)}) collective-permute-start(bf16[512,256]{1,0:T(8,128)(2,1)S(1)} %convolution_convert_fusion.10), channel_id=1, source_target_pairs={{0,4},{1,5},{2,6},{3,7},{4,0},{5,1},{6,2},{7,3},{8,12},{9,13},{10,... | collective-permute-start | bytes 786440 | tf_op jit(solution)/shard_map/ppermute | solution.py:27
  98.4 4.1 %collective-permute-start.18 = (bf16[512,256]{1,0:T(8,128)(2,1)S(1)}, bf16[512,256]{1,0:T(8,128)(2,1)S(1)}, u32[]{:S(2)}, u32[]{:S(2)}) collective-permute-start(bf16[512,256]{1,0:T(8,128)(2,1)S(1)} %convolution_convert_fusion.7), channel_id=1, source_target_pairs={{0,4},{1,5},{2,6},{3,7},{4,0},{5,1},{6,2},{7,3},{8,12},{9,13},{10,... | collective-permute-start | bytes 786440 | tf_op jit(solution)/shard_map/ppermute | solution.py:27
  104.0 9.2 %collective-permute-done.19 = bf16[512,256]{1,0:T(8,128)(2,1)S(1)} collective-permute-done((bf16[512,256]{1,0:T(8,128)(2,1)S(1)}, bf16[512,256]{1,0:T(8,128)(2,1)S(1)}, u32[]{:S(2)}, u32[]{:S(2)}) %collective-permute-start.19) | collective-permute-done | bytes 262176 | tf_op jit(solution)/shard_map/ppermute | solution.py:27
  113.3 3.2 %collective-permute-start.14 = (bf16[512,256]{1,0:T(8,128)(2,1)S(1)}, bf16[512,256]{1,0:T(8,128)(2,1)S(1)}, u32[]{:S(2)}, u32[]{:S(2)}) collective-permute-start(bf16[512,256]{1,0:T(8,128)(2,1)S(1)} %convolution_convert_fusion.11), channel_id=1, source_target_pairs={{0,2},{1,3},{2,4},{3,5},{4,6},{5,7},{6,0},{7,1},{8,10},{9,11},{10,... | collective-permute-start | bytes 786440 | tf_op jit(solution)/shard_map/ppermute | solution.py:27
  118.0 3.3 %collective-permute-done.14 = bf16[512,256]{1,0:T(8,128)(2,1)S(1)} collective-permute-done((bf16[512,256]{1,0:T(8,128)(2,1)S(1)}, bf16[512,256]{1,0:T(8,128)(2,1)S(1)}, u32[]{:S(2)}, u32[]{:S(2)}) %collective-permute-start.14) | collective-permute-done | bytes 262176 | tf_op jit(solution)/shard_map/ppermute | solution.py:27
  133.7 5.3 %shard_map.129 = (bf16[2,128,1024]{2,1,0:T(8,128)(2,1)}, bf16[2,128,1024]{2,1,0:T(8,128)(2,1)}, bf16[512,256]{1,0:T(8,128)(2,1)S(1)}) custom-call(s32[2]{0:T(128)S(1)} %pad_add_fusion.1.index, f32[1]{0:T(128)S(6)} %tanh.3.ratio_ref, bf16[2,128,1024]{2,1,0:T(8,128)(2,1)S(1)} %copy-done, bf16[2,128,1024]{2,1,0:T(8,128)(2,1)S(1)} %copy-done.1, ...), custom_call_target="tpu_custom_call" | custom-call | flops 939524096 | bytes 1441792 | tf_op jit(solution)/shard_map/pallas_call | solution.py:148
  143.3 5.3 %shard_map.130 = (bf16[2,128,1024]{2,1,0:T(8,128)(2,1)}, bf16[2,128,1024]{2,1,0:T(8,128)(2,1)}, bf16[512,256]{1,0:T(8,128)(2,1)S(1)}) custom-call(s32[2]{0:T(128)S(1)} %pad_add_fusion.index, f32[1]{0:T(128)S(6)} %tanh.3.ratio_ref, bf16[2,128,1024]{2,1,0:T(8,128)(2,1)S(1)} %copy-done, ...), custom_call_target="tpu_custom_call", output_to_operand_aliasing={{0}: (6, {}), {1}: (7, {})} | custom-call | flops 939524096 | bytes 1441792 | tf_op jit(solution)/shard_map/pallas_call | solution.py:148
  153.3 3.6 %collective-permute-start.25 = (bf16[512,256]{1,0:T(8,128)(2,1)S(1)}, bf16[512,256]{1,0:T(8,128)(2,1)S(1)}, u32[]{:S(2)}, u32[]{:S(2)}) collective-permute-start(bf16[512,256]{1,0:T(8,128)(2,1)S(1)} %pad_maximum_fusion.23), channel_id=1, source_target_pairs={{0,4},{1,5},{2,6},{3,7},{4,0},{5,1},{6,2},{7,3},{8,12},{9,13},{10,... | collective-permute-start | bytes 786440 | tf_op jit(solution)/shard_map/ppermute | solution.py:27
  157.1 3.7 %collective-permute-start.24 = (bf16[512,256]{1,0:T(8,128)(2,1)S(1)}, bf16[512,256]{1,0:T(8,128)(2,1)S(1)}, u32[]{:S(2)}, u32[]{:S(2)}) collective-permute-start(bf16[512,256]{1,0:T(8,128)(2,1)S(1)} %pad_maximum_fusion.22), channel_id=1, source_target_pairs={{0,4},{1,5},{2,6},{3,7},{4,0},{5,1},{6,2},{7,3},{8,12},{9,13},{10,... | collective-permute-start | bytes 786440 | tf_op jit(solution)/shard_map/ppermute | solution.py:27
  162.6 9.0 %collective-permute-start.22 = (bf16[512,256]{1,0:T(8,128)(2,1)S(1)}, bf16[512,256]{1,0:T(8,128)(2,1)S(1)}, u32[]{:S(2)}, u32[]{:S(2)}) collective-permute-start(bf16[512,256]{1,0:T(8,128)(2,1)S(1)} %pad_maximum_fusion.22), channel_id=1, source_target_pairs={{0,2},{1,3},{2,4},{3,5},{4,6},{5,7},{6,0},{7,1},{8,10},{9,11},{10,... | collective-permute-start | bytes 786440 | tf_op jit(solution)/shard_map/ppermute | solution.py:27
  174.8 3.5 %collective-permute-done.22 = bf16[512,256]{1,0:T(8,128)(2,1)S(1)} collective-permute-done((bf16[512,256]{1,0:T(8,128)(2,1)S(1)}, bf16[512,256]{1,0:T(8,128)(2,1)S(1)}, u32[]{:S(2)}, u32[]{:S(2)}) %collective-permute-start.22) | collective-permute-done | bytes 262176 | tf_op jit(solution)/shard_map/ppermute | solution.py:27
  179.5 4.2 %collective-permute-start.36 = (bf16[1024,256]{1,0:T(8,128)(2,1)S(1)}, bf16[1024,256]{1,0:T(8,128)(2,1)S(1)}, u32[]{:S(2)}, u32[]{:S(2)}) collective-permute-start(bf16[1024,256]{1,0:T(8,128)(2,1)S(1)} %convolution_convert_fusion), channel_id=1, source_target_pairs={{0,96},{8,104},{16,112},{24,120},{32,0},{40,8},{48,16},{56,24},{64... | collective-permute-start | bytes 1572872 | tf_op jit(solution)/shard_map/ppermute | solution.py:17
  190.0 16.3 %collective-permute-done.36 = bf16[1024,256]{1,0:T(8,128)(2,1)S(1)} collective-permute-done((bf16[1024,256]{1,0:T(8,128)(2,1)S(1)}, bf16[1024,256]{1,0:T(8,128)(2,1)S(1)}, u32[]{:S(2)}, u32[]{:S(2)}) %collective-permute-start.36) | collective-permute-done | bytes 524320 | tf_op jit(solution)/shard_map/ppermute | solution.py:17
  206.2 4.6 %collective-permute-done.34 = bf16[1024,256]{1,0:T(8,128)(2,1)S(1)} collective-permute-done((bf16[1024,256]{1,0:T(8,128)(2,1)S(1)}, bf16[1024,256]{1,0:T(8,128)(2,1)S(1)}, u32[]{:S(2)}, u32[]{:S(2)}) %collective-permute-start.34) | collective-permute-done | bytes 524320 | tf_op jit(solution)/shard_map/ppermute | solution.py:17
  214.4 10.0 %collective-permute-done.28 = bf16[256,1024]{1,0:T(8,128)(2,1)S(1)} collective-permute-done((bf16[256,1024]{1,0:T(8,128)(2,1)S(1)}, bf16[256,1024]{1,0:T(8,128)(2,1)S(1)}, u32[]{:S(2)}, u32[]{:S(2)}) %collective-permute-start.28) | collective-permute-done | bytes 524320 | tf_op jit(solution)/shard_map/ppermute | solution.py:22
  225.3 3.9 %collective-permute-start.33 = (bf16[256,256]{1,0:T(8,128)(2,1)S(1)}, bf16[256,256]{1,0:T(8,128)(2,1)S(1)}, u32[]{:S(2)}, u32[]{:S(2)}) collective-permute-start(bf16[256,256]{1,0:T(8,128)(2,1)S(1)} %get-tuple-element.53), channel_id=1, source_target_pairs={{0,96},{8,104},{16,112},{24,120},{32,0},{40,8},{48,16},{56,24},{64... | collective-permute-start | bytes 393224 | tf_op jit(solution)/shard_map/ppermute | solution.py:17
  236.9 5.6 %collective-permute-start.40 = (bf16[512,256]{1,0:T(8,128)(2,1)S(1)}, bf16[512,256]{1,0:T(8,128)(2,1)S(1)}, u32[]{:S(2)}, u32[]{:S(2)}) collective-permute-start(bf16[512,256]{1,0:T(8,128)(2,1)S(1)} %pad_maximum_fusion.24), channel_id=1, source_target_pairs={{0,0},{1,1},{2,32},{3,33},{4,64},{5,65},{6,96},{7,97},{8,8},{9,9},... | collective-permute-start | bytes 786440 | tf_op jit(solution)/shard_map/ppermute | solution.py:43
  242.6 6.5 %collective-permute-done.40 = bf16[512,256]{1,0:T(8,128)(2,1)S(1)} collective-permute-done((bf16[512,256]{1,0:T(8,128)(2,1)S(1)}, bf16[512,256]{1,0:T(8,128)(2,1)S(1)}, u32[]{:S(2)}, u32[]{:S(2)}) %collective-permute-start.40) | collective-permute-done | bytes 262176 | tf_op jit(solution)/shard_map/ppermute | solution.py:43
  (179 shorter events, 90.3 us)
Async XLA Ops:
  1.8 18.3 %collective-permute-start.1 = (bf16[512,256]{1,0:T(8,128)(2,1)S(1)}, bf16[512,256]{1,0:T(8,128)(2,1)S(1)}, u32[]{:S(2)}, u32[]{:S(2)}) collective-permute-start(bf16[512,256]{1,0:T(8,128)(2,1)S(1)} %pad_maximum_fusion.19), channel_id=1, source_target_pairs={{0,0},{1,1},{2,32},{3,33},{4,64},{5,65},{6,96},{7,97},{8,8},{9,9},... | collective-permute-start | bytes 786440 | tf_op jit(solution)/shard_map/ppermute | solution.py:43
  7.5 74.8 %collective-permute-start = (bf16[2,512,1024]{2,1,0:T(8,128)(2,1)}, bf16[2,512,1024]{2,1,0:T(8,128)(2,1)}, u32[]{:S(2)}, u32[]{:S(2)}) collective-permute-start(bf16[2,512,1024]{2,1,0:T(8,128)(2,1)} %param.11), channel_id=1, source_target_pairs={{0,1},{1,0},{2,3},{3,2},{4,5},{5,4},{6,7},{7,6},{8,9},{9,8},{10,11... | collective-permute-start | bytes 6291464 | tf_op jit(solution)/shard_map/ppermute | solution.py:31
  31.1 23.8 %collective-permute-start.13 = (bf16[1024,256]{1,0:T(8,128)(2,1)S(1)}, bf16[1024,256]{1,0:T(8,128)(2,1)}, u32[]{:S(2)}, u32[]{:S(2)}) collective-permute-start(bf16[1024,256]{1,0:T(8,128)(2,1)S(1)} %pad_maximum_fusion.18), channel_id=1, source_target_pairs={{0,96},{8,104},{16,112},{24,120},{32,0},{40,8},{48,16},{56,24},{64... | collective-permute-start | bytes 1572872 | tf_op jit(solution)/shard_map/ppermute | solution.py:17
  33.3 22.2 %collective-permute-start.12 = (bf16[1024,256]{1,0:T(8,128)(2,1)S(1)}, bf16[1024,256]{1,0:T(8,128)(2,1)}, u32[]{:S(2)}, u32[]{:S(2)}) collective-permute-start(bf16[1024,256]{1,0:T(8,128)(2,1)S(1)} %pad_maximum_fusion.18), channel_id=1, source_target_pairs={{0,64},{8,72},{16,80},{24,88},{32,96},{40,104},{48,112},{56,120},{... | collective-permute-start | bytes 1572872 | tf_op jit(solution)/shard_map/ppermute | solution.py:17
  34.6 26.0 %collective-permute-start.11 = (bf16[1024,256]{1,0:T(8,128)(2,1)S(1)}, bf16[1024,256]{1,0:T(8,128)(2,1)}, u32[]{:S(2)}, u32[]{:S(2)}) collective-permute-start(bf16[1024,256]{1,0:T(8,128)(2,1)S(1)} %pad_maximum_fusion.18), channel_id=1, source_target_pairs={{0,32},{8,40},{16,48},{24,56},{32,64},{40,72},{48,80},{56,88},{64,... | collective-permute-start | bytes 1572872 | tf_op jit(solution)/shard_map/ppermute | solution.py:17
  49.8 24.6 %collective-permute-start.7 = (bf16[256,1024]{1,0:T(8,128)(2,1)S(1)}, bf16[256,1024]{1,0:T(8,128)(2,1)}, u32[]{:S(2)}, u32[]{:S(2)}) collective-permute-start(bf16[256,1024]{1,0:T(8,128)(2,1)S(1)} %pad_maximum_fusion.17), channel_id=1, source_target_pairs={{0,24},{8,0},{16,8},{24,16},{32,56},{40,32},{48,40},{56,48},{64,88... | collective-permute-start | bytes 1572872 | tf_op jit(solution)/shard_map/ppermute | solution.py:22
  54.9 19.5 %collective-permute-start.6 = (bf16[256,1024]{1,0:T(8,128)(2,1)S(1)}, bf16[256,1024]{1,0:T(8,128)(2,1)}, u32[]{:S(2)}, u32[]{:S(2)}) collective-permute-start(bf16[256,1024]{1,0:T(8,128)(2,1)S(1)} %pad_maximum_fusion.17), channel_id=1, source_target_pairs={{0,16},{8,24},{16,0},{24,8},{32,48},{40,56},{48,32},{56,40},{64,80... | collective-permute-start | bytes 1572872 | tf_op jit(solution)/shard_map/ppermute | solution.py:22
  55.6 22.5 %collective-permute-start.5 = (bf16[256,1024]{1,0:T(8,128)(2,1)S(1)}, bf16[256,1024]{1,0:T(8,128)(2,1)}, u32[]{:S(2)}, u32[]{:S(2)}) collective-permute-start(bf16[256,1024]{1,0:T(8,128)(2,1)S(1)} %pad_maximum_fusion.17), channel_id=1, source_target_pairs={{0,8},{8,16},{16,24},{24,0},{32,40},{40,48},{48,56},{56,32},{64,72... | collective-permute-start | bytes 1572872 | tf_op jit(solution)/shard_map/ppermute | solution.py:22
  89.7 28.3 %collective-permute-start.16 = (bf16[512,256]{1,0:T(8,128)(2,1)S(1)}, bf16[512,256]{1,0:T(8,128)(2,1)S(1)}, u32[]{:S(2)}, u32[]{:S(2)}) collective-permute-start(bf16[512,256]{1,0:T(8,128)(2,1)S(1)} %convolution_convert_fusion.9), channel_id=1, source_target_pairs={{0,6},{1,7},{2,0},{3,1},{4,2},{5,3},{6,4},{7,5},{8,14},{9,15},{10,... | collective-permute-start | bytes 786440 | tf_op jit(solution)/shard_map/ppermute | solution.py:27
  92.1 25.8 %collective-permute-start.15 = (bf16[512,256]{1,0:T(8,128)(2,1)S(1)}, bf16[512,256]{1,0:T(8,128)(2,1)S(1)}, u32[]{:S(2)}, u32[]{:S(2)}) collective-permute-start(bf16[512,256]{1,0:T(8,128)(2,1)S(1)} %convolution_convert_fusion.10), channel_id=1, source_target_pairs={{0,4},{1,5},{2,6},{3,7},{4,0},{5,1},{6,2},{7,3},{8,12},{9,13},{10,... | collective-permute-start | bytes 786440 | tf_op jit(solution)/shard_map/ppermute | solution.py:27
  98.4 18.1 %collective-permute-start.18 = (bf16[512,256]{1,0:T(8,128)(2,1)S(1)}, bf16[512,256]{1,0:T(8,128)(2,1)S(1)}, u32[]{:S(2)}, u32[]{:S(2)}) collective-permute-start(bf16[512,256]{1,0:T(8,128)(2,1)S(1)} %convolution_convert_fusion.7), channel_id=1, source_target_pairs={{0,4},{1,5},{2,6},{3,7},{4,0},{5,1},{6,2},{7,3},{8,12},{9,13},{10,... | collective-permute-start | bytes 786440 | tf_op jit(solution)/shard_map/ppermute | solution.py:27
  153.3 20.1 %collective-permute-start.25 = (bf16[512,256]{1,0:T(8,128)(2,1)S(1)}, bf16[512,256]{1,0:T(8,128)(2,1)S(1)}, u32[]{:S(2)}, u32[]{:S(2)}) collective-permute-start(bf16[512,256]{1,0:T(8,128)(2,1)S(1)} %pad_maximum_fusion.23), channel_id=1, source_target_pairs={{0,4},{1,5},{2,6},{3,7},{4,0},{5,1},{6,2},{7,3},{8,12},{9,13},{10,... | collective-permute-start | bytes 786440 | tf_op jit(solution)/shard_map/ppermute | solution.py:27
  157.0 16.4 %collective-permute-start.26 = (bf16[512,256]{1,0:T(8,128)(2,1)S(1)}, bf16[512,256]{1,0:T(8,128)(2,1)S(1)}, u32[]{:S(2)}, u32[]{:S(2)}) collective-permute-start(bf16[512,256]{1,0:T(8,128)(2,1)S(1)} %pad_maximum_fusion.22), channel_id=1, source_target_pairs={{0,6},{1,7},{2,0},{3,1},{4,2},{5,3},{6,4},{7,5},{8,14},{9,15},{10,... | collective-permute-start | bytes 786440 | tf_op jit(solution)/shard_map/ppermute | solution.py:27
  157.1 16.3 %collective-permute-start.24 = (bf16[512,256]{1,0:T(8,128)(2,1)S(1)}, bf16[512,256]{1,0:T(8,128)(2,1)S(1)}, u32[]{:S(2)}, u32[]{:S(2)}) collective-permute-start(bf16[512,256]{1,0:T(8,128)(2,1)S(1)} %pad_maximum_fusion.22), channel_id=1, source_target_pairs={{0,4},{1,5},{2,6},{3,7},{4,0},{5,1},{6,2},{7,3},{8,12},{9,13},{10,... | collective-permute-start | bytes 786440 | tf_op jit(solution)/shard_map/ppermute | solution.py:27
  162.6 15.7 %collective-permute-start.22 = (bf16[512,256]{1,0:T(8,128)(2,1)S(1)}, bf16[512,256]{1,0:T(8,128)(2,1)S(1)}, u32[]{:S(2)}, u32[]{:S(2)}) collective-permute-start(bf16[512,256]{1,0:T(8,128)(2,1)S(1)} %pad_maximum_fusion.22), channel_id=1, source_target_pairs={{0,2},{1,3},{2,4},{3,5},{4,6},{5,7},{6,0},{7,1},{8,10},{9,11},{10,... | collective-permute-start | bytes 786440 | tf_op jit(solution)/shard_map/ppermute | solution.py:27
  179.5 26.7 %collective-permute-start.36 = (bf16[1024,256]{1,0:T(8,128)(2,1)S(1)}, bf16[1024,256]{1,0:T(8,128)(2,1)S(1)}, u32[]{:S(2)}, u32[]{:S(2)}) collective-permute-start(bf16[1024,256]{1,0:T(8,128)(2,1)S(1)} %convolution_convert_fusion), channel_id=1, source_target_pairs={{0,96},{8,104},{16,112},{24,120},{32,0},{40,8},{48,16},{56,24},{64... | collective-permute-start | bytes 1572872 | tf_op jit(solution)/shard_map/ppermute | solution.py:17
  184.5 21.7 %collective-permute-start.35 = (bf16[1024,256]{1,0:T(8,128)(2,1)S(1)}, bf16[1024,256]{1,0:T(8,128)(2,1)S(1)}, u32[]{:S(2)}, u32[]{:S(2)}) collective-permute-start(bf16[1024,256]{1,0:T(8,128)(2,1)S(1)} %convolution_convert_fusion.1), channel_id=1, source_target_pairs={{0,64},{8,72},{16,80},{24,88},{32,96},{40,104},{48,112},{56,120},{... | collective-permute-start | bytes 1572872 | tf_op jit(solution)/shard_map/ppermute | solution.py:17
  186.0 24.8 %collective-permute-start.34 = (bf16[1024,256]{1,0:T(8,128)(2,1)S(1)}, bf16[1024,256]{1,0:T(8,128)(2,1)S(1)}, u32[]{:S(2)}, u32[]{:S(2)}) collective-permute-start(bf16[1024,256]{1,0:T(8,128)(2,1)S(1)} %convolution_convert_fusion.2), channel_id=1, source_target_pairs={{0,32},{8,40},{16,48},{24,56},{32,64},{40,72},{48,80},{56,88},{64,... | collective-permute-start | bytes 1572872 | tf_op jit(solution)/shard_map/ppermute | solution.py:17
  187.0 26.1 %collective-permute-start.30 = (bf16[256,1024]{1,0:T(8,128)(2,1)S(1)}, bf16[256,1024]{1,0:T(8,128)(2,1)S(1)}, u32[]{:S(2)}, u32[]{:S(2)}) collective-permute-start(bf16[256,1024]{1,0:T(8,128)(2,1)S(1)} %convolution_convert_fusion.3), channel_id=1, source_target_pairs={{0,24},{8,0},{16,8},{24,16},{32,56},{40,32},{48,40},{56,48},{64,88... | collective-permute-start | bytes 1572872 | tf_op jit(solution)/shard_map/ppermute | solution.py:22
  187.8 26.6 %collective-permute-start.29 = (bf16[256,1024]{1,0:T(8,128)(2,1)S(1)}, bf16[256,1024]{1,0:T(8,128)(2,1)S(1)}, u32[]{:S(2)}, u32[]{:S(2)}) collective-permute-start(bf16[256,1024]{1,0:T(8,128)(2,1)S(1)} %convolution_convert_fusion.4), channel_id=1, source_target_pairs={{0,16},{8,24},{16,0},{24,8},{32,48},{40,56},{48,32},{56,40},{64,80... | collective-permute-start | bytes 1572872 | tf_op jit(solution)/shard_map/ppermute | solution.py:22
  206.2 18.2 %collective-permute-start.28 = (bf16[256,1024]{1,0:T(8,128)(2,1)S(1)}, bf16[256,1024]{1,0:T(8,128)(2,1)S(1)}, u32[]{:S(2)}, u32[]{:S(2)}) collective-permute-start(bf16[256,1024]{1,0:T(8,128)(2,1)S(1)} %convolution_convert_fusion.5), channel_id=1, source_target_pairs={{0,8},{8,16},{16,24},{24,0},{32,40},{40,48},{48,56},{56,32},{64,72... | collective-permute-start | bytes 1572872 | tf_op jit(solution)/shard_map/ppermute | solution.py:22
  211.6 17.6 %collective-permute-start.39 = (bf16[256,256]{1,0:T(8,128)(2,1)S(1)}, bf16[256,256]{1,0:T(8,128)(2,1)S(1)}, u32[]{:S(2)}, u32[]{:S(2)}) collective-permute-start(bf16[256,256]{1,0:T(8,128)(2,1)S(1)} %get-tuple-element.56), channel_id=1, source_target_pairs={{0,24},{8,0},{16,8},{24,16},{32,56},{40,32},{48,40},{56,48},{64,88... | collective-permute-start | bytes 393224 | tf_op jit(solution)/shard_map/ppermute | solution.py:22
  211.7 18.5 %collective-permute-start.38 = (bf16[256,256]{1,0:T(8,128)(2,1)S(1)}, bf16[256,256]{1,0:T(8,128)(2,1)S(1)}, u32[]{:S(2)}, u32[]{:S(2)}) collective-permute-start(bf16[256,256]{1,0:T(8,128)(2,1)S(1)} %get-tuple-element.57), channel_id=1, source_target_pairs={{0,16},{8,24},{16,0},{24,8},{32,48},{40,56},{48,32},{56,40},{64,80... | collective-permute-start | bytes 393224 | tf_op jit(solution)/shard_map/ppermute | solution.py:22
  213.1 17.1 %collective-permute-start.37 = (bf16[256,256]{1,0:T(8,128)(2,1)S(1)}, bf16[256,256]{1,0:T(8,128)(2,1)S(1)}, u32[]{:S(2)}, u32[]{:S(2)}) collective-permute-start(bf16[256,256]{1,0:T(8,128)(2,1)S(1)} %get-tuple-element.55), channel_id=1, source_target_pairs={{0,8},{8,16},{16,24},{24,0},{32,40},{40,48},{48,56},{56,32},{64,72... | collective-permute-start | bytes 393224 | tf_op jit(solution)/shard_map/ppermute | solution.py:22
  (40 other events, 455.8 us)

commit v2 on v1

--- a/solution.py
+++ b/solution.py
@@ -44,15 +44,64 @@
 
 
 def gathered(x, move):
-    return [x] + [move(x, step) for step in range(1, RING)]
-
-
-def scattered(blocks, move):
-    arrived = [move(blocks[step], step) for step in range(1, RING)]
-    total = blocks[0].astype(jnp.float32)
-    for block in arrived:
-        total = total + block.astype(jnp.float32)
-    return total
+    return [x] + [move(x, step) for step in (1, 3, 2)]
+
+
+def ring_gather(blocks, moves):
+    blocks = lax.optimization_barrier(tuple(blocks))
+    near = []
+    for block, move in zip(blocks, moves):
+        near += [move(block, 1), move(block, 3)]
+    near = lax.optimization_barrier(tuple(near))
+    halves = []
+    for i, move in enumerate(moves):
+        half = near[2 * i].shape[0] // 2
+        halves += [(near[2 * i][:half], 1, move), (near[2 * i + 1][half:], 3, move)]
+    far = [move(block, step) for block, step, move in halves]
+    return [
+        (blocks[i], near[2 * i], near[2 * i + 1], far[2 * i], far[2 * i + 1])
+        for i in range(len(moves))
+    ]
+
+
+def ring_sum(parts, moves):
+    outgoing = []
+    for part in parts:
+        outgoing += [part[3], part[4]]
+    outgoing = lax.optimization_barrier(tuple(outgoing))
+    passing = []
+    for i, move in enumerate(moves):
+        passing += [move(outgoing[2 * i], 1), move(outgoing[2 * i + 1], 3)]
+    passing = lax.optimization_barrier(tuple(passing))
+    sent = []
+    for i, part in enumerate(parts):
+        half = part[3].shape[0]
+        after, before = part[1], part[2]
+        upper = after[:half] + passing[2 * i].astype(jnp.float32)
+        lower = before[half:] + passing[2 * i + 1].astype(jnp.float32)
+        sent += [
+            jnp.concatenate([upper, after[half:]], axis=0).astype(jnp.bfloat16),
+            jnp.concatenate([before[:half], lower], axis=0).astype(jnp.bfloat16),
+        ]
+    sent = lax.optimization_barrier(tuple(sent))
+    arrived = []
+    for i, move in enumerate(moves):
+        arrived += [move(sent[2 * i], 1), move(sent[2 * i + 1], 3)]
+    arrived = lax.optimization_barrier(tuple(arrived))
+    return [
+        part[0] + arrived[2 * i].astype(jnp.float32) + arrived[2 * i + 1].astype(jnp.float32)
+        for i, part in enumerate(parts)
+    ]
+
+
+def scattered(parts, moves):
+    sent = [[part[step].astype(jnp.bfloat16) for step in (1, 3, 2)] for part in parts]
+    sent = lax.optimization_barrier(tuple(block for blocks in sent for block in blocks))
+    order = [(i, k) for k in range(3) for i in range(len(parts))]
+    totals = [part[0] for part in parts]
+    for i, k in order:
+        totals[i] = totals[i] + moves[i](sent[3 * i + k], (1, 3, 2)[k]).astype(jnp.float32)
+    return totals
 
 
 def rms_factor(values):
@@ -72,7 +121,145 @@
     return lax.dot_general(a, b, (contract, ((), ())), preferred_element_type=jnp.float32)
 
 
-def attend_kernel(heads, index, ratio_ref, q_ref, cot_ref, kv_ref, gain_ref, *refs):
+def project_kernel(index, rows_ref, *refs):
+    uppers, lowers, outs = refs[:5], refs[5:10], refs[10:]
+    own_ref, after_ref, before_ref, far_key_ref, far_value_ref = outs
+    both = own_ref.shape[1]
+    head_dim = both // 2
+    half = uppers[0].shape[0]
+    lower_at = RING * half
+    order = ((uppers[0], 0), (uppers[1], half), (uppers[3], 2 * half))
+    order += ((uppers[4], 2 * half + half // 2), (uppers[2], 3 * half))
+
+    def product(o):
+        total = None
+        for block, at in order:
+            part = matmul(
+                rows_ref[:, at : at + block.shape[0]],
+                block[:, o * both : (o + 1) * both],
+                ((1,), (0,)),
+            )
+            total = part if total is None else total + part
+        if o == 2:
+            middle = lower_at + lowers[3].shape[0]
+            total = total + matmul(rows_ref[:, lower_at:middle], lowers[3][...], ((1,), (0,)))
+            return total + matmul(rows_ref[:, middle:], lowers[4][...], ((1,), (0,)))
+        return total + matmul(rows_ref[:, lower_at:], lowers[min(o, 2)][...], ((1,), (0,)))
+
+    for o in range(RING):
+        total = product(o)
+        target = (index[0] - o + RING) % RING
+
+        @pl.when(target == 0)
+        def _():
+            own_ref[...] = total
+
+        @pl.when(target == 1)
+        def _():
+            after_ref[...] = total.astype(after_ref.dtype)
+
+        @pl.when(target == 3)
+        def _():
+            before_ref[...] = total.astype(before_ref.dtype)
+
+        @pl.when(target == 2)
+        def _():
+            far_key_ref[...] = total[:, :head_dim].astype(far_key_ref.dtype)
+            far_value_ref[...] = total[:, head_dim:].astype(far_value_ref.dtype)
+
+
+VMEM = pl.BlockSpec(memory_space=pltpu.VMEM)
+SMEM = pl.BlockSpec(memory_space=pltpu.SMEM)
+
+
+def project(shift, rows, upper, lower):
+    count, depth = rows.shape
+    both = lower[0].shape[1]
+    wide = jax.ShapeDtypeStruct((count, both), jnp.bfloat16)
+    narrow = jax.ShapeDtypeStruct((count, both // 2), jnp.bfloat16)
+    return pl.pallas_call(
+        project_kernel,
+        in_specs=[SMEM] + [VMEM] * 11,
+        out_specs=[VMEM] * 5,
+        out_shape=[jax.ShapeDtypeStruct((count, both), jnp.float32), wide, wide, narrow, narrow],
+        compiler_params=pltpu.CompilerParams(vmem_limit_bytes=24 * 1024 * 1024),
+        cost_estimate=pl.CostEstimate(
+            flops=2 * RING * count * depth * both, bytes_accessed=8 * 1024 * 1024, transcendentals=0
+        ),
+    )(shift, rows, *upper, *lower)
+
+
+def passed_kernel(after_ref, before_ref, key_ref, value_ref, to_after_ref, to_before_ref):
+    head_dim = key_ref.shape[1]
+
+    def added(block, piece):
+        return (block.astype(jnp.float32) + piece.astype(jnp.float32)).astype(jnp.bfloat16)
+
+    to_after_ref[:, :head_dim] = added(after_ref[:, :head_dim], key_ref[...])
+    to_after_ref[:, head_dim:] = after_ref[:, head_dim:]
+    to_before_ref[:, :head_dim] = before_ref[:, :head_dim]
+    to_before_ref[:, head_dim:] = added(before_ref[:, head_dim:], value_ref[...])
+
+
+def passed(after, before, key_piece, value_piece):
+    return pl.pallas_call(
+        passed_kernel,
+        in_specs=[VMEM] * 4,
+        out_specs=[VMEM] * 2,
+        out_shape=[jax.ShapeDtypeStruct(after.shape, after.dtype)] * 2,
+        cost_estimate=pl.CostEstimate(
+            flops=after.size, bytes_accessed=10 * after.size, transcendentals=0
+        ),
+    )(after, before, key_piece, value_piece)
+
+
+def finish_kernel(own_ref, left_ref, right_ref, gain_ref, raw_ref, key_value_ref):
+    head_dim = raw_ref.shape[1]
+    total = own_ref[...] + left_ref[...].astype(jnp.float32) + right_ref[...].astype(jnp.float32)
+    raw = total[:, :head_dim]
+    raw_ref[...] = raw
+    key_value_ref[:, :head_dim] = (raw * rms_factor(raw) * gain_ref[...]).astype(jnp.bfloat16)
+    key_value_ref[:, head_dim:] = total[:, head_dim:].astype(jnp.bfloat16)
+
+
+def finish(own, left, right, gain):
+    rows, both = own.shape
+    return pl.pallas_call(
+        finish_kernel,
+        in_specs=[VMEM] * 4,
+        out_specs=[VMEM] * 2,
+        out_shape=[
+            jax.ShapeDtypeStruct((rows, both // 2), jnp.float32),
+            jax.ShapeDtypeStruct((rows, both), jnp.bfloat16),
+        ],
+        cost_estimate=pl.CostEstimate(
+            flops=6 * own.size, bytes_accessed=12 * own.size, transcendentals=rows
+        ),
+    )(own, left, right, gain[None, :])
+
+
+def turn_kernel(flag, raw_ref, grad_ref, other_ref, gain_ref, out_ref):
+    head_dim = raw_ref.shape[1]
+    grad = jnp.where(flag[0] != 0, other_ref[...], grad_ref[...])
+    raw = raw_ref[...]
+    d_raw = norm_back(raw, rms_factor(raw), gain_ref[...], grad[:, :head_dim].astype(jnp.float32))
+    out_ref[:, :head_dim] = d_raw.astype(jnp.bfloat16)
+    out_ref[:, head_dim:] = grad[:, head_dim:]
+
+
+def turn(flag, raw, grad, other, gain):
+    return pl.pallas_call(
+        turn_kernel,
+        in_specs=[SMEM] + [VMEM] * 4,
+        out_specs=VMEM,
+        out_shape=jax.ShapeDtypeStruct(grad.shape, jnp.bfloat16),
+        cost_estimate=pl.CostEstimate(
+            flops=6 * grad.size, bytes_accessed=8 * grad.size, transcendentals=raw.shape[0]
+        ),
+    )(flag, raw, grad, other, gain[None, :])
+
+
+def attend_kernel(heads, index, ratio_ref, q_ref, cot_ref, kv_ref, away_ref, gain_ref, *refs):
     context_ref, d_query_ref, d_kv_ref, d_key_sum, d_value_sum = refs[-5:]
     step = pl.program_id(0)
     head_dim = gain_ref.shape[1]
@@ -80,8 +267,9 @@
     count = index[1]
     ratio = ratio_ref[0]
     gain = gain_ref[...]
-    keys = kv_ref[:, :head_dim]
-    vals = kv_ref[:, head_dim:]
+    key_value = jnp.where(index[2] != 0, away_ref[...], kv_ref[...])
+    keys = key_value[:, :head_dim]
+    vals = key_value[:, head_dim:]
 
     def stacked(ref):
         parts = [ref[0, :, h * head_dim : (h + 1) * head_dim] for h in range(heads)]
@@ -126,7 +314,7 @@
         d_kv_ref[:, head_dim:] = d_value_sum[...].astype(d_kv_ref.dtype)
 
 
-def attend(own, count, ratio, query, cot, key_value, gain, earlier, heads=2):
+def attend(own, count, flag, ratio, query, cot, key_value, away, gain, earlier, heads=2):
     rows, both = key_value.shape
     head_dim = both // 2
     text = query.shape[1]
@@ -138,12 +326,13 @@
         block,
         block,
         whole((rows, both)),
+        whole((rows, both)),
         whole((1, head_dim)),
     ]
     aliases = {}
     if earlier:
         in_specs += [pl.BlockSpec(memory_space=pl.ANY)] * 2
-        aliases = {6: 0, 7: 1}
+        aliases = {7: 0, 8: 1}
     steps = query.shape[2] // width
     return pl.pallas_call(
         functools.partial(attend_kernel, heads),
@@ -169,11 +358,12 @@
             transcendentals=steps * heads * text * rows,
         ),
     )(
-        jnp.stack([own, count]).astype(jnp.int32),
+        jnp.stack([own, count, flag]).astype(jnp.int32),
         ratio,
         query,
         cot,
         key_value,
+        away,
         gain[None, :],
         *earlier,
     )
@@ -199,15 +389,6 @@
     z, y = rank // RING, rank % RING
     x, core = place // 2, place % 2
 
-    shard = jnp.concatenate([key_weight_matrix, value_weight_matrix], axis=1)
-    shard = exchange_xz(shard)
-    half = shard.shape[0] // 2
-    both = shard.shape[1]
-    upper = jnp.concatenate(gathered(shard[:half], along_z), axis=1)
-    lower = jnp.concatenate(gathered(shard[half:], along_y), axis=0)
-    upper = jnp.concatenate(gathered(upper, along_y), axis=0)
-    lower = jnp.concatenate(gathered(lower, along_z), axis=1)
-
     first = rank * samp_local
     every = jnp.arange(tiles.shape[0], dtype=jnp.int32)
     local_ids = first + jnp.arange(samp_local, dtype=jnp.int32)
@@ -222,6 +403,11 @@
     far_own = jnp.where(swaps, jnp.where(own_away[1], 1, 0), own_of_slot)
     home_tiles = lax.dynamic_slice_in_dim(tiles, first, samp_local)
 
+    shard = jnp.concatenate([key_weight_matrix, value_weight_matrix], axis=1)
+    half = shard.shape[0] // 2
+    both = shard.shape[1]
+    shard = exchange_xz(shard)
+
     columns = jnp.concatenate([image, other_core(image)], axis=2)
     feats = []
     for slot in (far_slot, 1 - far_slot):
@@ -232,52 +418,51 @@
                 start = (slot, 0, block * 2 * half + h * half)
                 parts.append(lax.dynamic_slice(columns, start, (1, img_rows, half))[0])
         feats.append(jnp.concatenate(parts, axis=1))
-
+    shard, *feats = lax.optimization_barrier((shard, *feats))
+    upper, lower = shard[:half], shard[half:]
+    moved = [[upper], [lower]]
+    for step in (1, 3, 2):
+        moved[0].append(along_z(upper, step))
+        moved[1].append(along_y(lower, step))
+    moved = lax.optimization_barrier(tuple(moved[0]) + tuple(moved[1]))
+    upper = jnp.concatenate([moved[i] for i in (0, 1, 3, 2)], axis=1)
+    lower = jnp.concatenate([moved[i] for i in (4, 5, 7, 6)], axis=0)
+    upper, lower = ring_gather([upper, lower], [along_y, along_z])
+
+    shift = ((z - x) % RING).astype(jnp.int32)[None]
+    made = [project(shift, rows, upper, lower) for rows in feats]
+    arrived = []
+    for own, after, before, far_key, far_value in made:
+        arrived.append((along_x(far_key, 1), along_x(far_value, 3)))
     raw_rows, key_values = [], []
-    for rows in feats:
-        blocks = []
-        for d in range(RING):
-            group = (z - x - d) % RING * both
-            weights = jnp.concatenate(
-                [
-                    lax.dynamic_slice_in_dim(upper, group, both, 1),
-                    lax.dynamic_slice_in_dim(lower, group, both, 1),
-                ],
-                axis=0,
-            )
-            block = matmul(rows, weights, ((1,), (0,)))
-            blocks.append(block if d == 0 else block.astype(jnp.bfloat16))
-        projected = scattered(blocks, along_x)
-        raw = projected[:, :head_dim]
-        keys = (raw * rms_factor(raw) * key_gain).astype(jnp.bfloat16)
+    for (own, after, before, _, _), (key_piece, value_piece) in zip(made, arrived):
+        to_after, to_before = passed(after, before, key_piece, value_piece)
+        left, right = along_x(to_after, 1), along_x(to_before, 3)
+        raw, key_value = finish(own, left, right, key_gain)
         raw_rows.append(raw)
-        key_values.append(
-            jnp.concatenate([keys, projected[:, head_dim:].astype(jnp.bfloat16)], axis=1)
-        )
-
+        key_values.append(key_value)
+
+    flag = swaps.astype(jnp.int32)
     away = along_z(key_values[0], RING // 2)
-    away = jnp.where(swaps, away, key_values[0])
     near_own = 1 - far_own
-    earlier = ()
-    grads = [None, None]
-    order = ((0, far_own, away), (1, near_own, key_values[1]))
-    for slot, own, key_value in order:
-        result = attend(
-            own, home_tiles[own], ratio, query, cotangent, key_value, query_gain, earlier
-        )
-        earlier = result[:2]
-        grads[slot] = result[2]
-    context, d_query = earlier
-    back = along_z(grads[0], RING // 2)
-    grads[0] = jnp.where(swaps, back, grads[0])
-
-    d_rows = [[], []]
-    for slot in (1, 0):
-        raw = raw_rows[slot]
-        grad = grads[slot].astype(jnp.float32)
-        d_raw = norm_back(raw, rms_factor(raw), key_gain, grad[:, :head_dim])
-        own = jnp.concatenate([d_raw.astype(jnp.bfloat16), grads[slot][:, head_dim:]], axis=1)
-        d_rows[slot] = gathered(own, along_x)
+    shared = (ratio, query, cotangent)
+    *earlier, far_grad = attend(
+        far_own, home_tiles[far_own], flag, *shared, key_values[0], away, query_gain, ()
+    )
+    back = along_z(far_grad, RING // 2)
+    context, d_query, near_grad = attend(
+        near_own, home_tiles[near_own], 0, *shared, key_values[1], key_values[1], query_gain, earlier
+    )
+
+    near_rows = turn(jnp.zeros_like(flag)[None], raw_rows[1], near_grad, near_grad, key_gain)
+    far_rows = turn(flag[None], raw_rows[0], far_grad, back, key_gain)
+    d_rows = []
+    for rows in (far_rows, near_rows):
+        d_rows.append([rows, along_x(rows, 1), along_x(rows, 3)])
+    for entry in d_rows:
+        left = along_x(entry[1][:, :head_dim], 1)
+        right = along_x(entry[2][:, head_dim:], 3)
+        entry.insert(2, jnp.concatenate([left, right], axis=1))
     by_source = jnp.stack([jnp.concatenate([d_rows[0][o], d_rows[1][o]], axis=0) for o in range(RING)])
     groups = [
         lax.dynamic_index_in_dim(by_source, (x - z - d) % RING, 0, keepdims=False)
@@ -286,24 +471,35 @@
     all_groups = jnp.concatenate(groups, axis=1)
     all_feats = jnp.concatenate(feats, axis=0)
 
-    def sent(block, d):
-        return block if d == 0 else block.astype(jnp.bfloat16)
-
-    upper_blocks, lower_blocks = [], []
     wide = RING * half
-    for d in range(RING):
-        o = -d % RING
-        rows = all_feats[:, o * half : (o + 1) * half]
-        upper_blocks.append(sent(matmul(rows, all_groups, ((0,), (0,))), d))
-        lower_blocks.append(sent(matmul(all_feats[:, wide:], groups[d], ((0,), (0,))), d))
-    upper_sum = scattered(upper_blocks, along_y)
-    lower_sum = scattered(lower_blocks, along_z)
-    upper_parts = [sent(upper_sum[:, d * both : (d + 1) * both], d) for d in range(RING)]
-    lower_parts = [
-        sent(lower_sum[-d % RING * half : (-d % RING + 1) * half], d) for d in range(RING)
-    ]
-    upper_sum = scattered(upper_parts, along_z)
-    lower_sum = scattered(lower_parts, along_y)
+
+    def upper_product(start, count):
+        return matmul(all_feats[:, start : start + count], all_groups, ((0,), (0,)))
+
+    def lower_product(start, count, d):
+        return matmul(all_feats[:, wide + start : wide + start + count], groups[d], ((0,), (0,)))
+
+    def sent(block):
+        return block.astype(jnp.bfloat16)
+
+    upper_parts = (
+        upper_product(0, half),
+        upper_product(3 * half, half),
+        upper_product(half, half),
+        sent(upper_product(2 * half, half // 2)),
+        sent(upper_product(2 * half + half // 2, half // 2)),
+    )
+    lower_parts = (
+        lower_product(0, wide, 0),
+        lower_product(0, wide, 1),
+        lower_product(0, wide, 3),
+        sent(lower_product(0, wide // 2, 2)),
+        sent(lower_product(wide // 2, wide // 2, 2)),
+    )
+    upper_sum, lower_sum = ring_sum([upper_parts, lower_parts], [along_y, along_z])
+    upper_parts = [upper_sum[:, d * both : (d + 1) * both] for d in range(RING)]
+    lower_parts = [lower_sum[-d % RING * half : (-d % RING + 1) * half] for d in range(RING)]
+    upper_sum, lower_sum = scattered([upper_parts, lower_parts], [along_z, along_y])
     share = jnp.concatenate([upper_sum, lower_sum], axis=0).astype(jnp.bfloat16)
     share = exchange_xz(share).astype(jnp.float32)
     return (context, d_query, share[:, :head_dim], share[:, head_dim:])

time: 252 us -> 242 us (0.960); the launches traced: 250 us -> 237 us
  waiting for transfers between devices: 110 us -> 60.5 us
  Pallas kernels: 10.6 us -> 37.8 us
  local copies, waits for them, and re-layouts: 13.1 us -> 39.6 us
  other arithmetic: 19.1 us -> 6.09 us
  matrix products: 11.9 us -> 6.36 us
    unnamed x54 -> x89, local copies, waits for them, and re-layouts: 4.18 us -> 31.4 us
    pallas_call x0 -> x8, Pallas kernels: none -> 26.2 us  [the longest x2 14 us: project(): pl.pallas_call(project_kernel, in_specs=[SMEM] + [VMEM] * 11, out_specs=[...]
    ppermute x14 -> x16, waiting for transfers between devices: 41 us -> 16.1 us  [along_z(): return lax.ppermute(x, 'dp', pairs)]
    ppermute x12 -> x16, starting transfers between devices: 34.6 us -> 21.4 us  [along_x(): return lax.ppermute(x, 'tensor', pairs)]
    ppermute x12 -> x14, waiting for transfers between devices: 29.3 us -> 20 us  [along_y(): return lax.ppermute(x, 'dp', pairs)]
    concatenate x9 -> x6, other arithmetic: 8.5 us -> 0.24 us  [the longest x2 0.07 us: ring_sum(): jnp.concatenate([upper, after[half:]], axis=0).astype(jnp.bfloat16)]
    ppermute x2, waiting for transfers between devices: 19 us -> 10.8 us  [exchange_xz(): return lax.ppermute(x, ('dp', 'tensor'), pairs)]
    ppermute x12 -> x14, starting transfers between devices: 14.3 us -> 22.3 us  [along_y(): return lax.ppermute(x, 'dp', pairs)]
  transfers between devices with their start and end apart: 41 -> 49, of which waited for: 22 -> 23; matrix products, arithmetic and copies ran while one was open for 11% -> 7% of each run, Pallas kernels for 2% -> 11%
where the time goes in v2:
time: 242 us; the launch traced here: 237 us
  starting transfers between devices  81.6 us (34%)
  waiting for transfers between devices  60.5 us (25%)
  local copies, waits for them, and re-layouts  39.6 us (16%)
  Pallas kernels  37.8 us (16%)
  matrix products  6.36 us (3%)
  other arithmetic  6.09 us (3%)
  between operations  5.46 us (2%)
    unnamed x89, local copies, waits for them, and re-layouts  31.4 us
    ppermute x16, starting transfers between devices, along_z(): return lax.ppermute(x, 'dp', pairs)  24.8 us
    ppermute x14, starting transfers between devices, along_y(): return lax.ppermute(x, 'dp', pairs)  22.3 us
    ppermute x16, starting transfers between devices, along_x(): return lax.ppermute(x, 'tensor', pairs)  21.4 us
    ppermute x14, waiting for transfers between devices, along_y(): return lax.ppermute(x, 'dp', pairs)  20 us
    ppermute x16, waiting for transfers between devices, along_z(): return lax.ppermute(x, 'dp', pairs)  16.1 us
    pallas_call x2, Pallas kernels, project(): pl.pallas_call(project_kernel, in_specs=[SMEM] + [VMEM] * 11, out_specs=[...  14 us
    ppermute x16, waiting for transfers between devices, along_x(): return lax.ppermute(x, 'tensor', pairs)  13.5 us
  transfers between devices with their start and end apart: 49, of which 23 were waited for; matrix products, arithmetic and copies ran while one was open for 7% of the time, Pallas kernels for 11%

profile of v2, /device:TPU:4, one launch (start us, length us, event | category | flops | bytes accessed | tf_op | source)
XLA Modules:
  0.0 237.3 jit_solution(280839807479917022)
XLA Ops:
  1.7 5.7 %collective-permute-start = (bf16[512,256]{1,0:T(8,128)(2,1)S(1)}, bf16[512,256]{1,0:T(8,128)(2,1)S(1)}, u32[]{:S(2)}, u32[]{:S(2)}) collective-permute-start(bf16[512,256]{1,0:T(8,128)(2,1)S(1)} %pad_maximum_fusion.8), channel_id=1, source_target_pairs={{0,0},{1,1},{2,32},{3,33},{4,64},{5,65},{6,96},{7,97},{8,8},{9,9},... | collective-permute-start | bytes 786440 | tf_op jit(solution)/shard_map/ppermute | solution.py:43
  15.2 5.5 %collective-permute-done = bf16[512,256]{1,0:T(8,128)(2,1)S(1)} collective-permute-done((bf16[512,256]{1,0:T(8,128)(2,1)S(1)}, bf16[512,256]{1,0:T(8,128)(2,1)S(1)}, u32[]{:S(2)}, u32[]{:S(2)}) %collective-permute-start) | collective-permute-done | bytes 262176 | tf_op jit(solution)/shard_map/ppermute | solution.py:43
  20.9 3.2 %collective-permute-start.3 = (bf16[256,256]{1,0:T(8,128)(2,1)S(1)}, bf16[256,256]{1,0:T(8,128)(2,1)S(1)}, u32[]{:S(2)}, u32[]{:S(2)}) collective-permute-start(bf16[256,256]{1,0:T(8,128)(2,1)S(1)} %get-tuple-element.69), channel_id=1, source_target_pairs={{0,96},{8,104},{16,112},{24,120},{32,0},{40,8},{48,16},{56,24},{64... | collective-permute-start | bytes 393224 | tf_op jit(solution)/shard_map/ppermute | solution.py:17
  27.3 3.1 %collective-permute-start.7 = (bf16[256,256]{1,0:T(8,128)(2,1)S(1)}, bf16[256,256]{1,0:T(8,128)(2,1)S(1)}, u32[]{:S(2)}, u32[]{:S(2)}) collective-permute-start(bf16[256,256]{1,0:T(8,128)(2,1)S(1)} %get-tuple-element.73), channel_id=1, source_target_pairs={{0,16},{8,24},{16,0},{24,8},{32,48},{40,56},{48,32},{56,40},{64,80... | collective-permute-start | bytes 393224 | tf_op jit(solution)/shard_map/ppermute | solution.py:22
  40.8 6.8 %collective-permute-done.8.refs_1_ = bf16[256,1024]{1,0:T(8,128)(2,1)S(1)} collective-permute-done((bf16[256,1024]{1,0:T(8,128)(2,1)S(1)}, bf16[256,1024]{1,0:T(8,128)(2,1)S(1)}, u32[]{:S(2)}, u32[]{:S(2)}) %collective-permute-start.8) | collective-permute-done | bytes 524320 | tf_op jit(solution)/shard_map/ppermute | solution.py:22
  52.5 3.2 %collective-permute-start.13 = (bf16[128,1024]{1,0:T(8,128)(2,1)}, bf16[128,1024]{1,0:T(8,128)(2,1)}, u32[]{:S(2)}, u32[]{:S(2)}) collective-permute-start(bf16[128,1024]{1,0:T(8,128)(2,1)} %slice.135), channel_id=1, source_target_pairs={{0,24},{8,0},{16,8},{24,16},{32,56},{40,32},{48,40},{56,48},{64,88... | collective-permute-start | bytes 786440 | tf_op jit(solution)/shard_map/ppermute | solution.py:22
  59.2 2.7 %collective-permute-start.15 = (bf16[512,256]{1,0:T(8,128)(2,1)}, bf16[512,256]{1,0:T(8,128)(2,1)}, u32[]{:S(2)}, u32[]{:S(2)}) collective-permute-start(bf16[512,256]{1,0:T(8,128)(2,1)} %slice.137), channel_id=1, source_target_pairs={{0,96},{8,104},{16,112},{24,120},{32,0},{40,8},{48,16},{56,24},{64... | collective-permute-start | bytes 786440 | tf_op jit(solution)/shard_map/ppermute | solution.py:17
  62.0 3.1 %collective-permute-done.14.refs_8_ = bf16[512,256]{1,0:T(8,128)(2,1)} collective-permute-done((bf16[512,256]{1,0:T(8,128)(2,1)}, bf16[512,256]{1,0:T(8,128)(2,1)}, u32[]{:S(2)}, u32[]{:S(2)}) %collective-permute-start.14) | collective-permute-done | bytes 262176 | tf_op jit(solution)/shard_map/ppermute | solution.py:17
  72.0 6.7 %shard_map.132 = (f32[512,256]{1,0:T(8,128)S(1)}, bf16[512,256]{1,0:T(8,128)(2,1)S(1)}, bf16[512,256]{1,0:T(8,128)(2,1)S(1)}, bf16[512,128]{1,0:T(8,128)(2,1)S(1)}, bf16[512,128]{1,0:T(8,128)(2,1)S(1)}) custom-call(s32[1]{0:T(128)} %bitcast.4.index, bf16[512,2048]{1,0:T(8,128)(2,1)S(1)} %copy-done.1, bf16[256,1024]{1,0:T(8,128)(2,1)S(1)} %pad_maximum_fusion.2.refs_0_, ...), custom_call_target="tpu_custom_call" | custom-call | flops 2147483648 | bytes 8388608 | tf_op jit(solution)/shard_map/pallas_call | solution.py:180
  80.9 2.7 %collective-permute-start.20 = (bf16[512,128]{1,0:T(8,128)(2,1)S(1)}, bf16[512,128]{1,0:T(8,128)(2,1)S(1)}, u32[]{:S(2)}, u32[]{:S(2)}) collective-permute-start(bf16[512,128]{1,0:T(8,128)(2,1)S(1)} %get-tuple-element.95), channel_id=1, source_target_pairs={{0,2},{1,3},{2,4},{3,5},{4,6},{5,7},{6,0},{7,1},{8,10},{9,11},{10,... | collective-permute-start | bytes 393224 | tf_op jit(solution)/shard_map/ppermute | solution.py:27
  86.1 3.0 %collective-permute-done.21.value_ref = bf16[512,128]{1,0:T(8,128)(2,1)S(1)} collective-permute-done((bf16[512,128]{1,0:T(8,128)(2,1)S(1)}, bf16[512,128]{1,0:T(8,128)(2,1)S(1)}, u32[]{:S(2)}, u32[]{:S(2)}) %collective-permute-start.21) | collective-permute-done | bytes 131104 | tf_op jit(solution)/shard_map/ppermute | solution.py:27
  91.7 3.2 %collective-permute-start.22 = (bf16[512,256]{1,0:T(8,128)(2,1)}, bf16[512,256]{1,0:T(8,128)(2,1)}, u32[]{:S(2)}, u32[]{:S(2)}) collective-permute-start(bf16[512,256]{1,0:T(8,128)(2,1)} %get-tuple-element.97), channel_id=1, source_target_pairs={{0,2},{1,3},{2,4},{3,5},{4,6},{5,7},{6,0},{7,1},{8,10},{9,11},{10,... | collective-permute-start | bytes 786440 | tf_op jit(solution)/shard_map/ppermute | solution.py:27
  103.7 3.7 %collective-permute-start.24 = (bf16[512,256]{1,0:T(8,128)(2,1)}, bf16[512,256]{1,0:T(8,128)(2,1)}, u32[]{:S(2)}, u32[]{:S(2)}) collective-permute-start(bf16[512,256]{1,0:T(8,128)(2,1)} %get-tuple-element.99.kv_ref), channel_id=1, source_target_pairs={{0,64},{8,72},{16,80},{24,88},{32,96},{40,104},{48,112},{56,120},{... | collective-permute-start | bytes 786440 | tf_op jit(solution)/shard_map/ppermute | solution.py:17
  111.5 7.3 %shard_map.129 = (f32[512,256]{1,0:T(8,128)S(1)}, bf16[512,256]{1,0:T(8,128)(2,1)S(1)}, bf16[512,256]{1,0:T(8,128)(2,1)S(1)}, bf16[512,128]{1,0:T(8,128)(2,1)}, bf16[512,128]{1,0:T(8,128)(2,1)S(1)}) custom-call(s32[1]{0:T(128)} %bitcast.4.index, bf16[512,2048]{1,0:T(8,128)(2,1)S(1)} %get-tuple-element.67.rows_ref, ...), custom_call_target="tpu_custom_call" | custom-call | flops 2147483648 | bytes 8388608 | tf_op jit(solution)/shard_map/pallas_call | solution.py:180
  136.4 6.2 %shard_map.135 = (bf16[2,128,1024]{2,1,0:T(8,128)(2,1)}, bf16[2,128,1024]{2,1,0:T(8,128)(2,1)}, bf16[512,256]{1,0:T(8,128)(2,1)S(1)}) custom-call(s32[3]{0:T(128)S(1)} %pad_add_fusion.1.index, f32[1]{0:T(128)S(6)} %tanh.3.ratio_ref, bf16[2,128,1024]{2,1,0:T(8,128)(2,1)S(1)} %copy-done.23, bf16[2,128,1024]{2,1,0:T(8,128)(2,1)S(1)} %copy-done.25, ...), custom_call_target="tpu_custom_call" | custom-call | flops 939524096 | bytes 1441792 | tf_op jit(solution)/shard_map/pallas_call | solution.py:337
  148.7 5.3 %shard_map.136 = (bf16[2,128,1024]{2,1,0:T(8,128)(2,1)}, bf16[2,128,1024]{2,1,0:T(8,128)(2,1)}, bf16[512,256]{1,0:T(8,128)(2,1)S(1)}) custom-call(s32[3]{0:T(128)S(1)} %pad_add_fusion.index, f32[1]{0:T(128)S(6)} %tanh.3.ratio_ref, bf16[2,128,1024]{2,1,0:T(8,128)(2,1)S(1)} %copy-done.24, ...), custom_call_target="tpu_custom_call", output_to_operand_aliasing={{0}: (7, {}), {1}: (8, {})} | custom-call | flops 939524096 | bytes 1441792 | tf_op jit(solution)/shard_map/pallas_call | solution.py:337
  165.3 2.9 %collective-permute-start.31 = (bf16[512,128]{1,0:T(8,128)(2,1)S(1)}, bf16[512,128]{1,0:T(8,128)(2,1)S(1)}, u32[]{:S(2)}, u32[]{:S(2)}) collective-permute-start(bf16[512,128]{1,0:T(8,128)(2,1)S(1)} %slice.171), channel_id=1, source_target_pairs={{0,2},{1,3},{2,4},{3,5},{4,6},{5,7},{6,0},{7,1},{8,10},{9,11},{10,... | collective-permute-start | bytes 393224 | tf_op jit(solution)/shard_map/ppermute | solution.py:27
  168.4 3.5 %collective-permute-start.28 = (bf16[512,128]{1,0:T(8,128)(2,1)S(1)}, bf16[512,128]{1,0:T(8,128)(2,1)S(1)}, u32[]{:S(2)}, u32[]{:S(2)}) collective-permute-start(bf16[512,128]{1,0:T(8,128)(2,1)S(1)} %slice.169), channel_id=1, source_target_pairs={{0,2},{1,3},{2,4},{3,5},{4,6},{5,7},{6,0},{7,1},{8,10},{9,11},{10,... | collective-permute-start | bytes 393224 | tf_op jit(solution)/shard_map/ppermute | solution.py:27
  181.3 3.2 %collective-permute-start.35 = (bf16[128,1024]{1,0:T(8,128)(2,1)S(1)}, bf16[128,1024]{1,0:T(8,128)(2,1)S(1)}, u32[]{:S(2)}, u32[]{:S(2)}) collective-permute-start(bf16[128,1024]{1,0:T(8,128)(2,1)S(1)} %convolution_convert_fusion.2), channel_id=1, source_target_pairs={{0,24},{8,0},{16,8},{24,16},{32,56},{40,32},{48,40},{56,48},{64,88... | collective-permute-start | bytes 786440 | tf_op jit(solution)/shard_map/ppermute | solution.py:22
  191.4 2.7 %collective-permute-done.36 = bf16[512,256]{1,0:T(8,128)(2,1)S(1)} collective-permute-done((bf16[512,256]{1,0:T(8,128)(2,1)S(1)}, bf16[512,256]{1,0:T(8,128)(2,1)S(1)}, u32[]{:S(2)}, u32[]{:S(2)}) %collective-permute-start.36) | collective-permute-done | bytes 262176 | tf_op jit(solution)/shard_map/ppermute | solution.py:17
  194.7 3.2 %collective-permute-start.39 = (bf16[256,1024]{1,0:T(8,128)(2,1)S(1)}, bf16[256,1024]{1,0:T(8,128)(2,1)S(1)}, u32[]{:S(2)}, u32[]{:S(2)}) collective-permute-start(bf16[256,1024]{1,0:T(8,128)(2,1)S(1)} %pad_maximum_fusion.5), channel_id=1, source_target_pairs={{0,24},{8,0},{16,8},{24,16},{32,56},{40,32},{48,40},{56,48},{64,88... | collective-permute-start | bytes 1572872 | tf_op jit(solution)/shard_map/ppermute | solution.py:22
  201.9 5.4 %collective-permute-done.38 = bf16[256,1024]{1,0:T(8,128)(2,1)S(1)} collective-permute-done((bf16[256,1024]{1,0:T(8,128)(2,1)S(1)}, bf16[256,1024]{1,0:T(8,128)(2,1)S(1)}, u32[]{:S(2)}, u32[]{:S(2)}) %collective-permute-start.38) | collective-permute-done | bytes 524320 | tf_op jit(solution)/shard_map/ppermute | solution.py:22
  224.1 7.2 %collective-permute-start.48 = (bf16[512,256]{1,0:T(8,128)(2,1)S(1)}, bf16[512,256]{1,0:T(8,128)(2,1)S(1)}, u32[]{:S(2)}, u32[]{:S(2)}) collective-permute-start(bf16[512,256]{1,0:T(8,128)(2,1)S(1)} %pad_maximum_fusion.9), channel_id=1, source_target_pairs={{0,0},{1,1},{2,32},{3,33},{4,64},{5,65},{6,96},{7,97},{8,8},{9,9},... | collective-permute-start | bytes 786440 | tf_op jit(solution)/shard_map/ppermute | solution.py:43
  231.2 5.3 %collective-permute-done.48 = bf16[512,256]{1,0:T(8,128)(2,1)S(1)} collective-permute-done((bf16[512,256]{1,0:T(8,128)(2,1)S(1)}, bf16[512,256]{1,0:T(8,128)(2,1)S(1)}, u32[]{:S(2)}, u32[]{:S(2)}) %collective-permute-start.48) | collective-permute-done | bytes 262176 | tf_op jit(solution)/shard_map/ppermute | solution.py:43
  (232 shorter events, 126.9 us)
Async XLA Ops:
  0.6 12.3 %collective-permute-start.1 = (bf16[2,512,1024]{2,1,0:T(8,128)(2,1)}, bf16[2,512,1024]{2,1,0:T(8,128)(2,1)S(1)}, u32[]{:S(2)}, u32[]{:S(2)}) collective-permute-start(bf16[2,512,1024]{2,1,0:T(8,128)(2,1)} %param.11), channel_id=1, source_target_pairs={{0,1},{1,0},{2,3},{3,2},{4,5},{5,4},{6,7},{7,6},{8,9},{9,8},{10,11... | collective-permute-start | bytes 6291464 | tf_op jit(solution)/shard_map/ppermute | solution.py:31
  1.7 19.0 %collective-permute-start = (bf16[512,256]{1,0:T(8,128)(2,1)S(1)}, bf16[512,256]{1,0:T(8,128)(2,1)S(1)}, u32[]{:S(2)}, u32[]{:S(2)}) collective-permute-start(bf16[512,256]{1,0:T(8,128)(2,1)S(1)} %pad_maximum_fusion.8), channel_id=1, source_target_pairs={{0,0},{1,1},{2,32},{3,33},{4,64},{5,65},{6,96},{7,97},{8,8},{9,9},... | collective-permute-start | bytes 786440 | tf_op jit(solution)/shard_map/ppermute | solution.py:43
  20.9 9.6 %collective-permute-start.3 = (bf16[256,256]{1,0:T(8,128)(2,1)S(1)}, bf16[256,256]{1,0:T(8,128)(2,1)S(1)}, u32[]{:S(2)}, u32[]{:S(2)}) collective-permute-start(bf16[256,256]{1,0:T(8,128)(2,1)S(1)} %get-tuple-element.69), channel_id=1, source_target_pairs={{0,96},{8,104},{16,112},{24,120},{32,0},{40,8},{48,16},{56,24},{64... | collective-permute-start | bytes 393224 | tf_op jit(solution)/shard_map/ppermute | solution.py:17
  34.2 13.3 %collective-permute-start.8 = (bf16[256,1024]{1,0:T(8,128)(2,1)S(1)}, bf16[256,1024]{1,0:T(8,128)(2,1)S(1)}, u32[]{:S(2)}, u32[]{:S(2)}) collective-permute-start(bf16[256,1024]{1,0:T(8,128)(2,1)S(1)} %pad_maximum_fusion.2.refs_0_), channel_id=1, source_target_pairs={{0,8},{8,16},{16,24},{24,0},{32,40},{40,48},{48,56},{56,32},{64,72... | collective-permute-start | bytes 1572872 | tf_op jit(solution)/shard_map/ppermute | solution.py:22
  35.5 12.1 %collective-permute-start.9 = (bf16[256,1024]{1,0:T(8,128)(2,1)S(1)}, bf16[256,1024]{1,0:T(8,128)(2,1)S(1)}, u32[]{:S(2)}, u32[]{:S(2)}) collective-permute-start(bf16[256,1024]{1,0:T(8,128)(2,1)S(1)} %pad_maximum_fusion.2.refs_0_), channel_id=1, source_target_pairs={{0,24},{8,0},{16,8},{24,16},{32,56},{40,32},{48,40},{56,48},{64,88... | collective-permute-start | bytes 1572872 | tf_op jit(solution)/shard_map/ppermute | solution.py:22
  37.5 12.7 %collective-permute-start.10 = (bf16[1024,256]{1,0:T(8,128)(2,1)S(1)}, bf16[1024,256]{1,0:T(8,128)(2,1)S(1)}, u32[]{:S(2)}, u32[]{:S(2)}) collective-permute-start(bf16[1024,256]{1,0:T(8,128)(2,1)S(1)} %pad_maximum_fusion.3.refs_5_), channel_id=1, source_target_pairs={{0,32},{8,40},{16,48},{24,56},{32,64},{40,72},{48,80},{56,88},{64,... | collective-permute-start | bytes 1572872 | tf_op jit(solution)/shard_map/ppermute | solution.py:17
  38.7 11.6 %collective-permute-start.11 = (bf16[1024,256]{1,0:T(8,128)(2,1)S(1)}, bf16[1024,256]{1,0:T(8,128)(2,1)S(1)}, u32[]{:S(2)}, u32[]{:S(2)}) collective-permute-start(bf16[1024,256]{1,0:T(8,128)(2,1)S(1)} %pad_maximum_fusion.3.refs_5_), channel_id=1, source_target_pairs={{0,96},{8,104},{16,112},{24,120},{32,0},{40,8},{48,16},{56,24},{64... | collective-permute-start | bytes 1572872 | tf_op jit(solution)/shard_map/ppermute | solution.py:17
  51.7 10.2 %collective-permute-start.12 = (bf16[128,1024]{1,0:T(8,128)(2,1)}, bf16[128,1024]{1,0:T(8,128)(2,1)S(1)}, u32[]{:S(2)}, u32[]{:S(2)}) collective-permute-start(bf16[128,1024]{1,0:T(8,128)(2,1)} %slice.134), channel_id=1, source_target_pairs={{0,8},{8,16},{16,24},{24,0},{32,40},{40,48},{48,56},{56,32},{64,72... | collective-permute-start | bytes 786440 | tf_op jit(solution)/shard_map/ppermute | solution.py:22
  52.5 9.5 %collective-permute-start.13 = (bf16[128,1024]{1,0:T(8,128)(2,1)}, bf16[128,1024]{1,0:T(8,128)(2,1)}, u32[]{:S(2)}, u32[]{:S(2)}) collective-permute-start(bf16[128,1024]{1,0:T(8,128)(2,1)} %slice.135), channel_id=1, source_target_pairs={{0,24},{8,0},{16,8},{24,16},{32,56},{40,32},{48,40},{56,48},{64,88... | collective-permute-start | bytes 786440 | tf_op jit(solution)/shard_map/ppermute | solution.py:22
  103.7 29.6 %collective-permute-start.24 = (bf16[512,256]{1,0:T(8,128)(2,1)}, bf16[512,256]{1,0:T(8,128)(2,1)}, u32[]{:S(2)}, u32[]{:S(2)}) collective-permute-start(bf16[512,256]{1,0:T(8,128)(2,1)} %get-tuple-element.99.kv_ref), channel_id=1, source_target_pairs={{0,64},{8,72},{16,80},{24,88},{32,96},{40,104},{48,112},{56,120},{... | collective-permute-start | bytes 786440 | tf_op jit(solution)/shard_map/ppermute | solution.py:17
  131.3 13.0 %collective-permute-start.18 = (bf16[512,256]{1,0:T(8,128)(2,1)}, bf16[512,256]{1,0:T(8,128)(2,1)S(1)}, u32[]{:S(2)}, u32[]{:S(2)}) collective-permute-start(bf16[512,256]{1,0:T(8,128)(2,1)} %get-tuple-element.88), channel_id=1, source_target_pairs={{0,2},{1,3},{2,4},{3,5},{4,6},{5,7},{6,0},{7,1},{8,10},{9,11},{10,... | collective-permute-start | bytes 786440 | tf_op jit(solution)/shard_map/ppermute | solution.py:27
  132.5 12.5 %collective-permute-start.19 = (bf16[512,256]{1,0:T(8,128)(2,1)}, bf16[512,256]{1,0:T(8,128)(2,1)S(1)}, u32[]{:S(2)}, u32[]{:S(2)}) collective-permute-start(bf16[512,256]{1,0:T(8,128)(2,1)} %get-tuple-element.89), channel_id=1, source_target_pairs={{0,6},{1,7},{2,0},{3,1},{4,2},{5,3},{6,4},{7,5},{8,14},{9,15},{10,... | collective-permute-start | bytes 786440 | tf_op jit(solution)/shard_map/ppermute | solution.py:27
  142.6 16.2 %collective-permute-start.25 = (bf16[512,256]{1,0:T(8,128)(2,1)S(1)}, bf16[512,256]{1,0:T(8,128)(2,1)}, u32[]{:S(2)}, u32[]{:S(2)}) collective-permute-start(bf16[512,256]{1,0:T(8,128)(2,1)S(1)} %get-tuple-element.105.grad_ref), channel_id=1, source_target_pairs={{0,64},{8,72},{16,80},{24,88},{32,96},{40,104},{48,112},{56,120},{... | collective-permute-start | bytes 786440 | tf_op jit(solution)/shard_map/ppermute | solution.py:17
  156.8 8.0 %collective-permute-start.32 = (bf16[512,256]{1,0:T(8,128)(2,1)}, bf16[512,256]{1,0:T(8,128)(2,1)S(1)}, u32[]{:S(2)}, u32[]{:S(2)}) collective-permute-start(bf16[512,256]{1,0:T(8,128)(2,1)} %shard_map.138), channel_id=1, source_target_pairs={{0,6},{1,7},{2,0},{3,1},{4,2},{5,3},{6,4},{7,5},{8,14},{9,15},{10,... | collective-permute-start | bytes 786440 | tf_op jit(solution)/shard_map/ppermute | solution.py:27
  181.2 10.2 %collective-permute-start.34 = (bf16[128,1024]{1,0:T(8,128)(2,1)S(1)}, bf16[128,1024]{1,0:T(8,128)(2,1)S(1)}, u32[]{:S(2)}, u32[]{:S(2)}) collective-permute-start(bf16[128,1024]{1,0:T(8,128)(2,1)S(1)} %convolution_convert_fusion.3), channel_id=1, source_target_pairs={{0,8},{8,16},{16,24},{24,0},{32,40},{40,48},{48,56},{56,32},{64,72... | collective-permute-start | bytes 786440 | tf_op jit(solution)/shard_map/ppermute | solution.py:22
  181.3 10.1 %collective-permute-start.35 = (bf16[128,1024]{1,0:T(8,128)(2,1)S(1)}, bf16[128,1024]{1,0:T(8,128)(2,1)S(1)}, u32[]{:S(2)}, u32[]{:S(2)}) collective-permute-start(bf16[128,1024]{1,0:T(8,128)(2,1)S(1)} %convolution_convert_fusion.2), channel_id=1, source_target_pairs={{0,24},{8,0},{16,8},{24,16},{32,56},{40,32},{48,40},{56,48},{64,88... | collective-permute-start | bytes 786440 | tf_op jit(solution)/shard_map/ppermute | solution.py:22
  184.5 9.6 %collective-permute-start.36 = (bf16[512,256]{1,0:T(8,128)(2,1)S(1)}, bf16[512,256]{1,0:T(8,128)(2,1)S(1)}, u32[]{:S(2)}, u32[]{:S(2)}) collective-permute-start(bf16[512,256]{1,0:T(8,128)(2,1)S(1)} %convolution_convert_fusion.1), channel_id=1, source_target_pairs={{0,32},{8,40},{16,48},{24,56},{32,64},{40,72},{48,80},{56,88},{64,... | collective-permute-start | bytes 786440 | tf_op jit(solution)/shard_map/ppermute | solution.py:17
  185.7 8.4 %collective-permute-start.37 = (bf16[512,256]{1,0:T(8,128)(2,1)S(1)}, bf16[512,256]{1,0:T(8,128)(2,1)S(1)}, u32[]{:S(2)}, u32[]{:S(2)}) collective-permute-start(bf16[512,256]{1,0:T(8,128)(2,1)S(1)} %convolution_convert_fusion), channel_id=1, source_target_pairs={{0,96},{8,104},{16,112},{24,120},{32,0},{40,8},{48,16},{56,24},{64... | collective-permute-start | bytes 786440 | tf_op jit(solution)/shard_map/ppermute | solution.py:17
  194.6 12.7 %collective-permute-start.38 = (bf16[256,1024]{1,0:T(8,128)(2,1)S(1)}, bf16[256,1024]{1,0:T(8,128)(2,1)S(1)}, u32[]{:S(2)}, u32[]{:S(2)}) collective-permute-start(bf16[256,1024]{1,0:T(8,128)(2,1)S(1)} %pad_maximum_fusion.4), channel_id=1, source_target_pairs={{0,8},{8,16},{16,24},{24,0},{32,40},{40,48},{48,56},{56,32},{64,72... | collective-permute-start | bytes 1572872 | tf_op jit(solution)/shard_map/ppermute | solution.py:22
  194.7 12.6 %collective-permute-start.39 = (bf16[256,1024]{1,0:T(8,128)(2,1)S(1)}, bf16[256,1024]{1,0:T(8,128)(2,1)S(1)}, u32[]{:S(2)}, u32[]{:S(2)}) collective-permute-start(bf16[256,1024]{1,0:T(8,128)(2,1)S(1)} %pad_maximum_fusion.5), channel_id=1, source_target_pairs={{0,24},{8,0},{16,8},{24,16},{32,56},{40,32},{48,40},{56,48},{64,88... | collective-permute-start | bytes 1572872 | tf_op jit(solution)/shard_map/ppermute | solution.py:22
  197.9 11.8 %collective-permute-start.40 = (bf16[1024,256]{1,0:T(8,128)(2,1)S(1)}, bf16[1024,256]{1,0:T(8,128)(2,1)S(1)}, u32[]{:S(2)}, u32[]{:S(2)}) collective-permute-start(bf16[1024,256]{1,0:T(8,128)(2,1)S(1)} %pad_maximum_fusion.6), channel_id=1, source_target_pairs={{0,32},{8,40},{16,48},{24,56},{32,64},{40,72},{48,80},{56,88},{64,... | collective-permute-start | bytes 1572872 | tf_op jit(solution)/shard_map/ppermute | solution.py:17
  199.3 10.4 %collective-permute-start.41 = (bf16[1024,256]{1,0:T(8,128)(2,1)S(1)}, bf16[1024,256]{1,0:T(8,128)(2,1)S(1)}, u32[]{:S(2)}, u32[]{:S(2)}) collective-permute-start(bf16[1024,256]{1,0:T(8,128)(2,1)S(1)} %pad_maximum_fusion.7), channel_id=1, source_target_pairs={{0,96},{8,104},{16,112},{24,120},{32,0},{40,8},{48,16},{56,24},{64... | collective-permute-start | bytes 1572872 | tf_op jit(solution)/shard_map/ppermute | solution.py:17
  213.6 8.2 %collective-permute-start.44 = (bf16[256,256]{1,0:T(8,128)(2,1)S(1)}, bf16[256,256]{1,0:T(8,128)(2,1)S(1)}, u32[]{:S(2)}, u32[]{:S(2)}) collective-permute-start(bf16[256,256]{1,0:T(8,128)(2,1)S(1)} %get-tuple-element.126), channel_id=1, source_target_pairs={{0,64},{8,72},{16,80},{24,88},{32,96},{40,104},{48,112},{56,120},{... | collective-permute-start | bytes 393224 | tf_op jit(solution)/shard_map/ppermute | solution.py:17
  224.1 12.5 %collective-permute-start.48 = (bf16[512,256]{1,0:T(8,128)(2,1)S(1)}, bf16[512,256]{1,0:T(8,128)(2,1)S(1)}, u32[]{:S(2)}, u32[]{:S(2)}) collective-permute-start(bf16[512,256]{1,0:T(8,128)(2,1)S(1)} %pad_maximum_fusion.9), channel_id=1, source_target_pairs={{0,0},{1,1},{2,32},{3,33},{4,64},{5,65},{6,96},{7,97},{8,8},{9,9},... | collective-permute-start | bytes 786440 | tf_op jit(solution)/shard_map/ppermute | solution.py:43
  (65 other events, 288.0 us)

commit v3 on v1

--- a/solution.py
+++ b/solution.py
@@ -44,13 +44,21 @@
 
 
 def gathered(x, move):
-    return [x] + [move(x, step) for step in range(1, RING)]
-
-
-def scattered(blocks, move):
-    arrived = [move(blocks[step], step) for step in range(1, RING)]
+    far, after, before = (move(x, step) for step in (2, 1, 3))
+    return [x, after, far, before]
+
+
+def scattered(parts, moves):
+    totals = [[part[0]] for part in parts]
+    for step in (2, 1, 3):
+        for i, move in enumerate(moves):
+            totals[i].append(move(parts[i][step].astype(jnp.bfloat16), step))
+    return totals
+
+
+def summed(blocks):
     total = blocks[0].astype(jnp.float32)
-    for block in arrived:
+    for block in blocks[1:]:
         total = total + block.astype(jnp.float32)
     return total
 
@@ -72,7 +80,221 @@
     return lax.dot_general(a, b, (contract, ((), ())), preferred_element_type=jnp.float32)
 
 
-def attend_kernel(heads, index, ratio_ref, q_ref, cot_ref, kv_ref, gain_ref, *refs):
+VMEM = pl.BlockSpec(memory_space=pltpu.VMEM)
+SMEM = pl.BlockSpec(memory_space=pltpu.SMEM)
+HBM = pl.BlockSpec(memory_space=pltpu.HBM)
+PARAMS = pltpu.CompilerParams(vmem_limit_bytes=60 * 1024 * 1024)
+
+
+def arrange_kernel(half, index, own_ref, other_ref, out_ref, sems):
+    slots, rows, depth = own_ref.shape
+    waits = []
+    for s in range(slots):
+        for h in range(2):
+            for o in range(RING):
+                block = ((index[0] - o + RING) % RING) ^ (2 * index[1])
+                start = pl.multiple_of(block % 2 * 2 * half + h * half, half)
+                target = out_ref.at[pl.ds(s * rows, rows), pl.ds((h * RING + o) * half, half)]
+                sem = sems.at[len(waits)]
+                columns = pl.ds(start, half)
+                own = pltpu.make_async_copy(own_ref.at[s ^ index[2], :, columns], target, sem)
+                other = pltpu.make_async_copy(other_ref.at[s ^ index[2], :, columns], target, sem)
+                pl.when(block < 2)(own.start)
+                pl.when(block >= 2)(other.start)
+                waits.append(own)
+    for copy in waits:
+        copy.wait()
+
+
+def arrange(index, own, other, half):
+    slots, rows, depth = own.shape
+    return pl.pallas_call(
+        functools.partial(arrange_kernel, half),
+        in_specs=[SMEM, HBM, HBM],
+        out_specs=HBM,
+        out_shape=jax.ShapeDtypeStruct((slots * rows, 2 * depth), own.dtype),
+        scratch_shapes=[pltpu.SemaphoreType.DMA((slots * 2 * RING,))],
+        compiler_params=PARAMS,
+        cost_estimate=pl.CostEstimate(flops=0, bytes_accessed=8 * own.size, transcendentals=0),
+    )(index, own, other)
+
+
+def project_kernel(index, rows_ref, *refs):
+    uppers, lowers, outs = refs[:RING], refs[RING : 2 * RING], refs[2 * RING : 3 * RING]
+    rows, weights, stage, row_sems, sems, out_sems = refs[3 * RING :]
+    half = uppers[0].shape[0]
+    both = lowers[0].shape[1]
+    slots = row_sems.shape[0]
+    count = rows.shape[0] // slots
+    row_copies, copies = [], []
+    for s in range(slots):
+        part = pl.ds(s * count, count)
+        row_copies.append(pltpu.make_async_copy(rows_ref.at[part], rows.at[part], row_sems.at[s]))
+    row_copies[0].start()
+    for o in range(RING):
+        for k in range(RING):
+            source = uppers[k].at[:, pl.ds(o * both, both)]
+            target = weights.at[o, pl.ds(k * half, half)]
+            copies.append(pltpu.make_async_copy(source, target, sems.at[o, k]))
+        target = weights.at[o, pl.ds(RING * half, RING * half)]
+        copies.append(pltpu.make_async_copy(lowers[o], target, sems.at[o, RING]))
+    for copy in copies:
+        copy.start()
+    for copy in row_copies[1:]:
+        copy.start()
+    row_copies[0].wait()
+    for copy in copies:
+        copy.wait()
+    stores = []
+    for s in range(slots):
+        if s:
+            row_copies[s].wait()
+        for d in (2, 1, 3, 0):
+            o = (index[0] - d + RING) % RING
+            part = pl.ds(s * count, count)
+            stage[d, part] = matmul(rows[part], weights[o], ((1,), (0,))).astype(stage.dtype)
+            store = pltpu.make_async_copy(stage.at[d, part], outs[d].at[part], out_sems.at[d, s])
+            store.start()
+            stores.append(store)
+    for store in stores:
+        store.wait()
+
+
+def project(shift, rows, uppers, lowers):
+    count, depth = rows.shape
+    both = lowers[0].shape[1]
+    slots = 2
+    return pl.pallas_call(
+        project_kernel,
+        in_specs=[SMEM] + [HBM] * (1 + 2 * RING),
+        out_specs=[HBM] * RING,
+        out_shape=[jax.ShapeDtypeStruct((count, both), jnp.bfloat16)] * RING,
+        scratch_shapes=[
+            pltpu.VMEM((count, depth), jnp.bfloat16),
+            pltpu.VMEM((RING, depth, both), jnp.bfloat16),
+            pltpu.VMEM((RING, count, both), jnp.bfloat16),
+            pltpu.SemaphoreType.DMA((slots,)),
+            pltpu.SemaphoreType.DMA((RING, RING + 1)),
+            pltpu.SemaphoreType.DMA((RING, slots)),
+        ],
+        compiler_params=PARAMS,
+        cost_estimate=pl.CostEstimate(
+            flops=2 * RING * count * depth * both,
+            bytes_accessed=2 * count * depth + 2 * RING * both * (depth + count),
+            transcendentals=0,
+        ),
+    )(shift, rows, *uppers, *lowers)
+
+
+def finish_kernel(own_ref, far_ref, left_ref, right_ref, gain_ref, raw_ref, first_ref, second_ref):
+    step = pl.program_id(0)
+    head_dim = raw_ref.shape[1]
+    total = summed([own_ref[...], far_ref[...], left_ref[...], right_ref[...]])
+    raw = total[:, :head_dim]
+    raw_ref[...] = raw
+    keys = (raw * rms_factor(raw) * gain_ref[...]).astype(jnp.bfloat16)
+    vals = total[:, head_dim:].astype(jnp.bfloat16)
+    parts = pl.num_programs(0) // 2
+
+    @pl.when(step < parts)
+    def _():
+        first_ref[:, :head_dim] = keys
+        first_ref[:, head_dim:] = vals
+
+    @pl.when(step >= parts)
+    def _():
+        second_ref[:, :head_dim] = keys
+        second_ref[:, head_dim:] = vals
+
+
+def finish(blocks, gain, parts=2):
+    rows, both = blocks[0].shape
+    count = rows // (2 * parts)
+    block = pl.BlockSpec((count, both), lambda i: (i, 0))
+    return pl.pallas_call(
+        finish_kernel,
+        grid=(2 * parts,),
+        in_specs=[block] * RING + [pl.BlockSpec((1, both // 2), lambda i: (0, 0))],
+        out_specs=[
+            pl.BlockSpec((count, both // 2), lambda i: (i, 0)),
+            pl.BlockSpec((count, both), lambda i: (jnp.minimum(i, parts - 1), 0)),
+            pl.BlockSpec((count, both), lambda i: (jnp.maximum(i - parts, 0), 0)),
+        ],
+        out_shape=[
+            jax.ShapeDtypeStruct((rows, both // 2), jnp.float32),
+            jax.ShapeDtypeStruct((rows // 2, both), jnp.bfloat16),
+            jax.ShapeDtypeStruct((rows // 2, both), jnp.bfloat16),
+        ],
+        compiler_params=PARAMS,
+        cost_estimate=pl.CostEstimate(
+            flops=6 * rows * both, bytes_accessed=12 * rows * both, transcendentals=rows
+        ),
+    )(*blocks, gain[None, :])
+
+
+def turn_kernel(flag, raw_ref, grad_ref, other_ref, gain_ref, out_ref):
+    head_dim = raw_ref.shape[1]
+    grad = jnp.where(flag[0] != 0, other_ref[...], grad_ref[...])
+    raw = raw_ref[...]
+    d_raw = norm_back(raw, rms_factor(raw), gain_ref[...], grad[:, :head_dim].astype(jnp.float32))
+    out_ref[:, :head_dim] = d_raw.astype(jnp.bfloat16)
+    out_ref[:, head_dim:] = grad[:, head_dim:]
+
+
+def turn(flag, slot, raw, grad, other, gain, parts=2):
+    rows, both = grad.shape
+    count = rows // parts
+    block = pl.BlockSpec((count, both), lambda i: (i, 0))
+    return pl.pallas_call(
+        turn_kernel,
+        grid=(parts,),
+        in_specs=[
+            SMEM,
+            pl.BlockSpec((count, both // 2), lambda i: (slot * parts + i, 0)),
+            block,
+            block,
+            pl.BlockSpec((1, both // 2), lambda i: (0, 0)),
+        ],
+        out_specs=block,
+        out_shape=jax.ShapeDtypeStruct(grad.shape, jnp.bfloat16),
+        compiler_params=PARAMS,
+        cost_estimate=pl.CostEstimate(
+            flops=6 * grad.size, bytes_accessed=8 * grad.size, transcendentals=rows
+        ),
+    )(flag, raw, grad, other, gain[None, :])
+
+
+def collect_kernel(index, *refs):
+    sources, out_ref, sems = refs[:-2], refs[-2], refs[-1]
+    rows, both = sources[0].shape
+    copies = []
+    for i, source in enumerate(sources):
+        slot, o = i // RING, i % RING
+        start = pl.multiple_of((index[0] - o + RING) % RING * both, both)
+        target = out_ref.at[pl.ds(slot * rows, rows), pl.ds(start, both)]
+        copies.append(pltpu.make_async_copy(source, target, sems.at[i]))
+    for copy in copies:
+        copy.start()
+    for copy in copies:
+        copy.wait()
+
+
+def collect(shift, first, second):
+    rows, both = first[0].shape
+    return pl.pallas_call(
+        collect_kernel,
+        in_specs=[SMEM] + [HBM] * (2 * RING),
+        out_specs=HBM,
+        out_shape=jax.ShapeDtypeStruct((2 * rows, RING * both), first[0].dtype),
+        scratch_shapes=[pltpu.SemaphoreType.DMA((2 * RING,))],
+        compiler_params=PARAMS,
+        cost_estimate=pl.CostEstimate(
+            flops=0, bytes_accessed=8 * RING * rows * both, transcendentals=0
+        ),
+    )(shift, *first, *second)
+
+
+def attend_kernel(heads, index, ratio_ref, q_ref, cot_ref, kv_ref, away_ref, gain_ref, *refs):
     context_ref, d_query_ref, d_kv_ref, d_key_sum, d_value_sum = refs[-5:]
     step = pl.program_id(0)
     head_dim = gain_ref.shape[1]
@@ -80,8 +302,9 @@
     count = index[1]
     ratio = ratio_ref[0]
     gain = gain_ref[...]
-    keys = kv_ref[:, :head_dim]
-    vals = kv_ref[:, head_dim:]
+    key_value = jnp.where(index[2] != 0, away_ref[...], kv_ref[...])
+    keys = key_value[:, :head_dim]
+    vals = key_value[:, head_dim:]
 
     def stacked(ref):
         parts = [ref[0, :, h * head_dim : (h + 1) * head_dim] for h in range(heads)]
@@ -126,7 +349,7 @@
         d_kv_ref[:, head_dim:] = d_value_sum[...].astype(d_kv_ref.dtype)
 
 
-def attend(own, count, ratio, query, cot, key_value, gain, earlier, heads=2):
+def attend(own, count, flag, ratio, query, cot, key_value, away, gain, earlier, heads=2):
     rows, both = key_value.shape
     head_dim = both // 2
     text = query.shape[1]
@@ -138,12 +361,13 @@
         block,
         block,
         whole((rows, both)),
+        whole((rows, both)),
         whole((1, head_dim)),
     ]
     aliases = {}
     if earlier:
         in_specs += [pl.BlockSpec(memory_space=pl.ANY)] * 2
-        aliases = {6: 0, 7: 1}
+        aliases = {7: 0, 8: 1}
     steps = query.shape[2] // width
     return pl.pallas_call(
         functools.partial(attend_kernel, heads),
@@ -161,7 +385,7 @@
         ],
         input_output_aliases=aliases,
         compiler_params=pltpu.CompilerParams(
-            dimension_semantics=("arbitrary",), vmem_limit_bytes=24 * 1024 * 1024
+            vmem_limit_bytes=60 * 1024 * 1024
         ),
         cost_estimate=pl.CostEstimate(
             flops=14 * steps * heads * text * rows * head_dim,
@@ -169,11 +393,12 @@
             transcendentals=steps * heads * text * rows,
         ),
     )(
-        jnp.stack([own, count]).astype(jnp.int32),
+        jnp.stack([own, count, flag]).astype(jnp.int32),
         ratio,
         query,
         cot,
         key_value,
+        away,
         gain[None, :],
         *earlier,
     )
@@ -199,14 +424,18 @@
     z, y = rank // RING, rank % RING
     x, core = place // 2, place % 2
 
-    shard = jnp.concatenate([key_weight_matrix, value_weight_matrix], axis=1)
-    shard = exchange_xz(shard)
-    half = shard.shape[0] // 2
-    both = shard.shape[1]
-    upper = jnp.concatenate(gathered(shard[:half], along_z), axis=1)
-    lower = jnp.concatenate(gathered(shard[half:], along_y), axis=0)
-    upper = jnp.concatenate(gathered(upper, along_y), axis=0)
-    lower = jnp.concatenate(gathered(lower, along_z), axis=1)
+    half = key_weight_matrix.shape[0] // 2
+    both = 2 * head_dim
+    halves = []
+    for start in (0, half):
+        key_rows = key_weight_matrix[start : start + half]
+        value_rows = value_weight_matrix[start : start + half]
+        halves.append(jnp.concatenate([key_rows, value_rows], axis=1))
+    *halves, image = lax.optimization_barrier((*halves, image))
+    upper, lower = (exchange_xz(rows) for rows in halves)
+    upper = jnp.concatenate(gathered(upper, along_z), axis=1)
+    lower = jnp.concatenate(gathered(lower, along_y), axis=0)
+    uppers, lowers = gathered(upper, along_y), gathered(lower, along_z)
 
     first = rank * samp_local
     every = jnp.arange(tiles.shape[0], dtype=jnp.int32)
@@ -222,89 +451,44 @@
     far_own = jnp.where(swaps, jnp.where(own_away[1], 1, 0), own_of_slot)
     home_tiles = lax.dynamic_slice_in_dim(tiles, first, samp_local)
 
-    columns = jnp.concatenate([image, other_core(image)], axis=2)
-    feats = []
-    for slot in (far_slot, 1 - far_slot):
-        parts = []
-        for h in range(2):
-            for o in range(RING):
-                block = ((y - o) % RING) ^ (2 * core)
-                start = (slot, 0, block * 2 * half + h * half)
-                parts.append(lax.dynamic_slice(columns, start, (1, img_rows, half))[0])
-        feats.append(jnp.concatenate(parts, axis=1))
-
-    raw_rows, key_values = [], []
-    for rows in feats:
-        blocks = []
-        for d in range(RING):
-            group = (z - x - d) % RING * both
-            weights = jnp.concatenate(
-                [
-                    lax.dynamic_slice_in_dim(upper, group, both, 1),
-                    lax.dynamic_slice_in_dim(lower, group, both, 1),
-                ],
-                axis=0,
-            )
-            block = matmul(rows, weights, ((1,), (0,)))
-            blocks.append(block if d == 0 else block.astype(jnp.bfloat16))
-        projected = scattered(blocks, along_x)
-        raw = projected[:, :head_dim]
-        keys = (raw * rms_factor(raw) * key_gain).astype(jnp.bfloat16)
-        raw_rows.append(raw)
-        key_values.append(
-            jnp.concatenate([keys, projected[:, head_dim:].astype(jnp.bfloat16)], axis=1)
-        )
-
-    away = along_z(key_values[0], RING // 2)
-    away = jnp.where(swaps, away, key_values[0])
+    feats = arrange(jnp.stack([y, core, far_slot]).astype(jnp.int32), image, other_core(image), half)
+
+    made = project(((z - x) % RING).astype(jnp.int32)[None], feats, uppers, lowers)
+    (blocks,) = scattered([made], [along_x])
+    raw, far_key_value, near_key_value = finish(blocks, key_gain)
+
+    flag = swaps.astype(jnp.int32)
+    away = along_z(far_key_value, RING // 2)
     near_own = 1 - far_own
-    earlier = ()
-    grads = [None, None]
-    order = ((0, far_own, away), (1, near_own, key_values[1]))
-    for slot, own, key_value in order:
-        result = attend(
-            own, home_tiles[own], ratio, query, cotangent, key_value, query_gain, earlier
-        )
-        earlier = result[:2]
-        grads[slot] = result[2]
-    context, d_query = earlier
-    back = along_z(grads[0], RING // 2)
-    grads[0] = jnp.where(swaps, back, grads[0])
-
-    d_rows = [[], []]
-    for slot in (1, 0):
-        raw = raw_rows[slot]
-        grad = grads[slot].astype(jnp.float32)
-        d_raw = norm_back(raw, rms_factor(raw), key_gain, grad[:, :head_dim])
-        own = jnp.concatenate([d_raw.astype(jnp.bfloat16), grads[slot][:, head_dim:]], axis=1)
-        d_rows[slot] = gathered(own, along_x)
-    by_source = jnp.stack([jnp.concatenate([d_rows[0][o], d_rows[1][o]], axis=0) for o in range(RING)])
-    groups = [
-        lax.dynamic_index_in_dim(by_source, (x - z - d) % RING, 0, keepdims=False)
-        for d in range(RING)
-    ]
-    all_groups = jnp.concatenate(groups, axis=1)
-    all_feats = jnp.concatenate(feats, axis=0)
-
-    def sent(block, d):
-        return block if d == 0 else block.astype(jnp.bfloat16)
-
-    upper_blocks, lower_blocks = [], []
+    shared = (ratio, query, cotangent)
+    *earlier, near_grad = attend(
+        near_own, home_tiles[near_own], 0, *shared, near_key_value, near_key_value, query_gain, ()
+    )
+    near_rows = turn(jnp.zeros_like(flag)[None], 1, raw, near_grad, near_grad, key_gain)
+    context, d_query, far_grad = attend(
+        far_own, home_tiles[far_own], flag, *shared, far_key_value, away, query_gain, earlier
+    )
+    back = along_z(far_grad, RING // 2)
+    far_rows = turn(flag[None], 0, raw, far_grad, back, key_gain)
+
+    near_all = gathered(near_rows, along_x)
+    far_all = gathered(far_rows, along_x)
+    grads = collect(((x - z) % RING).astype(jnp.int32)[None], far_all, near_all)
+
     wide = RING * half
-    for d in range(RING):
+    upper_parts, lower_parts = [None] * RING, [None] * RING
+    for d in (2, 1, 3, 0):
         o = -d % RING
-        rows = all_feats[:, o * half : (o + 1) * half]
-        upper_blocks.append(sent(matmul(rows, all_groups, ((0,), (0,))), d))
-        lower_blocks.append(sent(matmul(all_feats[:, wide:], groups[d], ((0,), (0,))), d))
-    upper_sum = scattered(upper_blocks, along_y)
-    lower_sum = scattered(lower_blocks, along_z)
-    upper_parts = [sent(upper_sum[:, d * both : (d + 1) * both], d) for d in range(RING)]
-    lower_parts = [
-        sent(lower_sum[-d % RING * half : (-d % RING + 1) * half], d) for d in range(RING)
-    ]
-    upper_sum = scattered(upper_parts, along_z)
-    lower_sum = scattered(lower_parts, along_y)
-    share = jnp.concatenate([upper_sum, lower_sum], axis=0).astype(jnp.bfloat16)
+        rows = feats[:, o * half : (o + 1) * half]
+        upper_parts[d] = matmul(rows, grads, ((0,), (0,)))
+        columns = grads[:, d * both : (d + 1) * both]
+        lower_parts[d] = matmul(feats[:, wide:], columns, ((0,), (0,)))
+    upper_sum, lower_sum = scattered([upper_parts, lower_parts], [along_y, along_z])
+    upper_sum, lower_sum = summed(upper_sum), summed(lower_sum)
+    upper_parts = [upper_sum[:, d * both : (d + 1) * both] for d in range(RING)]
+    lower_parts = [lower_sum[-d % RING * half : (-d % RING + 1) * half] for d in range(RING)]
+    upper_sum, lower_sum = scattered([upper_parts, lower_parts], [along_z, along_y])
+    share = jnp.concatenate([summed(upper_sum), summed(lower_sum)], axis=0).astype(jnp.bfloat16)
     share = exchange_xz(share).astype(jnp.float32)
     return (context, d_query, share[:, :head_dim], share[:, head_dim:])
 

time: 252 us -> 414 us (1.64)
  Pallas kernels: 10.6 us -> 223 us
  waiting for transfers between devices: 110 us -> 89 us
  other arithmetic: 19.1 us -> 4.16 us
  starting transfers between devices: 80.5 us -> 74.5 us
    pallas_call x0 -> x6, Pallas kernels: none -> 210 us  [the longest x1 129 us: arrange(): pl.pallas_call(functools.partial(arrange_kernel, half), in_specs=[SMEM, H...]
    ppermute x12 -> x9, starting transfers between devices: 34.6 us -> 11.8 us  [along_x(): return lax.ppermute(x, 'tensor', pairs)]
    ppermute x12, waiting for transfers between devices: 29.3 us -> 10.8 us  [along_y(): return lax.ppermute(x, 'dp', pairs)]
    concatenate x11 -> x2, other arithmetic: 9.67 us -> 0.05 us  [the longest x1 0.03 us: per_device(): halves.append(jnp.concatenate([key_rows, value_rows], axis=1))]
    ppermute x12 -> x9, waiting for transfers between devices: 20.5 us -> 27 us  [along_x(): return lax.ppermute(x, 'tensor', pairs)]
    ppermute x2 -> x3, starting transfers between devices: 11.4 us -> 17.9 us  [exchange_xz(): return lax.ppermute(x, ('dp', 'tensor'), pairs)]
    ppermute x14, starting transfers between devices: 20.2 us -> 26.1 us  [along_z(): return lax.ppermute(x, 'dp', pairs)]
    ppermute x14, waiting for transfers between devices: 41 us -> 35.7 us  [along_z(): return lax.ppermute(x, 'dp', pairs)]
  transfers between devices with their start and end apart: 41 -> 39, of which waited for: 22 -> 17; matrix products, arithmetic and copies ran while one was open for 11% -> 2% of each run, Pallas kernels for 2% -> 34%
where the time goes in v3:
time: 414 us; the launch traced here: 413 us
  Pallas kernels  223 us (54%)
  waiting for transfers between devices  89 us (21%)
  starting transfers between devices  74.5 us (18%)
  local copies, waits for them, and re-layouts  9.06 us (2%)
  matrix products  7.92 us (2%)
  between operations  5.05 us (1%)
  other arithmetic  4.16 us (1%)
    pallas_call x1, Pallas kernels, arrange(): pl.pallas_call(functools.partial(arrange_kernel, half), in_specs=[SMEM, H...  129 us
    pallas_call x1, Pallas kernels, collect(): pl.pallas_call(collect_kernel, in_specs=[SMEM] + [HBM] * (2 * RING), out_...  64.7 us
    ppermute x14, waiting for transfers between devices, along_z(): return lax.ppermute(x, 'dp', pairs)  35.7 us
    ppermute x9, waiting for transfers between devices, along_x(): return lax.ppermute(x, 'tensor', pairs)  27 us
    ppermute x14, starting transfers between devices, along_z(): return lax.ppermute(x, 'dp', pairs)  26.1 us
    ppermute x12, starting transfers between devices, along_y(): return lax.ppermute(x, 'dp', pairs)  18.7 us
    ppermute x3, starting transfers between devices, exchange_xz(): return lax.ppermute(x, ('dp', 'tensor'), pairs)  17.9 us
    ppermute x3, waiting for transfers between devices, exchange_xz(): return lax.ppermute(x, ('dp', 'tensor'), pairs)  15.5 us
  transfers between devices with their start and end apart: 39, of which 17 were waited for; matrix products, arithmetic and copies ran while one was open for 2% of the time, Pallas kernels for 34%

profile of v3, /device:TPU:4, one launch (start us, length us, event | category | flops | bytes accessed | tf_op | source)
XLA Modules:
  0.0 413.1 jit_solution(16409657356212020625)
XLA Ops:
  2.6 5.7 %collective-permute-start.1 = (bf16[256,256]{1,0:T(8,128)(2,1)S(1)}, bf16[256,256]{1,0:T(8,128)(2,1)S(1)}, u32[]{:S(2)}, u32[]{:S(2)}) collective-permute-start(bf16[256,256]{1,0:T(8,128)(2,1)S(1)} %get-tuple-element.21), channel_id=1, source_target_pairs={{0,0},{1,1},{2,32},{3,33},{4,64},{5,65},{6,96},{7,97},{8,8},{9,9},... | collective-permute-start | bytes 393224 | tf_op jit(solution)/shard_map/ppermute | solution.py:43
  8.3 8.1 %collective-permute-done.1 = bf16[256,256]{1,0:T(8,128)(2,1)S(1)} collective-permute-done((bf16[256,256]{1,0:T(8,128)(2,1)S(1)}, bf16[256,256]{1,0:T(8,128)(2,1)S(1)}, u32[]{:S(2)}, u32[]{:S(2)}) %collective-permute-start.1) | collective-permute-done | bytes 131104 | tf_op jit(solution)/shard_map/ppermute | solution.py:43
  16.4 7.4 %collective-permute-start.8 = (bf16[256,256]{1,0:T(8,128)(2,1)S(1)}, bf16[256,256]{1,0:T(8,128)(2,1)S(1)}, u32[]{:S(2)}, u32[]{:S(2)}) collective-permute-start(bf16[256,256]{1,0:T(8,128)(2,1)S(1)} %get-tuple-element.22), channel_id=1, source_target_pairs={{0,0},{1,1},{2,32},{3,33},{4,64},{5,65},{6,96},{7,97},{8,8},{9,9},... | collective-permute-start | bytes 393224 | tf_op jit(solution)/shard_map/ppermute | solution.py:43
  24.5 7.2 %collective-permute-done.3 = bf16[256,256]{1,0:T(8,128)(2,1)S(1)} collective-permute-done((bf16[256,256]{1,0:T(8,128)(2,1)S(1)}, bf16[256,256]{1,0:T(8,128)(2,1)S(1)}, u32[]{:S(2)}, u32[]{:S(2)}) %collective-permute-start.3) | collective-permute-done | bytes 131104 | tf_op jit(solution)/shard_map/ppermute | solution.py:17
  39.0 10.7 %collective-permute-done.9 = bf16[256,256]{1,0:T(8,128)(2,1)S(1)} collective-permute-done((bf16[256,256]{1,0:T(8,128)(2,1)S(1)}, bf16[256,256]{1,0:T(8,128)(2,1)S(1)}, u32[]{:S(2)}, u32[]{:S(2)}) %collective-permute-start.9) | collective-permute-done | bytes 131104 | tf_op jit(solution)/shard_map/ppermute | solution.py:22
  49.7 4.7 %collective-permute-start.6 = (bf16[256,1024]{1,0:T(8,128)(2,1)S(1)}, bf16[256,1024]{1,0:T(8,128)(2,1)}, u32[]{:S(2)}, u32[]{:S(2)}) collective-permute-start(bf16[256,1024]{1,0:T(8,128)(2,1)S(1)} %constant_dynamic-update-slice_fusion.refs_0_), channel_id=1, source_target_pairs={{0,16},{8,24},{16,0},{24,8},{32,48},{40,56},{48,32},{56,40},{64,80... | collective-permute-start | bytes 1572872 | tf_op jit(solution)/shard_map/ppermute | solution.py:22
  54.6 4.3 %collective-permute-start.12 = (bf16[1024,256]{1,0:T(8,128)(2,1)S(1)}, bf16[1024,256]{1,0:T(8,128)(2,1)}, u32[]{:S(2)}, u32[]{:S(2)}) collective-permute-start(bf16[1024,256]{1,0:T(8,128)(2,1)S(1)} %constant_dynamic-update-slice_fusion.4.refs_4_), channel_id=1, source_target_pairs={{0,32},{8,40},{16,48},{24,56},{32,64},{40,72},{48,80},{56,88},{64,... | collective-permute-start | bytes 1572872 | tf_op jit(solution)/shard_map/ppermute | solution.py:17
  65.2 129.0 %shard_map.129.rows_ref = bf16[1024,2048]{1,0:T(8,128)(2,1)} custom-call(s32[3]{0:T(128)} %pad_add_fusion.1.index, bf16[2,512,1024]{2,1,0:T(8,128)(2,1)} %own_ref, bf16[2,512,1024]{2,1,0:T(8,128)(2,1)} %copy-done.2), custom_call_target="tpu_custom_call" | custom-call | bytes 8388608 | tf_op jit(solution)/shard_map/pallas_call | solution.py:111
  194.2 8.7 %shard_map.130 = (bf16[1024,256]{1,0:T(8,128)(2,1)}, bf16[1024,256]{1,0:T(8,128)(2,1)}, bf16[1024,256]{1,0:T(8,128)(2,1)}, bf16[1024,256]{1,0:T(8,128)(2,1)}) custom-call(s32[1]{0:T(128)} %bitcast.5.index, bf16[1024,2048]{1,0:T(8,128)(2,1)} %shard_map.129.rows_ref, bf16[256,1024]{1,0:T(8,128)(2,1)} %copy-done.14, ...), custom_call_target="tpu_custom_call" | custom-call | flops 4294967296 | bytes 10485760 | tf_op jit(solution)/shard_map/pallas_call | solution.py:167
  210.3 7.3 %collective-permute-done.15.far_ref = bf16[1024,256]{1,0:T(8,128)(2,1)S(1)} collective-permute-done((bf16[1024,256]{1,0:T(8,128)(2,1)}, bf16[1024,256]{1,0:T(8,128)(2,1)S(1)}, u32[]{:S(2)}, u32[]{:S(2)}) %collective-permute-start.15) | collective-permute-done | bytes 524320 | tf_op jit(solution)/shard_map/ppermute | solution.py:27
  217.6 5.5 %collective-permute-done.16.left_ref = bf16[1024,256]{1,0:T(8,128)(2,1)S(1)} collective-permute-done((bf16[1024,256]{1,0:T(8,128)(2,1)}, bf16[1024,256]{1,0:T(8,128)(2,1)S(1)}, u32[]{:S(2)}, u32[]{:S(2)}) %collective-permute-start.16) | collective-permute-done | bytes 524320 | tf_op jit(solution)/shard_map/ppermute | solution.py:27
  224.7 4.0 shard_map.131
  232.8 6.5 %shard_map.132 = (bf16[2,128,1024]{2,1,0:T(8,128)(2,1)}, bf16[2,128,1024]{2,1,0:T(8,128)(2,1)}, bf16[512,256]{1,0:T(8,128)(2,1)}) custom-call(s32[3]{0:T(128)} %pad_add_fusion.2.index, f32[1]{0:T(128)S(6)} %tanh.3.ratio_ref, bf16[2,128,1024]{2,1,0:T(8,128)(2,1)} %q_ref.3, bf16[2,128,1024]{2,1,0:T(8,128)(2,1)} %cot_ref.3, ...), custom_call_target="tpu_custom_call" | custom-call | flops 939524096 | bytes 1441792 | tf_op jit(solution)/shard_map/pallas_call | solution.py:372
  240.1 6.5 %shard_map.133 = (bf16[2,128,1024]{2,1,0:T(8,128)(2,1)}, bf16[2,128,1024]{2,1,0:T(8,128)(2,1)}, bf16[512,256]{1,0:T(8,128)(2,1)}) custom-call(s32[3]{0:T(128)} %pad_add_fusion.index, f32[1]{0:T(128)S(6)} %tanh.3.ratio_ref, bf16[2,128,1024]{2,1,0:T(8,128)(2,1)} %q_ref.3, bf16[2,128,1024]{2,1,0:T(8,128)(2,1)} %cot_ref.3, ...), custom_call_target="tpu_custom_call", output_to_operand_aliasing={{0}: (7, {}), {1}: (8, {})} | custom-call | flops 939524096 | bytes 1441792 | tf_op jit(solution)/shard_map/pallas_call | solution.py:372
  267.8 3.7 collective-permute-done.20.refs_1_
  271.5 4.8 %collective-permute-done.21.refs_2_ = bf16[512,256]{1,0:T(8,128)(2,1)S(1)} collective-permute-done((bf16[512,256]{1,0:T(8,128)(2,1)}, bf16[512,256]{1,0:T(8,128)(2,1)S(1)}, u32[]{:S(2)}, u32[]{:S(2)}) %collective-permute-start.21) | collective-permute-done | bytes 262176 | tf_op jit(solution)/shard_map/ppermute | solution.py:27
  277.6 64.7 %shard_map.136 = bf16[1024,1024]{1,0:T(8,128)(2,1)} custom-call(s32[1]{0:T(128)} %bitcast.11.index, bf16[512,256]{1,0:T(8,128)(2,1)} %shard_map.134.refs_0_, bf16[512,256]{1,0:T(8,128)(2,1)} %copy-done.9, bf16[512,256]{1,0:T(8,128)(2,1)} %copy-done.10, bf16[512,256]{1,0:T(8,128)(2,1)} %copy-done.11, bf16[512,256]{1,0:T(8,128)(2,1)} %shard_map.135.refs_4_, ...), custom_call_target="tpu_custom_call" | custom-call | bytes 4194304 | tf_op jit(solution)/shard_map/pallas_call | solution.py:284
  355.4 7.7 %collective-permute-done.34 = bf16[1024,256]{1,0:T(8,128)(2,1)S(1)} collective-permute-done((bf16[1024,256]{1,0:T(8,128)(2,1)S(1)}, bf16[1024,256]{1,0:T(8,128)(2,1)S(1)}, u32[]{:S(2)}, u32[]{:S(2)}) %collective-permute-start.34) | collective-permute-done | bytes 524320 | tf_op jit(solution)/shard_map/ppermute | solution.py:17
  363.8 10.4 %collective-permute-done.33 = bf16[1024,256]{1,0:T(8,128)(2,1)S(1)} collective-permute-done((bf16[1024,256]{1,0:T(8,128)(2,1)S(1)}, bf16[1024,256]{1,0:T(8,128)(2,1)S(1)}, u32[]{:S(2)}, u32[]{:S(2)}) %collective-permute-start.33) | collective-permute-done | bytes 524320 | tf_op jit(solution)/shard_map/ppermute | solution.py:17
  379.8 3.4 collective-permute-start.31
  386.3 3.8 collective-permute-start.29
  391.5 8.5 %collective-permute-done.29 = bf16[256,256]{1,0:T(8,128)(2,1)S(1)} collective-permute-done((bf16[256,256]{1,0:T(8,128)(2,1)S(1)}, bf16[256,256]{1,0:T(8,128)(2,1)S(1)}, u32[]{:S(2)}, u32[]{:S(2)}) %collective-permute-start.29) | collective-permute-done | bytes 131104 | tf_op jit(solution)/shard_map/ppermute | solution.py:17
  400.1 4.8 %collective-permute-start.38 = (bf16[512,256]{1,0:T(8,128)(2,1)S(1)}, bf16[512,256]{1,0:T(8,128)(2,1)S(1)}, u32[]{:S(2)}, u32[]{:S(2)}) collective-permute-start(bf16[512,256]{1,0:T(8,128)(2,1)S(1)} %pad_maximum_fusion), channel_id=1, source_target_pairs={{0,0},{1,1},{2,32},{3,33},{4,64},{5,65},{6,96},{7,97},{8,8},{9,9},... | collective-permute-start | bytes 786440 | tf_op jit(solution)/shard_map/ppermute | solution.py:43
  404.9 7.4 %collective-permute-done.38 = bf16[512,256]{1,0:T(8,128)(2,1)S(1)} collective-permute-done((bf16[512,256]{1,0:T(8,128)(2,1)S(1)}, bf16[512,256]{1,0:T(8,128)(2,1)S(1)}, u32[]{:S(2)}, u32[]{:S(2)}) %collective-permute-start.38) | collective-permute-done | bytes 262176 | tf_op jit(solution)/shard_map/ppermute | solution.py:43
  (133 shorter events, 73.3 us)
Async XLA Ops:
  2.5 57.5 %collective-permute-start = (bf16[2,512,1024]{2,1,0:T(8,128)(2,1)}, bf16[2,512,1024]{2,1,0:T(8,128)(2,1)S(1)}, u32[]{:S(2)}, u32[]{:S(2)}) collective-permute-start(bf16[2,512,1024]{2,1,0:T(8,128)(2,1)} %own_ref), channel_id=1, source_target_pairs={{0,1},{1,0},{2,3},{3,2},{4,5},{5,4},{6,7},{7,6},{8,9},{9,8},{10,11... | collective-permute-start | bytes 6291464 | tf_op jit(solution)/shard_map/ppermute | solution.py:31
  16.4 17.0 %collective-permute-start.8 = (bf16[256,256]{1,0:T(8,128)(2,1)S(1)}, bf16[256,256]{1,0:T(8,128)(2,1)S(1)}, u32[]{:S(2)}, u32[]{:S(2)}) collective-permute-start(bf16[256,256]{1,0:T(8,128)(2,1)S(1)} %get-tuple-element.22), channel_id=1, source_target_pairs={{0,0},{1,1},{2,32},{3,33},{4,64},{5,65},{6,96},{7,97},{8,8},{9,9},... | collective-permute-start | bytes 393224 | tf_op jit(solution)/shard_map/ppermute | solution.py:43
  31.7 27.2 %collective-permute-start.5 = (bf16[256,1024]{1,0:T(8,128)(2,1)S(1)}, bf16[256,1024]{1,0:T(8,128)(2,1)}, u32[]{:S(2)}, u32[]{:S(2)}) collective-permute-start(bf16[256,1024]{1,0:T(8,128)(2,1)S(1)} %constant_dynamic-update-slice_fusion.refs_0_), channel_id=1, source_target_pairs={{0,8},{8,16},{16,24},{24,0},{32,40},{40,48},{48,56},{56,32},{64,72... | collective-permute-start | bytes 1572872 | tf_op jit(solution)/shard_map/ppermute | solution.py:22
  33.4 16.3 %collective-permute-start.9 = (bf16[256,256]{1,0:T(8,128)(2,1)S(1)}, bf16[256,256]{1,0:T(8,128)(2,1)S(1)}, u32[]{:S(2)}, u32[]{:S(2)}) collective-permute-start(bf16[256,256]{1,0:T(8,128)(2,1)S(1)} %collective-permute-done.8), channel_id=1, source_target_pairs={{0,8},{8,16},{16,24},{24,0},{32,40},{40,48},{48,56},{56,32},{64,72... | collective-permute-start | bytes 393224 | tf_op jit(solution)/shard_map/ppermute | solution.py:22
  35.0 19.5 %collective-permute-start.10 = (bf16[256,256]{1,0:T(8,128)(2,1)S(1)}, bf16[256,256]{1,0:T(8,128)(2,1)S(1)}, u32[]{:S(2)}, u32[]{:S(2)}) collective-permute-start(bf16[256,256]{1,0:T(8,128)(2,1)S(1)} %collective-permute-done.8), channel_id=1, source_target_pairs={{0,16},{8,24},{16,0},{24,8},{32,48},{40,56},{48,32},{56,40},{64,80... | collective-permute-start | bytes 393224 | tf_op jit(solution)/shard_map/ppermute | solution.py:22
  36.5 18.1 %collective-permute-start.11 = (bf16[256,256]{1,0:T(8,128)(2,1)S(1)}, bf16[256,256]{1,0:T(8,128)(2,1)S(1)}, u32[]{:S(2)}, u32[]{:S(2)}) collective-permute-start(bf16[256,256]{1,0:T(8,128)(2,1)S(1)} %collective-permute-done.8), channel_id=1, source_target_pairs={{0,24},{8,0},{16,8},{24,16},{32,56},{40,32},{48,40},{56,48},{64,88... | collective-permute-start | bytes 393224 | tf_op jit(solution)/shard_map/ppermute | solution.py:22
  49.7 144.4 %collective-permute-start.6 = (bf16[256,1024]{1,0:T(8,128)(2,1)S(1)}, bf16[256,1024]{1,0:T(8,128)(2,1)}, u32[]{:S(2)}, u32[]{:S(2)}) collective-permute-start(bf16[256,1024]{1,0:T(8,128)(2,1)S(1)} %constant_dynamic-update-slice_fusion.refs_0_), channel_id=1, source_target_pairs={{0,16},{8,24},{16,0},{24,8},{32,48},{40,56},{48,32},{56,40},{64,80... | collective-permute-start | bytes 1572872 | tf_op jit(solution)/shard_map/ppermute | solution.py:22
  54.5 139.7 %collective-permute-start.7 = (bf16[256,1024]{1,0:T(8,128)(2,1)S(1)}, bf16[256,1024]{1,0:T(8,128)(2,1)}, u32[]{:S(2)}, u32[]{:S(2)}) collective-permute-start(bf16[256,1024]{1,0:T(8,128)(2,1)S(1)} %constant_dynamic-update-slice_fusion.refs_0_), channel_id=1, source_target_pairs={{0,24},{8,0},{16,8},{24,16},{32,56},{40,32},{48,40},{56,48},{64,88... | collective-permute-start | bytes 1572872 | tf_op jit(solution)/shard_map/ppermute | solution.py:22
  54.6 139.6 %collective-permute-start.12 = (bf16[1024,256]{1,0:T(8,128)(2,1)S(1)}, bf16[1024,256]{1,0:T(8,128)(2,1)}, u32[]{:S(2)}, u32[]{:S(2)}) collective-permute-start(bf16[1024,256]{1,0:T(8,128)(2,1)S(1)} %constant_dynamic-update-slice_fusion.4.refs_4_), channel_id=1, source_target_pairs={{0,32},{8,40},{16,48},{24,56},{32,64},{40,72},{48,80},{56,88},{64,... | collective-permute-start | bytes 1572872 | tf_op jit(solution)/shard_map/ppermute | solution.py:17
  58.9 135.3 %collective-permute-start.13 = (bf16[1024,256]{1,0:T(8,128)(2,1)S(1)}, bf16[1024,256]{1,0:T(8,128)(2,1)}, u32[]{:S(2)}, u32[]{:S(2)}) collective-permute-start(bf16[1024,256]{1,0:T(8,128)(2,1)S(1)} %constant_dynamic-update-slice_fusion.4.refs_4_), channel_id=1, source_target_pairs={{0,64},{8,72},{16,80},{24,88},{32,96},{40,104},{48,112},{56,120},{... | collective-permute-start | bytes 1572872 | tf_op jit(solution)/shard_map/ppermute | solution.py:17
  60.0 134.2 %collective-permute-start.14 = (bf16[1024,256]{1,0:T(8,128)(2,1)S(1)}, bf16[1024,256]{1,0:T(8,128)(2,1)}, u32[]{:S(2)}, u32[]{:S(2)}) collective-permute-start(bf16[1024,256]{1,0:T(8,128)(2,1)S(1)} %constant_dynamic-update-slice_fusion.4.refs_4_), channel_id=1, source_target_pairs={{0,96},{8,104},{16,112},{24,120},{32,0},{40,8},{48,16},{56,24},{64... | collective-permute-start | bytes 1572872 | tf_op jit(solution)/shard_map/ppermute | solution.py:17
  203.0 14.7 %collective-permute-start.15 = (bf16[1024,256]{1,0:T(8,128)(2,1)}, bf16[1024,256]{1,0:T(8,128)(2,1)S(1)}, u32[]{:S(2)}, u32[]{:S(2)}) collective-permute-start(bf16[1024,256]{1,0:T(8,128)(2,1)} %get-tuple-element.24), channel_id=1, source_target_pairs={{0,4},{1,5},{2,6},{3,7},{4,0},{5,1},{6,2},{7,3},{8,12},{9,13},{10,... | collective-permute-start | bytes 1572872 | tf_op jit(solution)/shard_map/ppermute | solution.py:27
  203.1 20.1 %collective-permute-start.16 = (bf16[1024,256]{1,0:T(8,128)(2,1)}, bf16[1024,256]{1,0:T(8,128)(2,1)S(1)}, u32[]{:S(2)}, u32[]{:S(2)}) collective-permute-start(bf16[1024,256]{1,0:T(8,128)(2,1)} %get-tuple-element.25), channel_id=1, source_target_pairs={{0,2},{1,3},{2,4},{3,5},{4,6},{5,7},{6,0},{7,1},{8,10},{9,11},{10,... | collective-permute-start | bytes 1572872 | tf_op jit(solution)/shard_map/ppermute | solution.py:27
  203.5 20.4 %collective-permute-start.17 = (bf16[1024,256]{1,0:T(8,128)(2,1)}, bf16[1024,256]{1,0:T(8,128)(2,1)S(1)}, u32[]{:S(2)}, u32[]{:S(2)}) collective-permute-start(bf16[1024,256]{1,0:T(8,128)(2,1)} %get-tuple-element.26), channel_id=1, source_target_pairs={{0,6},{1,7},{2,0},{3,1},{4,2},{5,3},{6,4},{7,5},{8,14},{9,15},{10,... | collective-permute-start | bytes 1572872 | tf_op jit(solution)/shard_map/ppermute | solution.py:27
  253.5 14.3 %collective-permute-start.25 = (bf16[512,256]{1,0:T(8,128)(2,1)}, bf16[512,256]{1,0:T(8,128)(2,1)S(1)}, u32[]{:S(2)}, u32[]{:S(2)}) collective-permute-start(bf16[512,256]{1,0:T(8,128)(2,1)} %shard_map.135.refs_4_), channel_id=1, source_target_pairs={{0,6},{1,7},{2,0},{3,1},{4,2},{5,3},{6,4},{7,5},{8,14},{9,15},{10,... | collective-permute-start | bytes 786440 | tf_op jit(solution)/shard_map/ppermute | solution.py:27
  259.8 16.5 %collective-permute-start.21 = (bf16[512,256]{1,0:T(8,128)(2,1)}, bf16[512,256]{1,0:T(8,128)(2,1)S(1)}, u32[]{:S(2)}, u32[]{:S(2)}) collective-permute-start(bf16[512,256]{1,0:T(8,128)(2,1)} %shard_map.134.refs_0_), channel_id=1, source_target_pairs={{0,4},{1,5},{2,6},{3,7},{4,0},{5,1},{6,2},{7,3},{8,12},{9,13},{10,... | collective-permute-start | bytes 786440 | tf_op jit(solution)/shard_map/ppermute | solution.py:27
  261.9 15.0 %collective-permute-start.22 = (bf16[512,256]{1,0:T(8,128)(2,1)}, bf16[512,256]{1,0:T(8,128)(2,1)S(1)}, u32[]{:S(2)}, u32[]{:S(2)}) collective-permute-start(bf16[512,256]{1,0:T(8,128)(2,1)} %shard_map.134.refs_0_), channel_id=1, source_target_pairs={{0,6},{1,7},{2,0},{3,1},{4,2},{5,3},{6,4},{7,5},{8,14},{9,15},{10,... | collective-permute-start | bytes 786440 | tf_op jit(solution)/shard_map/ppermute | solution.py:27
  348.2 14.9 %collective-permute-start.34 = (bf16[1024,256]{1,0:T(8,128)(2,1)S(1)}, bf16[1024,256]{1,0:T(8,128)(2,1)S(1)}, u32[]{:S(2)}, u32[]{:S(2)}) collective-permute-start(bf16[1024,256]{1,0:T(8,128)(2,1)S(1)} %fusion.17), channel_id=1, source_target_pairs={{0,96},{8,104},{16,112},{24,120},{32,0},{40,8},{48,16},{56,24},{64... | collective-permute-start | bytes 1572872 | tf_op jit(solution)/shard_map/ppermute | solution.py:17
  349.2 24.9 %collective-permute-start.33 = (bf16[1024,256]{1,0:T(8,128)(2,1)S(1)}, bf16[1024,256]{1,0:T(8,128)(2,1)S(1)}, u32[]{:S(2)}, u32[]{:S(2)}) collective-permute-start(bf16[1024,256]{1,0:T(8,128)(2,1)S(1)} %fusion.14), channel_id=1, source_target_pairs={{0,32},{8,40},{16,48},{24,56},{32,64},{40,72},{48,80},{56,88},{64,... | collective-permute-start | bytes 1572872 | tf_op jit(solution)/shard_map/ppermute | solution.py:17
  350.3 23.9 %collective-permute-start.32 = (bf16[1024,256]{1,0:T(8,128)(2,1)S(1)}, bf16[1024,256]{1,0:T(8,128)(2,1)S(1)}, u32[]{:S(2)}, u32[]{:S(2)}) collective-permute-start(bf16[1024,256]{1,0:T(8,128)(2,1)S(1)} %fusion.11), channel_id=1, source_target_pairs={{0,64},{8,72},{16,80},{24,88},{32,96},{40,104},{48,112},{56,120},{... | collective-permute-start | bytes 1572872 | tf_op jit(solution)/shard_map/ppermute | solution.py:17
  351.8 25.2 %collective-permute-start.28 = (bf16[256,1024]{1,0:T(8,128)(2,1)S(1)}, bf16[256,1024]{1,0:T(8,128)(2,1)S(1)}, u32[]{:S(2)}, u32[]{:S(2)}) collective-permute-start(bf16[256,1024]{1,0:T(8,128)(2,1)S(1)} %convolution_convert_fusion), channel_id=1, source_target_pairs={{0,24},{8,0},{16,8},{24,16},{32,56},{40,32},{48,40},{56,48},{64,88... | collective-permute-start | bytes 1572872 | tf_op jit(solution)/shard_map/ppermute | solution.py:22
  353.5 25.3 %collective-permute-start.27 = (bf16[256,1024]{1,0:T(8,128)(2,1)S(1)}, bf16[256,1024]{1,0:T(8,128)(2,1)S(1)}, u32[]{:S(2)}, u32[]{:S(2)}) collective-permute-start(bf16[256,1024]{1,0:T(8,128)(2,1)S(1)} %convolution_convert_fusion.1), channel_id=1, source_target_pairs={{0,8},{8,16},{16,24},{24,0},{32,40},{40,48},{48,56},{56,32},{64,72... | collective-permute-start | bytes 1572872 | tf_op jit(solution)/shard_map/ppermute | solution.py:22
  363.1 15.7 %collective-permute-start.26 = (bf16[256,1024]{1,0:T(8,128)(2,1)S(1)}, bf16[256,1024]{1,0:T(8,128)(2,1)S(1)}, u32[]{:S(2)}, u32[]{:S(2)}) collective-permute-start(bf16[256,1024]{1,0:T(8,128)(2,1)S(1)} %convolution_convert_fusion.2), channel_id=1, source_target_pairs={{0,16},{8,24},{16,0},{24,8},{32,48},{40,56},{48,32},{56,40},{64,80... | collective-permute-start | bytes 1572872 | tf_op jit(solution)/shard_map/ppermute | solution.py:22
  375.9 14.1 %collective-permute-start.36 = (bf16[256,256]{1,0:T(8,128)(2,1)S(1)}, bf16[256,256]{1,0:T(8,128)(2,1)S(1)}, u32[]{:S(2)}, u32[]{:S(2)}) collective-permute-start(bf16[256,256]{1,0:T(8,128)(2,1)S(1)} %get-tuple-element.45), channel_id=1, source_target_pairs={{0,8},{8,16},{16,24},{24,0},{32,40},{40,48},{48,56},{56,32},{64,72... | collective-permute-start | bytes 393224 | tf_op jit(solution)/shard_map/ppermute | solution.py:22
  (33 other events, 605.4 us)

commit v4 on v3

--- a/solution.py
+++ b/solution.py
@@ -43,17 +43,20 @@
     return lax.ppermute(x, ("dp", "tensor"), pairs)
 
 
-def gathered(x, move):
-    far, after, before = (move(x, step) for step in (2, 1, 3))
-    return [x, after, far, before]
-
-
-def scattered(parts, moves):
-    totals = [[part[0]] for part in parts]
+def gathered(blocks, moves):
+    found = [[x, None, None, None] for x in blocks]
     for step in (2, 1, 3):
         for i, move in enumerate(moves):
-            totals[i].append(move(parts[i][step].astype(jnp.bfloat16), step))
-    return totals
+            found[i][step] = move(blocks[i], step)
+    return found
+
+
+def scattered(parts, moves):
+    arrived = [[] for _ in parts]
+    for step in (2, 1, 3):
+        for i, move in enumerate(moves):
+            arrived[i].append(move(parts[i][step].astype(jnp.bfloat16), step))
+    return arrived
 
 
 def summed(blocks):
@@ -86,7 +89,7 @@
 PARAMS = pltpu.CompilerParams(vmem_limit_bytes=60 * 1024 * 1024)
 
 
-def arrange_kernel(half, index, own_ref, other_ref, out_ref, sems):
+def arrange_kernel(half, index, own_ref, other_ref, out_ref, held, sems):
     slots, rows, depth = own_ref.shape
     waits = []
     for s in range(slots):
@@ -94,7 +97,7 @@
             for o in range(RING):
                 block = ((index[0] - o + RING) % RING) ^ (2 * index[1])
                 start = pl.multiple_of(block % 2 * 2 * half + h * half, half)
-                target = out_ref.at[pl.ds(s * rows, rows), pl.ds((h * RING + o) * half, half)]
+                target = held.at[pl.ds(s * rows, rows), pl.ds((h * RING + o) * half, half)]
                 sem = sems.at[len(waits)]
                 columns = pl.ds(start, half)
                 own = pltpu.make_async_copy(own_ref.at[s ^ index[2], :, columns], target, sem)
@@ -102,8 +105,16 @@
                 pl.when(block < 2)(own.start)
                 pl.when(block >= 2)(other.start)
                 waits.append(own)
-    for copy in waits:
-        copy.wait()
+    stores = []
+    for s in range(slots):
+        for copy in waits[s * 2 * RING : (s + 1) * 2 * RING]:
+            copy.wait()
+        part = pl.ds(s * rows, rows)
+        sem = sems.at[len(waits) + s]
+        stores.append(pltpu.make_async_copy(held.at[part], out_ref.at[part], sem))
+        stores[s].start()
+    for store in stores:
+        store.wait()
 
 
 def arrange(index, own, other, half):
@@ -113,7 +124,10 @@
         in_specs=[SMEM, HBM, HBM],
         out_specs=HBM,
         out_shape=jax.ShapeDtypeStruct((slots * rows, 2 * depth), own.dtype),
-        scratch_shapes=[pltpu.SemaphoreType.DMA((slots * 2 * RING,))],
+        scratch_shapes=[
+            pltpu.VMEM((slots * rows, 2 * depth), own.dtype),
+            pltpu.SemaphoreType.DMA((slots * (2 * RING + 1),)),
+        ],
         compiler_params=PARAMS,
         cost_estimate=pl.CostEstimate(flops=0, bytes_accessed=8 * own.size, transcendentals=0),
     )(index, own, other)
@@ -126,33 +140,37 @@
     both = lowers[0].shape[1]
     slots = row_sems.shape[0]
     count = rows.shape[0] // slots
-    row_copies, copies = [], []
+    row_copies = []
     for s in range(slots):
         part = pl.ds(s * count, count)
         row_copies.append(pltpu.make_async_copy(rows_ref.at[part], rows.at[part], row_sems.at[s]))
     row_copies[0].start()
-    for o in range(RING):
+    order = (2, 1, 3, 0)
+    copies = {}
+    for d in order:
+        o = (index[0] - d + RING) % RING
+        copies[d] = []
         for k in range(RING):
-            source = uppers[k].at[:, pl.ds(o * both, both)]
-            target = weights.at[o, pl.ds(k * half, half)]
-            copies.append(pltpu.make_async_copy(source, target, sems.at[o, k]))
-        target = weights.at[o, pl.ds(RING * half, RING * half)]
-        copies.append(pltpu.make_async_copy(lowers[o], target, sems.at[o, RING]))
-    for copy in copies:
-        copy.start()
+            source = uppers[k].at[:, pl.ds(pl.multiple_of(o * both, both), both)]
+            target = weights.at[d, pl.ds(k * half, half)]
+            copies[d].append(pltpu.make_async_copy(source, target, sems.at[d, k]))
+            copies[d][k].start()
+        target = weights.at[d, pl.ds(RING * half, RING * half)]
+        for k in range(RING):
+            copy = pltpu.make_async_copy(lowers[k], target, sems.at[d, RING])
+            pl.when(o == k)(copy.start)
+        copies[d].append(copy)
     for copy in row_copies[1:]:
         copy.start()
-    row_copies[0].wait()
-    for copy in copies:
-        copy.wait()
     stores = []
     for s in range(slots):
-        if s:
-            row_copies[s].wait()
-        for d in (2, 1, 3, 0):
-            o = (index[0] - d + RING) % RING
+        row_copies[s].wait()
+        for d in order:
+            if s == 0:
+                for copy in copies[d]:
+                    copy.wait()
             part = pl.ds(s * count, count)
-            stage[d, part] = matmul(rows[part], weights[o], ((1,), (0,))).astype(stage.dtype)
+            stage[d, part] = matmul(rows[part], weights[d], ((1,), (0,))).astype(stage.dtype)
             store = pltpu.make_async_copy(stage.at[d, part], outs[d].at[part], out_sems.at[d, s])
             store.start()
             stores.append(store)
@@ -265,18 +283,21 @@
 
 
 def collect_kernel(index, *refs):
-    sources, out_ref, sems = refs[:-2], refs[-2], refs[-1]
+    sources, (out_ref, held, sems) = refs[:-3], refs[-3:]
     rows, both = sources[0].shape
     copies = []
     for i, source in enumerate(sources):
         slot, o = i // RING, i % RING
         start = pl.multiple_of((index[0] - o + RING) % RING * both, both)
-        target = out_ref.at[pl.ds(slot * rows, rows), pl.ds(start, both)]
+        target = held.at[pl.ds(slot * rows, rows), pl.ds(start, both)]
         copies.append(pltpu.make_async_copy(source, target, sems.at[i]))
     for copy in copies:
         copy.start()
     for copy in copies:
         copy.wait()
+    store = pltpu.make_async_copy(held, out_ref, sems.at[len(sources)])
+    store.start()
+    store.wait()
 
 
 def collect(shift, first, second):
@@ -286,7 +307,10 @@
         in_specs=[SMEM] + [HBM] * (2 * RING),
         out_specs=HBM,
         out_shape=jax.ShapeDtypeStruct((2 * rows, RING * both), first[0].dtype),
-        scratch_shapes=[pltpu.SemaphoreType.DMA((2 * RING,))],
+        scratch_shapes=[
+            pltpu.VMEM((2 * rows, RING * both), first[0].dtype),
+            pltpu.SemaphoreType.DMA((2 * RING + 1,)),
+        ],
         compiler_params=PARAMS,
         cost_estimate=pl.CostEstimate(
             flops=0, bytes_accessed=8 * RING * rows * both, transcendentals=0
@@ -433,9 +457,12 @@
         halves.append(jnp.concatenate([key_rows, value_rows], axis=1))
     *halves, image = lax.optimization_barrier((*halves, image))
     upper, lower = (exchange_xz(rows) for rows in halves)
-    upper = jnp.concatenate(gathered(upper, along_z), axis=1)
-    lower = jnp.concatenate(gathered(lower, along_y), axis=0)
-    uppers, lowers = gathered(upper, along_y), gathered(lower, along_z)
+    upper, lower, other = lax.optimization_barrier((upper, lower, other_core(image)))
+    uppers, lowers = gathered([upper, lower], [along_z, along_y])
+    *uppers, y1, y2, y3, y4 = lax.optimization_barrier((*uppers, *lowers))
+    upper = jnp.concatenate(uppers, axis=1)
+    lower = jnp.concatenate([y1, y2, y3, y4], axis=0)
+    uppers, lowers = gathered([upper, lower], [along_y, along_z])
 
     first = rank * samp_local
     every = jnp.arange(tiles.shape[0], dtype=jnp.int32)
@@ -451,11 +478,11 @@
     far_own = jnp.where(swaps, jnp.where(own_away[1], 1, 0), own_of_slot)
     home_tiles = lax.dynamic_slice_in_dim(tiles, first, samp_local)
 
-    feats = arrange(jnp.stack([y, core, far_slot]).astype(jnp.int32), image, other_core(image), half)
+    feats = arrange(jnp.stack([y, core, far_slot]).astype(jnp.int32), image, other, half)
 
     made = project(((z - x) % RING).astype(jnp.int32)[None], feats, uppers, lowers)
-    (blocks,) = scattered([made], [along_x])
-    raw, far_key_value, near_key_value = finish(blocks, key_gain)
+    (arrived,) = scattered([made], [along_x])
+    raw, far_key_value, near_key_value = finish([made[0], *arrived], key_gain)
 
     flag = swaps.astype(jnp.int32)
     away = along_z(far_key_value, RING // 2)
@@ -471,24 +498,33 @@
     back = along_z(far_grad, RING // 2)
     far_rows = turn(flag[None], 0, raw, far_grad, back, key_gain)
 
-    near_all = gathered(near_rows, along_x)
-    far_all = gathered(far_rows, along_x)
+    (near_all,) = gathered([near_rows], [along_x])
+    (far_all,) = gathered([far_rows], [along_x])
     grads = collect(((x - z) % RING).astype(jnp.int32)[None], far_all, near_all)
 
     wide = RING * half
-    upper_parts, lower_parts = [None] * RING, [None] * RING
-    for d in (2, 1, 3, 0):
+
+    def products(feats, grads, d):
         o = -d % RING
         rows = feats[:, o * half : (o + 1) * half]
-        upper_parts[d] = matmul(rows, grads, ((0,), (0,)))
         columns = grads[:, d * both : (d + 1) * both]
-        lower_parts[d] = matmul(feats[:, wide:], columns, ((0,), (0,)))
-    upper_sum, lower_sum = scattered([upper_parts, lower_parts], [along_y, along_z])
-    upper_sum, lower_sum = summed(upper_sum), summed(lower_sum)
+        return (
+            matmul(rows, grads, ((0,), (0,))),
+            matmul(feats[:, wide:], columns, ((0,), (0,))),
+        )
+
+    sent = [None] + [products(feats, grads, d) for d in range(1, RING)]
+    sent = [None] + [[part.astype(jnp.bfloat16) for part in parts] for parts in sent[1:]]
+    upper, lower = scattered([[parts and parts[i] for parts in sent] for i in range(2)], [along_y, along_z])
+    feats, grads, upper[0], lower[0] = lax.optimization_barrier((feats, grads, upper[0], lower[0]))
+    own = products(feats, grads, 0)
+    upper_sum, lower_sum = summed([own[0], *upper]), summed([own[1], *lower])
     upper_parts = [upper_sum[:, d * both : (d + 1) * both] for d in range(RING)]
     lower_parts = [lower_sum[-d % RING * half : (-d % RING + 1) * half] for d in range(RING)]
-    upper_sum, lower_sum = scattered([upper_parts, lower_parts], [along_z, along_y])
-    share = jnp.concatenate([summed(upper_sum), summed(lower_sum)], axis=0).astype(jnp.bfloat16)
+    upper, lower = scattered([upper_parts, lower_parts], [along_z, along_y])
+    share = jnp.concatenate(
+        [summed([upper_parts[0], *upper]), summed([lower_parts[0], *lower])], axis=0
+    ).astype(jnp.bfloat16)
     share = exchange_xz(share).astype(jnp.float32)
     return (context, d_query, share[:, :head_dim], share[:, head_dim:])
 

time: 414 us -> 230 us (0.56)
  Pallas kernels: 223 us -> 39.7 us
  starting transfers between devices: 74.5 us -> 69.4 us
    pallas_call x1, Pallas kernels: 129 us -> 4.41 us  [arrange(): pl.pallas_call(functools.partial(arrange_kernel, half), in_specs=[SMEM, H...]
    pallas_call x1, Pallas kernels: 64.7 us -> 2.94 us  [collect(): pl.pallas_call(collect_kernel, in_specs=[SMEM] + [HBM] * (2 * RING), out_...]
    ppermute x14, waiting for transfers between devices: 35.7 us -> 21.5 us  [along_z(): return lax.ppermute(x, 'dp', pairs)]
    ppermute x14, starting transfers between devices: 26.1 us -> 15.8 us  [along_z(): return lax.ppermute(x, 'dp', pairs)]
    ppermute x12, waiting for transfers between devices: 10.8 us -> 18.7 us  [along_y(): return lax.ppermute(x, 'dp', pairs)]
    ppermute x12, starting transfers between devices: 18.7 us -> 25.1 us  [along_y(): return lax.ppermute(x, 'dp', pairs)]
  transfers between devices with their start and end apart: 39 -> 39, of which waited for: 17 -> 22; matrix products, arithmetic and copies ran while one was open for 2% -> 5% of each run, Pallas kernels for 34% -> 7%
where the time goes in v4:
time: 230 us; the launch traced here: 226 us
  waiting for transfers between devices  88.5 us (38%)
  starting transfers between devices  69.4 us (30%)
  Pallas kernels  39.7 us (17%)
  local copies, waits for them, and re-layouts  11.7 us (5%)
  matrix products  7.92 us (3%)
  between operations  5.01 us (2%)
  other arithmetic  4.11 us (2%)
    ppermute x9, waiting for transfers between devices, along_x(): return lax.ppermute(x, 'tensor', pairs)  29.6 us
    ppermute x12, starting transfers between devices, along_y(): return lax.ppermute(x, 'dp', pairs)  25.1 us
    ppermute x14, waiting for transfers between devices, along_z(): return lax.ppermute(x, 'dp', pairs)  21.5 us
    ppermute x3, waiting for transfers between devices, exchange_xz(): return lax.ppermute(x, ('dp', 'tensor'), pairs)  18.8 us
    ppermute x12, waiting for transfers between devices, along_y(): return lax.ppermute(x, 'dp', pairs)  18.7 us
    ppermute x14, starting transfers between devices, along_z(): return lax.ppermute(x, 'dp', pairs)  15.8 us
    ppermute x3, starting transfers between devices, exchange_xz(): return lax.ppermute(x, ('dp', 'tensor'), pairs)  14.6 us
    ppermute x9, starting transfers between devices, along_x(): return lax.ppermute(x, 'tensor', pairs)  13.8 us
  transfers between devices with their start and end apart: 39, of which 22 were waited for; matrix products, arithmetic and copies ran while one was open for 5% of the time, Pallas kernels for 7%

profile of v4, /device:TPU:4, one launch (start us, length us, event | category | flops | bytes accessed | tf_op | source)
XLA Modules:
  0.0 226.3 jit_solution(125360124650584067)
XLA Ops:
  2.6 5.7 %collective-permute-start = (bf16[256,256]{1,0:T(8,128)(2,1)S(1)}, bf16[256,256]{1,0:T(8,128)(2,1)S(1)}, u32[]{:S(2)}, u32[]{:S(2)}) collective-permute-start(bf16[256,256]{1,0:T(8,128)(2,1)S(1)} %get-tuple-element.36), channel_id=1, source_target_pairs={{0,0},{1,1},{2,32},{3,33},{4,64},{5,65},{6,96},{7,97},{8,8},{9,9},... | collective-permute-start | bytes 393224 | tf_op jit(solution)/shard_map/ppermute | solution.py:43
  8.3 4.0 %collective-permute-start.1 = (bf16[256,256]{1,0:T(8,128)(2,1)S(1)}, bf16[256,256]{1,0:T(8,128)(2,1)S(1)}, u32[]{:S(2)}, u32[]{:S(2)}) collective-permute-start(bf16[256,256]{1,0:T(8,128)(2,1)S(1)} %get-tuple-element.37), channel_id=1, source_target_pairs={{0,0},{1,1},{2,32},{3,33},{4,64},{5,65},{6,96},{7,97},{8,8},{9,9},... | collective-permute-start | bytes 393224 | tf_op jit(solution)/shard_map/ppermute | solution.py:43
  12.3 4.1 %collective-permute-done = bf16[256,256]{1,0:T(8,128)(2,1)S(1)} collective-permute-done((bf16[256,256]{1,0:T(8,128)(2,1)S(1)}, bf16[256,256]{1,0:T(8,128)(2,1)S(1)}, u32[]{:S(2)}, u32[]{:S(2)}) %collective-permute-start) | collective-permute-done | bytes 131104 | tf_op jit(solution)/shard_map/ppermute | solution.py:43
  16.4 5.8 %collective-permute-done.1 = bf16[256,256]{1,0:T(8,128)(2,1)S(1)} collective-permute-done((bf16[256,256]{1,0:T(8,128)(2,1)S(1)}, bf16[256,256]{1,0:T(8,128)(2,1)S(1)}, u32[]{:S(2)}, u32[]{:S(2)}) %collective-permute-start.1) | collective-permute-done | bytes 131104 | tf_op jit(solution)/shard_map/ppermute | solution.py:43
  34.3 7.7 %collective-permute-done.8 = bf16[256,256]{1,0:T(8,128)(2,1)S(1)} collective-permute-done((bf16[256,256]{1,0:T(8,128)(2,1)S(1)}, bf16[256,256]{1,0:T(8,128)(2,1)S(1)}, u32[]{:S(2)}, u32[]{:S(2)}) %collective-permute-start.8) | collective-permute-done | bytes 131104 | tf_op jit(solution)/shard_map/ppermute | solution.py:22
  42.2 5.2 %collective-permute-start.10 = (bf16[256,1024]{1,0:T(8,128)(2,1)S(1)}, bf16[256,1024]{1,0:T(8,128)(2,1)}, u32[]{:S(2)}, u32[]{:S(2)}) collective-permute-start(bf16[256,1024]{1,0:T(8,128)(2,1)S(1)} %constant_dynamic-update-slice_fusion.refs_0_), channel_id=1, source_target_pairs={{0,16},{8,24},{16,0},{24,8},{32,48},{40,56},{48,32},{56,40},{64,80... | collective-permute-start | bytes 1572872 | tf_op jit(solution)/shard_map/ppermute | solution.py:22
  50.1 3.6 %collective-permute-done.9.refs_1_ = bf16[256,1024]{1,0:T(8,128)(2,1)} collective-permute-done((bf16[256,1024]{1,0:T(8,128)(2,1)S(1)}, bf16[256,1024]{1,0:T(8,128)(2,1)}, u32[]{:S(2)}, u32[]{:S(2)}) %collective-permute-start.9) | collective-permute-done | bytes 524320 | tf_op jit(solution)/shard_map/ppermute | solution.py:22
  56.4 4.4 %shard_map.129.rows_ref = bf16[1024,2048]{1,0:T(8,128)(2,1)} custom-call(s32[3]{0:T(128)} %pad_add_fusion.1.index, bf16[2,512,1024]{2,1,0:T(8,128)(2,1)} %own_ref, bf16[2,512,1024]{2,1,0:T(8,128)(2,1)} %copy-done.2), custom_call_target="tpu_custom_call" | custom-call | bytes 8388608 | tf_op jit(solution)/shard_map/pallas_call | solution.py:122
  60.9 7.9 %collective-permute-done.12.refs_5_ = bf16[1024,256]{1,0:T(8,128)(2,1)} collective-permute-done((bf16[1024,256]{1,0:T(8,128)(2,1)}, bf16[1024,256]{1,0:T(8,128)(2,1)}, u32[]{:S(2)}, u32[]{:S(2)}) %collective-permute-start.12) | collective-permute-done | bytes 524320 | tf_op jit(solution)/shard_map/ppermute | solution.py:17
  68.8 11.3 %shard_map.130 = (bf16[1024,256]{1,0:T(8,128)(2,1)}, bf16[1024,256]{1,0:T(8,128)(2,1)}, bf16[1024,256]{1,0:T(8,128)(2,1)}, bf16[1024,256]{1,0:T(8,128)(2,1)}) custom-call(s32[1]{0:T(128)} %bitcast.5.index, bf16[1024,2048]{1,0:T(8,128)(2,1)} %shard_map.129.rows_ref, bf16[256,1024]{1,0:T(8,128)(2,1)} %copy-done.13, ...), custom_call_target="tpu_custom_call" | custom-call | flops 4294967296 | bytes 10485760 | tf_op jit(solution)/shard_map/pallas_call | solution.py:185
  89.3 7.5 %collective-permute-done.15.far_ref = bf16[1024,256]{1,0:T(8,128)(2,1)S(1)} collective-permute-done((bf16[1024,256]{1,0:T(8,128)(2,1)}, bf16[1024,256]{1,0:T(8,128)(2,1)S(1)}, u32[]{:S(2)}, u32[]{:S(2)}) %collective-permute-start.15) | collective-permute-done | bytes 524320 | tf_op jit(solution)/shard_map/ppermute | solution.py:27
  96.8 6.6 %collective-permute-done.16.left_ref = bf16[1024,256]{1,0:T(8,128)(2,1)S(1)} collective-permute-done((bf16[1024,256]{1,0:T(8,128)(2,1)}, bf16[1024,256]{1,0:T(8,128)(2,1)S(1)}, u32[]{:S(2)}, u32[]{:S(2)}) %collective-permute-start.16) | collective-permute-done | bytes 524320 | tf_op jit(solution)/shard_map/ppermute | solution.py:27
  105.8 4.0 %shard_map.131 = (f32[1024,128]{1,0:T(8,128)}, bf16[512,256]{1,0:T(8,128)(2,1)}, bf16[512,256]{1,0:T(8,128)(2,1)}) custom-call(bf16[1024,256]{1,0:T(8,128)(2,1)} %get-tuple-element.49.own_ref, bf16[1024,256]{1,0:T(8,128)(2,1)} %copy-done.3, bf16[1024,256]{1,0:T(8,128)(2,1)} %copy-done.4, bf16[1024,256]{1,0:T(8,128)(2,1)} %copy-done.5, f32[1,128]{1,0:T(1,128)} %bitcast.16), custom_call_target="tpu_custom_call" | custom-call | flops 1572864 | bytes 3145728 | tf_op jit(solution)/shard_map/pallas_call | solution.py:232
  113.1 6.6 %shard_map.132 = (bf16[2,128,1024]{2,1,0:T(8,128)(2,1)}, bf16[2,128,1024]{2,1,0:T(8,128)(2,1)}, bf16[512,256]{1,0:T(8,128)(2,1)}) custom-call(s32[3]{0:T(128)} %pad_add_fusion.2.index, f32[1]{0:T(128)S(6)} %tanh.3.ratio_ref, bf16[2,128,1024]{2,1,0:T(8,128)(2,1)} %q_ref.3, bf16[2,128,1024]{2,1,0:T(8,128)(2,1)} %cot_ref.3, ...), custom_call_target="tpu_custom_call" | custom-call | flops 939524096 | bytes 1441792 | tf_op jit(solution)/shard_map/pallas_call | solution.py:396
  120.4 6.5 %shard_map.133 = (bf16[2,128,1024]{2,1,0:T(8,128)(2,1)}, bf16[2,128,1024]{2,1,0:T(8,128)(2,1)}, bf16[512,256]{1,0:T(8,128)(2,1)}) custom-call(s32[3]{0:T(128)} %pad_add_fusion.index, f32[1]{0:T(128)S(6)} %tanh.3.ratio_ref, bf16[2,128,1024]{2,1,0:T(8,128)(2,1)} %q_ref.3, bf16[2,128,1024]{2,1,0:T(8,128)(2,1)} %cot_ref.3, ...), custom_call_target="tpu_custom_call", output_to_operand_aliasing={{0}: (7, {}), {1}: (8, {})} | custom-call | flops 939524096 | bytes 1441792 | tf_op jit(solution)/shard_map/pallas_call | solution.py:396
  148.9 4.4 %collective-permute-done.20.refs_1_ = bf16[512,256]{1,0:T(8,128)(2,1)S(1)} collective-permute-done((bf16[512,256]{1,0:T(8,128)(2,1)}, bf16[512,256]{1,0:T(8,128)(2,1)S(1)}, u32[]{:S(2)}, u32[]{:S(2)}) %collective-permute-start.20) | collective-permute-done | bytes 262176 | tf_op jit(solution)/shard_map/ppermute | solution.py:27
  153.3 4.1 %collective-permute-done.21.refs_2_ = bf16[512,256]{1,0:T(8,128)(2,1)S(1)} collective-permute-done((bf16[512,256]{1,0:T(8,128)(2,1)}, bf16[512,256]{1,0:T(8,128)(2,1)S(1)}, u32[]{:S(2)}, u32[]{:S(2)}) %collective-permute-start.21) | collective-permute-done | bytes 262176 | tf_op jit(solution)/shard_map/ppermute | solution.py:27
  167.6 3.8 %collective-permute-start.34 = (bf16[1024,256]{1,0:T(8,128)(2,1)S(1)}, bf16[1024,256]{1,0:T(8,128)(2,1)S(1)}, u32[]{:S(2)}, u32[]{:S(2)}) collective-permute-start(bf16[1024,256]{1,0:T(8,128)(2,1)S(1)} %fusion.25), channel_id=1, source_target_pairs={{0,96},{8,104},{16,112},{24,120},{32,0},{40,8},{48,16},{56,24},{64... | collective-permute-start | bytes 1572872 | tf_op jit(solution)/shard_map/ppermute | solution.py:17
  178.9 6.6 %collective-permute-done.26 = bf16[256,1024]{1,0:T(8,128)(2,1)S(1)} collective-permute-done((bf16[256,1024]{1,0:T(8,128)(2,1)S(1)}, bf16[256,1024]{1,0:T(8,128)(2,1)S(1)}, u32[]{:S(2)}, u32[]{:S(2)}) %collective-permute-start.26) | collective-permute-done | bytes 524320 | tf_op jit(solution)/shard_map/ppermute | solution.py:22
  185.4 4.0 %collective-permute-start.28 = (bf16[256,1024]{1,0:T(8,128)(2,1)S(1)}, bf16[256,1024]{1,0:T(8,128)(2,1)S(1)}, u32[]{:S(2)}, u32[]{:S(2)}) collective-permute-start(bf16[256,1024]{1,0:T(8,128)(2,1)S(1)} %convolution_convert_fusion.1), channel_id=1, source_target_pairs={{0,8},{8,16},{16,24},{24,0},{32,40},{40,48},{48,56},{56,32},{64,72... | collective-permute-start | bytes 1572872 | tf_op jit(solution)/shard_map/ppermute | solution.py:22
  189.5 5.6 %collective-permute-done.27 = bf16[1024,256]{1,0:T(8,128)(2,1)S(1)} collective-permute-done((bf16[1024,256]{1,0:T(8,128)(2,1)S(1)}, bf16[1024,256]{1,0:T(8,128)(2,1)S(1)}, u32[]{:S(2)}, u32[]{:S(2)}) %collective-permute-start.27) | collective-permute-done | bytes 524320 | tf_op jit(solution)/shard_map/ppermute | solution.py:17
  207.0 4.7 %collective-permute-done.31 = bf16[256,256]{1,0:T(8,128)(2,1)S(1)} collective-permute-done((bf16[256,256]{1,0:T(8,128)(2,1)S(1)}, bf16[256,256]{1,0:T(8,128)(2,1)S(1)}, u32[]{:S(2)}, u32[]{:S(2)}) %collective-permute-start.31) | collective-permute-done | bytes 131104 | tf_op jit(solution)/shard_map/ppermute | solution.py:17
  211.8 4.8 %collective-permute-start.38 = (bf16[512,256]{1,0:T(8,128)(2,1)S(1)}, bf16[512,256]{1,0:T(8,128)(2,1)S(1)}, u32[]{:S(2)}, u32[]{:S(2)}) collective-permute-start(bf16[512,256]{1,0:T(8,128)(2,1)S(1)} %pad_maximum_fusion), channel_id=1, source_target_pairs={{0,0},{1,1},{2,32},{3,33},{4,64},{5,65},{6,96},{7,97},{8,8},{9,9},... | collective-permute-start | bytes 786440 | tf_op jit(solution)/shard_map/ppermute | solution.py:43
  216.6 8.9 %collective-permute-done.38 = bf16[512,256]{1,0:T(8,128)(2,1)S(1)} collective-permute-done((bf16[512,256]{1,0:T(8,128)(2,1)S(1)}, bf16[512,256]{1,0:T(8,128)(2,1)S(1)}, u32[]{:S(2)}, u32[]{:S(2)}) %collective-permute-start.38) | collective-permute-done | bytes 262176 | tf_op jit(solution)/shard_map/ppermute | solution.py:43
  (131 shorter events, 83.5 us)
Async XLA Ops:
  2.5 19.8 %collective-permute-start.2 = (bf16[2,512,1024]{2,1,0:T(8,128)(2,1)}, bf16[2,512,1024]{2,1,0:T(8,128)(2,1)S(1)}, u32[]{:S(2)}, u32[]{:S(2)}) collective-permute-start(bf16[2,512,1024]{2,1,0:T(8,128)(2,1)} %own_ref), channel_id=1, source_target_pairs={{0,1},{1,0},{2,3},{3,2},{4,5},{5,4},{6,7},{7,6},{8,9},{9,8},{10,11... | collective-permute-start | bytes 6291464 | tf_op jit(solution)/shard_map/ppermute | solution.py:31
  2.6 13.9 %collective-permute-start = (bf16[256,256]{1,0:T(8,128)(2,1)S(1)}, bf16[256,256]{1,0:T(8,128)(2,1)S(1)}, u32[]{:S(2)}, u32[]{:S(2)}) collective-permute-start(bf16[256,256]{1,0:T(8,128)(2,1)S(1)} %get-tuple-element.36), channel_id=1, source_target_pairs={{0,0},{1,1},{2,32},{3,33},{4,64},{5,65},{6,96},{7,97},{8,8},{9,9},... | collective-permute-start | bytes 393224 | tf_op jit(solution)/shard_map/ppermute | solution.py:43
  8.3 13.9 %collective-permute-start.1 = (bf16[256,256]{1,0:T(8,128)(2,1)S(1)}, bf16[256,256]{1,0:T(8,128)(2,1)S(1)}, u32[]{:S(2)}, u32[]{:S(2)}) collective-permute-start(bf16[256,256]{1,0:T(8,128)(2,1)S(1)} %get-tuple-element.37), channel_id=1, source_target_pairs={{0,0},{1,1},{2,32},{3,33},{4,64},{5,65},{6,96},{7,97},{8,8},{9,9},... | collective-permute-start | bytes 393224 | tf_op jit(solution)/shard_map/ppermute | solution.py:43
  42.1 11.7 %collective-permute-start.9 = (bf16[256,1024]{1,0:T(8,128)(2,1)S(1)}, bf16[256,1024]{1,0:T(8,128)(2,1)}, u32[]{:S(2)}, u32[]{:S(2)}) collective-permute-start(bf16[256,1024]{1,0:T(8,128)(2,1)S(1)} %constant_dynamic-update-slice_fusion.refs_0_), channel_id=1, source_target_pairs={{0,8},{8,16},{16,24},{24,0},{32,40},{40,48},{48,56},{56,32},{64,72... | collective-permute-start | bytes 1572872 | tf_op jit(solution)/shard_map/ppermute | solution.py:22
  42.2 18.6 %collective-permute-start.10 = (bf16[256,1024]{1,0:T(8,128)(2,1)S(1)}, bf16[256,1024]{1,0:T(8,128)(2,1)}, u32[]{:S(2)}, u32[]{:S(2)}) collective-permute-start(bf16[256,1024]{1,0:T(8,128)(2,1)S(1)} %constant_dynamic-update-slice_fusion.refs_0_), channel_id=1, source_target_pairs={{0,16},{8,24},{16,0},{24,8},{32,48},{40,56},{48,32},{56,40},{64,80... | collective-permute-start | bytes 1572872 | tf_op jit(solution)/shard_map/ppermute | solution.py:22
  47.5 13.4 %collective-permute-start.11 = (bf16[256,1024]{1,0:T(8,128)(2,1)S(1)}, bf16[256,1024]{1,0:T(8,128)(2,1)}, u32[]{:S(2)}, u32[]{:S(2)}) collective-permute-start(bf16[256,1024]{1,0:T(8,128)(2,1)S(1)} %constant_dynamic-update-slice_fusion.refs_0_), channel_id=1, source_target_pairs={{0,24},{8,0},{16,8},{24,16},{32,56},{40,32},{48,40},{56,48},{64,88... | collective-permute-start | bytes 1572872 | tf_op jit(solution)/shard_map/ppermute | solution.py:22
  50.1 18.7 %collective-permute-start.12 = (bf16[1024,256]{1,0:T(8,128)(2,1)}, bf16[1024,256]{1,0:T(8,128)(2,1)}, u32[]{:S(2)}, u32[]{:S(2)}) collective-permute-start(bf16[1024,256]{1,0:T(8,128)(2,1)} %constant_dynamic-update-slice_fusion.4.refs_4_), channel_id=1, source_target_pairs={{0,32},{8,40},{16,48},{24,56},{32,64},{40,72},{48,80},{56,88},{64,... | collective-permute-start | bytes 1572872 | tf_op jit(solution)/shard_map/ppermute | solution.py:17
  50.1 18.7 %collective-permute-start.13 = (bf16[1024,256]{1,0:T(8,128)(2,1)}, bf16[1024,256]{1,0:T(8,128)(2,1)}, u32[]{:S(2)}, u32[]{:S(2)}) collective-permute-start(bf16[1024,256]{1,0:T(8,128)(2,1)} %constant_dynamic-update-slice_fusion.4.refs_4_), channel_id=1, source_target_pairs={{0,64},{8,72},{16,80},{24,88},{32,96},{40,104},{48,112},{56,120},{... | collective-permute-start | bytes 1572872 | tf_op jit(solution)/shard_map/ppermute | solution.py:17
  53.8 15.1 %collective-permute-start.14 = (bf16[1024,256]{1,0:T(8,128)(2,1)}, bf16[1024,256]{1,0:T(8,128)(2,1)}, u32[]{:S(2)}, u32[]{:S(2)}) collective-permute-start(bf16[1024,256]{1,0:T(8,128)(2,1)} %constant_dynamic-update-slice_fusion.4.refs_4_), channel_id=1, source_target_pairs={{0,96},{8,104},{16,112},{24,120},{32,0},{40,8},{48,16},{56,24},{64... | collective-permute-start | bytes 1572872 | tf_op jit(solution)/shard_map/ppermute | solution.py:17
  80.1 16.7 %collective-permute-start.15 = (bf16[1024,256]{1,0:T(8,128)(2,1)}, bf16[1024,256]{1,0:T(8,128)(2,1)S(1)}, u32[]{:S(2)}, u32[]{:S(2)}) collective-permute-start(bf16[1024,256]{1,0:T(8,128)(2,1)} %get-tuple-element.50), channel_id=1, source_target_pairs={{0,4},{1,5},{2,6},{3,7},{4,0},{5,1},{6,2},{7,3},{8,12},{9,13},{10,... | collective-permute-start | bytes 1572872 | tf_op jit(solution)/shard_map/ppermute | solution.py:27
  82.1 21.3 %collective-permute-start.16 = (bf16[1024,256]{1,0:T(8,128)(2,1)}, bf16[1024,256]{1,0:T(8,128)(2,1)S(1)}, u32[]{:S(2)}, u32[]{:S(2)}) collective-permute-start(bf16[1024,256]{1,0:T(8,128)(2,1)} %get-tuple-element.51), channel_id=1, source_target_pairs={{0,2},{1,3},{2,4},{3,5},{4,6},{5,7},{6,0},{7,1},{8,10},{9,11},{10,... | collective-permute-start | bytes 1572872 | tf_op jit(solution)/shard_map/ppermute | solution.py:27
  82.6 22.4 %collective-permute-start.17 = (bf16[1024,256]{1,0:T(8,128)(2,1)}, bf16[1024,256]{1,0:T(8,128)(2,1)S(1)}, u32[]{:S(2)}, u32[]{:S(2)}) collective-permute-start(bf16[1024,256]{1,0:T(8,128)(2,1)} %get-tuple-element.52), channel_id=1, source_target_pairs={{0,6},{1,7},{2,0},{3,1},{4,2},{5,3},{6,4},{7,5},{8,14},{9,15},{10,... | collective-permute-start | bytes 1572872 | tf_op jit(solution)/shard_map/ppermute | solution.py:27
  135.0 12.8 %collective-permute-start.24 = (bf16[512,256]{1,0:T(8,128)(2,1)}, bf16[512,256]{1,0:T(8,128)(2,1)S(1)}, u32[]{:S(2)}, u32[]{:S(2)}) collective-permute-start(bf16[512,256]{1,0:T(8,128)(2,1)} %shard_map.135.refs_4_), channel_id=1, source_target_pairs={{0,4},{1,5},{2,6},{3,7},{4,0},{5,1},{6,2},{7,3},{8,12},{9,13},{10,... | collective-permute-start | bytes 786440 | tf_op jit(solution)/shard_map/ppermute | solution.py:27
  135.0 14.0 %collective-permute-start.25 = (bf16[512,256]{1,0:T(8,128)(2,1)}, bf16[512,256]{1,0:T(8,128)(2,1)S(1)}, u32[]{:S(2)}, u32[]{:S(2)}) collective-permute-start(bf16[512,256]{1,0:T(8,128)(2,1)} %shard_map.135.refs_4_), channel_id=1, source_target_pairs={{0,6},{1,7},{2,0},{3,1},{4,2},{5,3},{6,4},{7,5},{8,14},{9,15},{10,... | collective-permute-start | bytes 786440 | tf_op jit(solution)/shard_map/ppermute | solution.py:27
  139.8 13.6 %collective-permute-start.20 = (bf16[512,256]{1,0:T(8,128)(2,1)}, bf16[512,256]{1,0:T(8,128)(2,1)S(1)}, u32[]{:S(2)}, u32[]{:S(2)}) collective-permute-start(bf16[512,256]{1,0:T(8,128)(2,1)} %shard_map.134.refs_0_), channel_id=1, source_target_pairs={{0,2},{1,3},{2,4},{3,5},{4,6},{5,7},{6,0},{7,1},{8,10},{9,11},{10,... | collective-permute-start | bytes 786440 | tf_op jit(solution)/shard_map/ppermute | solution.py:27
  142.6 14.8 %collective-permute-start.21 = (bf16[512,256]{1,0:T(8,128)(2,1)}, bf16[512,256]{1,0:T(8,128)(2,1)S(1)}, u32[]{:S(2)}, u32[]{:S(2)}) collective-permute-start(bf16[512,256]{1,0:T(8,128)(2,1)} %shard_map.134.refs_0_), channel_id=1, source_target_pairs={{0,4},{1,5},{2,6},{3,7},{4,0},{5,1},{6,2},{7,3},{8,12},{9,13},{10,... | collective-permute-start | bytes 786440 | tf_op jit(solution)/shard_map/ppermute | solution.py:27
  143.3 14.9 %collective-permute-start.22 = (bf16[512,256]{1,0:T(8,128)(2,1)}, bf16[512,256]{1,0:T(8,128)(2,1)S(1)}, u32[]{:S(2)}, u32[]{:S(2)}) collective-permute-start(bf16[512,256]{1,0:T(8,128)(2,1)} %shard_map.134.refs_0_), channel_id=1, source_target_pairs={{0,6},{1,7},{2,0},{3,1},{4,2},{5,3},{6,4},{7,5},{8,14},{9,15},{10,... | collective-permute-start | bytes 786440 | tf_op jit(solution)/shard_map/ppermute | solution.py:27
  167.6 27.4 %collective-permute-start.34 = (bf16[1024,256]{1,0:T(8,128)(2,1)S(1)}, bf16[1024,256]{1,0:T(8,128)(2,1)S(1)}, u32[]{:S(2)}, u32[]{:S(2)}) collective-permute-start(bf16[1024,256]{1,0:T(8,128)(2,1)S(1)} %fusion.25), channel_id=1, source_target_pairs={{0,96},{8,104},{16,112},{24,120},{32,0},{40,8},{48,16},{56,24},{64... | collective-permute-start | bytes 1572872 | tf_op jit(solution)/shard_map/ppermute | solution.py:17
  171.4 25.0 %collective-permute-start.33 = (bf16[1024,256]{1,0:T(8,128)(2,1)S(1)}, bf16[1024,256]{1,0:T(8,128)(2,1)S(1)}, u32[]{:S(2)}, u32[]{:S(2)}) collective-permute-start(bf16[1024,256]{1,0:T(8,128)(2,1)S(1)} %fusion.22), channel_id=1, source_target_pairs={{0,32},{8,40},{16,48},{24,56},{32,64},{40,72},{48,80},{56,88},{64,... | collective-permute-start | bytes 1572872 | tf_op jit(solution)/shard_map/ppermute | solution.py:17
  171.4 14.0 %collective-permute-start.26 = (bf16[256,1024]{1,0:T(8,128)(2,1)S(1)}, bf16[256,1024]{1,0:T(8,128)(2,1)S(1)}, u32[]{:S(2)}, u32[]{:S(2)}) collective-permute-start(bf16[256,1024]{1,0:T(8,128)(2,1)S(1)} %convolution_convert_fusion.2), channel_id=1, source_target_pairs={{0,16},{8,24},{16,0},{24,8},{32,48},{40,56},{48,32},{56,40},{64,80... | collective-permute-start | bytes 1572872 | tf_op jit(solution)/shard_map/ppermute | solution.py:22
  172.5 22.6 %collective-permute-start.27 = (bf16[1024,256]{1,0:T(8,128)(2,1)S(1)}, bf16[1024,256]{1,0:T(8,128)(2,1)S(1)}, u32[]{:S(2)}, u32[]{:S(2)}) collective-permute-start(bf16[1024,256]{1,0:T(8,128)(2,1)S(1)} %fusion.19), channel_id=1, source_target_pairs={{0,64},{8,72},{16,80},{24,88},{32,96},{40,104},{48,112},{56,120},{... | collective-permute-start | bytes 1572872 | tf_op jit(solution)/shard_map/ppermute | solution.py:17
  174.8 26.3 %collective-permute-start.29 = (bf16[256,1024]{1,0:T(8,128)(2,1)S(1)}, bf16[256,1024]{1,0:T(8,128)(2,1)S(1)}, u32[]{:S(2)}, u32[]{:S(2)}) collective-permute-start(bf16[256,1024]{1,0:T(8,128)(2,1)S(1)} %convolution_convert_fusion), channel_id=1, source_target_pairs={{0,24},{8,0},{16,8},{24,16},{32,56},{40,32},{48,40},{56,48},{64,88... | collective-permute-start | bytes 1572872 | tf_op jit(solution)/shard_map/ppermute | solution.py:22
  185.4 15.6 %collective-permute-start.28 = (bf16[256,1024]{1,0:T(8,128)(2,1)S(1)}, bf16[256,1024]{1,0:T(8,128)(2,1)S(1)}, u32[]{:S(2)}, u32[]{:S(2)}) collective-permute-start(bf16[256,1024]{1,0:T(8,128)(2,1)S(1)} %convolution_convert_fusion.1), channel_id=1, source_target_pairs={{0,8},{8,16},{16,24},{24,0},{32,40},{40,48},{48,56},{56,32},{64,72... | collective-permute-start | bytes 1572872 | tf_op jit(solution)/shard_map/ppermute | solution.py:22
  211.8 13.8 %collective-permute-start.38 = (bf16[512,256]{1,0:T(8,128)(2,1)S(1)}, bf16[512,256]{1,0:T(8,128)(2,1)S(1)}, u32[]{:S(2)}, u32[]{:S(2)}) collective-permute-start(bf16[512,256]{1,0:T(8,128)(2,1)S(1)} %pad_maximum_fusion), channel_id=1, source_target_pairs={{0,0},{1,1},{2,32},{3,33},{4,64},{5,65},{6,96},{7,97},{8,8},{9,9},... | collective-permute-start | bytes 786440 | tf_op jit(solution)/shard_map/ppermute | solution.py:43
  (32 other events, 313.5 us)

commit v5 on v3

v5 whole, which is shorter than its diff:
```python
import functools

import jax
import jax.numpy as jnp
from jax import lax
from jax.experimental import pallas as pl
from jax.experimental.pallas import tpu as pltpu
from jax.sharding import PartitionSpec as P

TILE = 128
RING = 4
EPS = 1e-06


def along_z(x, step):
    pairs = [(z * RING + y, (z + step) % RING * RING + y) for z in range(RING) for y in range(RING)]
    return lax.ppermute(x, "dp", pairs)


def by_core(x, step, z_core):
    pairs = []
    for z in range(RING):
        for y in range(RING):
            for i in range(RING):
                for c in range(2):
                    to_z, to_y = (z + step, y) if c == z_core else (z, y + step)
                    source = (z * RING + y) * 2 * RING + i * 2 + c
                    target = (to_z % RING * RING + to_y % RING) * 2 * RING + i * 2 + c
                    pairs.append((source, target))
    return lax.ppermute(x, ("dp", "tensor"), pairs)


def inner(x, step):
    return by_core(x, step, 0)


def outer(x, step):
    return by_core(x, step, 1)


def along_x(x, step):
    pairs = [(i * 2 + c, (i + step) % RING * 2 + c) for i in range(RING) for c in range(2)]
    return lax.ppermute(x, "tensor", pairs)


def other_core(x):
    return lax.ppermute(x, "tensor", [(i, i ^ 1) for i in range(2 * RING)])


def exchange_xz(x):
    pairs = []
    for z in range(RING):
        for y in range(RING):
            for i in range(RING):
                for c in range(2):
                    source = (z * RING + y) * 2 * RING + i * 2 + c
                    target = (i * RING + y) * 2 * RING + z * 2 + c
                    pairs.append((source, target))
    return lax.ppermute(x, ("dp", "tensor"), pairs)


def gathered(block, move):
    far, after, before = (move(block, step) for step in (2, 1, 3))
    return [block, after, far, before]


def scattered(parts, move):
    return [move(parts[step], step) for step in (2, 1, 3)]


def summed(blocks):
    total = blocks[0].astype(jnp.float32)
    for block in blocks[1:]:
        total = total + block.astype(jnp.float32)
    return total


def rms_factor(values):
    return lax.rsqrt(jnp.mean(values * values, axis=-1, keepdims=True) + EPS)


def norm_back(values, norm_multiplier, gain, grad):
    weighted = grad * gain
    inner = jnp.sum(weighted * values, axis=-1, keepdims=True)
    return (
        norm_multiplier * weighted
        - values * (norm_multiplier * norm_multiplier * norm_multiplier) * inner / values.shape[-1]
    )


def matmul(a, b, contract):
    return lax.dot_general(a, b, (contract, ((), ())), preferred_element_type=jnp.float32)


VMEM = pl.BlockSpec(memory_space=pltpu.VMEM)
SMEM = pl.BlockSpec(memory_space=pltpu.SMEM)
ANY = pl.BlockSpec(memory_space=pl.ANY)
PARAMS = pltpu.CompilerParams(vmem_limit_bytes=16 * 1024 * 1024)


def arrange_kernel(index, own_ref, other_ref, out_ref, sems):
    slots, rows, depth = own_ref.shape
    width = 2 * depth // RING
    y, core, far_slot = index[0], index[1], index[2]
    waits = []
    for s in range(slots):
        for o in range(RING):
            block = ((y - o + RING) % RING) ^ (2 * core)
            columns = pl.ds(pl.multiple_of(block % 2 * width, width), width)
            target = out_ref.at[pl.ds(s * rows, rows), pl.ds(o * width, width)]
            sem = sems.at[len(waits)]
            own = pltpu.make_async_copy(own_ref.at[s ^ far_slot, :, columns], target, sem)
            other = pltpu.make_async_copy(other_ref.at[s ^ far_slot, :, columns], target, sem)
            pl.when(block < 2)(own.start)
            pl.when(block >= 2)(other.start)
            waits.append(own)
    for copy in waits:
        copy.wait()


def arrange(index, own, other):
    slots, rows, depth = own.shape
    return pl.pallas_call(
        arrange_kernel,
        in_specs=[SMEM, ANY, ANY],
        out_specs=VMEM,
        out_shape=jax.ShapeDtypeStruct((slots * rows, 2 * depth), own.dtype),
        scratch_shapes=[pltpu.SemaphoreType.DMA((slots * RING,))],
        compiler_params=PARAMS,
        cost_estimate=pl.CostEstimate(flops=0, bytes_accessed=8 * own.size, transcendentals=0),
    )(index, own, other)


def assemble_kernel(index, *refs):
    pieces, out_ref, sems = refs[:RING], refs[RING], refs[RING + 1]
    rows, both = pieces[0].shape
    count = rows // RING
    shift, core = index[0], index[1]
    copies = []
    for b in range(RING):
        for a in range(RING):
            along_z_by = jnp.where(core == 0, a, b)
            along_y_by = jnp.where(core == 0, b, a)
            start = pl.multiple_of(along_y_by * count, count)
            column = pl.multiple_of((shift - along_z_by + RING) % RING * both, both)
            target = out_ref.at[pl.ds(start, count), pl.ds(column, both)]
            source = pieces[b].at[pl.ds(a * count, count)]
            copies.append(pltpu.make_async_copy(source, target, sems.at[b, a]))
    for copy in copies:
        copy.start()
    for copy in copies:
        copy.wait()


def assemble(index, pieces):
    rows, both = pieces[0].shape
    return pl.pallas_call(
        assemble_kernel,
        in_specs=[SMEM] + [ANY] * RING,
        out_specs=VMEM,
        out_shape=jax.ShapeDtypeStruct((rows, RING * both), pieces[0].dtype),
        scratch_shapes=[pltpu.SemaphoreType.DMA((RING, RING))],
        compiler_params=PARAMS,
        cost_estimate=pl.CostEstimate(
            flops=0, bytes_accessed=4 * RING * rows * both, transcendentals=0
        ),
    )(index, *pieces)


def finish_kernel(own_ref, far_ref, left_ref, right_ref, gain_ref, raw_ref, first_ref, second_ref):
    rows, head_dim = raw_ref.shape
    total = summed([own_ref[...], far_ref[...], left_ref[...], right_ref[...]])
    raw = total[:, :head_dim]
    raw_ref[...] = raw
    keys = (raw * rms_factor(raw) * gain_ref[...]).astype(jnp.bfloat16)
    vals = total[:, head_dim:].astype(jnp.bfloat16)
    for i, out_ref in enumerate((first_ref, second_ref)):
        part = slice(i * rows // 2, (i + 1) * rows // 2)
        out_ref[:, :head_dim] = keys[part]
        out_ref[:, head_dim:] = vals[part]


def finish(blocks, gain):
    rows, both = blocks[0].shape
    return pl.pallas_call(
        finish_kernel,
        in_specs=[VMEM] * (RING + 1),
        out_specs=[VMEM] * 3,
        out_shape=[
            jax.ShapeDtypeStruct((rows, both // 2), jnp.float32),
            jax.ShapeDtypeStruct((rows // 2, both), jnp.bfloat16),
            jax.ShapeDtypeStruct((rows // 2, both), jnp.bfloat16),
        ],
        compiler_params=PARAMS,
        cost_estimate=pl.CostEstimate(
            flops=6 * rows * both, bytes_accessed=12 * rows * both, transcendentals=rows
        ),
    )(*blocks, gain[None, :])


def turn_kernel(slot, flag, raw_ref, grad_ref, other_ref, gain_ref, out_ref):
    rows, head_dim = grad_ref.shape[0], raw_ref.shape[1]
    grad = jnp.where(flag[2] != 0, other_ref[...], grad_ref[...])
    raw = raw_ref[slot * rows : (slot + 1) * rows]
    d_raw = norm_back(raw, rms_factor(raw), gain_ref[...], grad[:, :head_dim].astype(jnp.float32))
    out_ref[:, :head_dim] = d_raw.astype(jnp.bfloat16)
    out_ref[:, head_dim:] = grad[:, head_dim:]


def turn(flag, slot, raw, grad, other, gain):
    return pl.pallas_call(
        functools.partial(turn_kernel, slot),
        in_specs=[SMEM] + [VMEM] * 4,
        out_specs=VMEM,
        out_shape=jax.ShapeDtypeStruct(grad.shape, jnp.bfloat16),
        compiler_params=PARAMS,
        cost_estimate=pl.CostEstimate(
            flops=6 * grad.size, bytes_accessed=8 * grad.size, transcendentals=grad.shape[0]
        ),
    )(flag, raw, grad, other, gain[None, :])


def collect_kernel(index, *refs):
    sources, (out_ref, sems) = refs[:-2], refs[-2:]
    rows, both = sources[0].shape
    copies = []
    for i, source in enumerate(sources):
        slot, o = i // RING, i % RING
        start = pl.multiple_of((RING - index[0] - o + RING) % RING * both, both)
        target = out_ref.at[pl.ds(slot * rows, rows), pl.ds(start, both)]
        copies.append(pltpu.make_async_copy(source, target, sems.at[i]))
    for copy in copies:
        copy.start()
    for copy in copies:
        copy.wait()


def collect(index, first, second):
    rows, both = first[0].shape
    return pl.pallas_call(
        collect_kernel,
        in_specs=[SMEM] + [ANY] * (2 * RING),
        out_specs=VMEM,
        out_shape=jax.ShapeDtypeStruct((2 * rows, RING * both), first[0].dtype),
        scratch_shapes=[pltpu.SemaphoreType.DMA((2 * RING,))],
        compiler_params=PARAMS,
        cost_estimate=pl.CostEstimate(
            flops=0, bytes_accessed=8 * RING * rows * both, transcendentals=0
        ),
    )(index, *first, *second)


def product_kernel(step, index, feats_ref, grads_ref, out_ref):
    both = out_ref.shape[1]
    count = out_ref.shape[0] // RING
    core = index[1]
    for s in range(RING):
        row = jnp.where(core == 0, -step % RING, -s % RING)
        column = jnp.where(core == 0, s, step)
        block = matmul(
            feats_ref[:, pl.ds(pl.multiple_of(row * count, count), count)],
            grads_ref[:, pl.ds(pl.multiple_of(column * both, both), both)],
            ((0,), (0,)),
        )
        out_ref[s * count : (s + 1) * count] = block.astype(out_ref.dtype)


def product(step, index, feats, grads):
    shape = (feats.shape[1], grads.shape[1] // RING)
    return pl.pallas_call(
        functools.partial(product_kernel, step),
        in_specs=[SMEM, VMEM, VMEM],
        out_specs=VMEM,
        out_shape=jax.ShapeDtypeStruct(shape, jnp.bfloat16),
        compiler_params=PARAMS,
        cost_estimate=pl.CostEstimate(
            flops=2 * feats.shape[0] * shape[0] * shape[1],
            bytes_accessed=2 * feats.size + 2 * grads.size + 2 * shape[0] * shape[1],
            transcendentals=0,
        ),
    )(index, feats, grads)


def attend_kernel(heads, index, ratio_ref, q_ref, cot_ref, kv_ref, away_ref, gain_ref, *refs):
    context_ref, d_query_ref, d_kv_ref, d_key_sum, d_value_sum = refs[-5:]
    step = pl.program_id(0)
    head_dim = gain_ref.shape[1]
    scale = head_dim ** (-0.5)
    count = index[1]
    ratio = ratio_ref[0]
    gain = gain_ref[...]
    key_value = jnp.where(index[2] != 0, away_ref[...], kv_ref[...])
    keys = key_value[:, :head_dim]
    vals = key_value[:, head_dim:]

    def stacked(ref):
        parts = [ref[0, :, h * head_dim : (h + 1) * head_dim] for h in range(heads)]
        return jnp.concatenate(parts, axis=0).astype(jnp.float32)

    def unstacked(ref, rows):
        text = rows.shape[0] // heads
        for h in range(heads):
            part = rows[h * text : (h + 1) * text]
            ref[0, :, h * head_dim : (h + 1) * head_dim] = part.astype(ref.dtype)

    @pl.when(step == 0)
    def _():
        d_key_sum[...] = jnp.zeros_like(d_key_sum)
        d_value_sum[...] = jnp.zeros_like(d_value_sum)

    q_raw = stacked(q_ref)
    q_factor = rms_factor(q_raw)
    q_norm = (q_raw * q_factor * gain).astype(jnp.bfloat16)
    raw = matmul(q_norm, keys, ((1,), (1,))) * scale
    place = lax.broadcasted_iota(jnp.int32, raw.shape, 1)
    expo = jnp.where(place < count * TILE, jnp.exp(raw), 0.0)
    total = jnp.sum(expo, axis=1, keepdims=True) + (count == 0).astype(jnp.float32)
    inverse = 1.0 / total
    weights_b = expo.astype(jnp.bfloat16)
    attended = matmul(weights_b, vals, ((1,), (0,))) * inverse
    unstacked(context_ref, ratio * attended)
    d_att = ratio * stacked(cot_ref)
    d_att_b = d_att.astype(jnp.bfloat16)
    scaled_b = (d_att * inverse).astype(jnp.bfloat16)
    delta = jnp.sum(d_att * attended, axis=1, keepdims=True)
    d_prob = matmul(d_att_b, vals, ((1,), (1,)))
    d_score = (expo * inverse * (d_prob - delta)).astype(jnp.bfloat16)
    d_qn = scale * matmul(d_score, keys, ((1,), (0,)))
    unstacked(d_query_ref, norm_back(q_raw, q_factor, gain, d_qn))
    d_key_sum[...] += matmul(d_score, q_norm, ((0,), (0,)))
    d_value_sum[...] += matmul(weights_b, scaled_b, ((0,), (0,)))

    @pl.when(step == pl.num_programs(0) - 1)
    def _():
        d_kv_ref[:, :head_dim] = (scale * d_key_sum[...]).astype(d_kv_ref.dtype)
        d_kv_ref[:, head_dim:] = d_value_sum[...].astype(d_kv_ref.dtype)


def attend(index, ratio, query, cot, key_value, away, gain, earlier, heads=2):
    rows, both = key_value.shape
    head_dim = both // 2
    text = query.shape[1]
    width = heads * head_dim
    block = pl.BlockSpec((1, text, width), lambda h, index: (index[0], 0, h))
    whole = lambda shape: pl.BlockSpec(shape, lambda h, index: (0, 0))
    in_specs = [
        pl.BlockSpec(memory_space=pltpu.SMEM),
        block,
        block,
        whole((rows, both)),
        whole((rows, both)),
        whole((1, head_dim)),
    ]
    aliases = {}
    if earlier:
        in_specs += [pl.BlockSpec(memory_space=pl.ANY)] * 2
        aliases = {7: 0, 8: 1}
    steps = query.shape[2] // width
    return pl.pallas_call(
        functools.partial(attend_kernel, heads),
        grid_spec=pltpu.PrefetchScalarGridSpec(
            num_scalar_prefetch=1,
            grid=(steps,),
            in_specs=in_specs,
            out_specs=[block, block, whole((rows, both))],
            scratch_shapes=[pltpu.VMEM((rows, head_dim), jnp.float32)] * 2,
        ),
        out_shape=[
            jax.ShapeDtypeStruct(query.shape, jnp.bfloat16),
            jax.ShapeDtypeStruct(query.shape, jnp.bfloat16),
            jax.ShapeDtypeStruct((rows, both), jnp.bfloat16),
        ],
        input_output_aliases=aliases,
        compiler_params=pltpu.CompilerParams(
            vmem_limit_bytes=24 * 1024 * 1024
        ),
        cost_estimate=pl.CostEstimate(
            flops=14 * steps * heads * text * rows * head_dim,
            bytes_accessed=8 * text * steps * width + 6 * rows * head_dim,
            transcendentals=steps * heads * text * rows,
        ),
    )(
        index,
        ratio,
        query,
        cot,
        key_value,
        away,
        gain[None, :],
        *earlier,
    )


def per_device(
    query,
    image,
    tiles,
    image_slot,
    key_weight_matrix,
    value_weight_matrix,
    query_gain,
    key_gain,
    gate,
    cotangent,
):
    head_dim = query_gain.shape[0]
    samp_local, img_rows, depth = image.shape
    ratio = jnp.tanh(gate)
    rank = lax.axis_index("dp")
    place = lax.axis_index("tensor")
    z, y = rank // RING, rank % RING
    x, core = place // 2, place % 2

    first = rank * samp_local
    every = jnp.arange(tiles.shape[0], dtype=jnp.int32)
    local_ids = first + jnp.arange(samp_local, dtype=jnp.int32)
    match = image_slot[None, :] == local_ids[:, None]
    slot_sample = jnp.sum(jnp.where(match, every[None, :], 0), axis=1)
    slot_away = slot_sample // samp_local != rank
    swaps = jnp.any(slot_away)
    far_slot = jnp.where(slot_away[1], 1, 0)
    home_slot = lax.dynamic_slice_in_dim(image_slot, first, samp_local)
    own_away = home_slot // samp_local != rank
    own_of_slot = (home_slot[1] == first + far_slot).astype(jnp.int32)
    far_own = jnp.where(swaps, jnp.where(own_away[1], 1, 0), own_of_slot)
    home_tiles = lax.dynamic_slice_in_dim(tiles, first, samp_local)

    near_own = 1 - far_own
    zero = jnp.zeros((), jnp.int32)
    swapped = swaps.astype(jnp.int32)
    near_index = jnp.stack([near_own, home_tiles[near_own], zero]).astype(jnp.int32)
    far_index = jnp.stack([far_own, home_tiles[far_own], swapped]).astype(jnp.int32)
    feat_index = jnp.stack([y, core, far_slot]).astype(jnp.int32)
    ring_index = jnp.stack([(z - x + RING) % RING, core]).astype(jnp.int32)

    shard = jnp.concatenate([key_weight_matrix, value_weight_matrix], axis=1)
    shard, image = lax.optimization_barrier((shard, image))
    shard = exchange_xz(shard)
    other = other_core(image)
    shard, other, near_index, far_index, feat_index, ring_index, ratio = lax.optimization_barrier(
        (shard, other, near_index, far_index, feat_index, ring_index, ratio)
    )
    pieces = gathered(jnp.concatenate(gathered(shard, inner), axis=0), outer)
    weights = assemble(ring_index, pieces)

    feats = arrange(feat_index, image, other)

    both = 2 * head_dim
    blocks = [None] * RING
    for d in (2, 1, 3, 0):
        columns = weights[:, d * both : (d + 1) * both]
        blocks[d] = matmul(feats, columns, ((1,), (0,))).astype(jnp.bfloat16)
    arrived = scattered(blocks, along_x)
    raw, far_key_value, near_key_value = finish([blocks[0], *arrived], key_gain)

    away = along_z(far_key_value, RING // 2)
    shared = (ratio, query, cotangent)
    *earlier, near_grad = attend(
        near_index, *shared, near_key_value, near_key_value, query_gain, ()
    )
    near_rows = turn(near_index, 1, raw, near_grad, near_grad, key_gain)
    near_rows, away = lax.optimization_barrier((near_rows, away))
    near_all = gathered(near_rows, along_x)
    context, d_query, far_grad = attend(
        far_index, *shared, far_key_value, away, query_gain, earlier
    )
    back = along_z(far_grad, RING // 2)
    far_rows = turn(far_index, 0, raw, far_grad, back, key_gain)

    far_all = gathered(far_rows, along_x)
    grads = collect(ring_index, far_all, near_all)

    sent = [None] + [product(d, ring_index, feats, grads) for d in range(1, RING)]
    arrived = scattered(sent, outer)
    feats, grads, arrived[0] = lax.optimization_barrier((feats, grads, arrived[0]))
    total = summed([product(0, ring_index, feats, grads), *arrived])
    count = total.shape[0] // RING
    parts = [total[d * count : (d + 1) * count] for d in range(RING)]
    sent = [None] + [part.astype(jnp.bfloat16) for part in parts[1:]]
    arrived = scattered(sent, inner)
    share = summed([parts[0], *arrived]).astype(jnp.bfloat16)
    share = exchange_xz(share).astype(jnp.float32)
    return (context, d_query, share[:, :head_dim], share[:, head_dim:])


def solution(mesh):
    placed = (
        P("dp", None, "tensor"),
        P("dp", None, "tensor"),
        P(),
        P(),
        P("dp", "tensor"),
        P("dp", "tensor"),
        P(),
        P(),
        P(),
        P("dp", None, "tensor"),
    )
    return jax.shard_map(
        per_device,
        mesh=mesh,
        in_specs=placed,
        out_specs=(
            P("dp", None, "tensor"),
            P("dp", None, "tensor"),
            P("dp", "tensor"),
            P("dp", "tensor"),
        ),
        check_vma=False,
    )
```

time: 414 us -> 193 us (0.47)
  Pallas kernels: 223 us -> 25.2 us
  starting transfers between devices: 74.5 us -> 52.4 us
  waiting for transfers between devices: 89 us -> 94.1 us
  local copies, waits for them, and re-layouts: 9.06 us -> 4.05 us
    pallas_call x6 -> x10, Pallas kernels: 210 us -> 14.6 us  [the longest x4 8.13 us: product(): pl.pallas_call(functools.partial(product_kernel, step), in_specs=[SMEM, V...]
    ppermute x12, waiting for transfers between devices: 10.8 us -> 54.1 us  [by_core(): return lax.ppermute(x, ('dp', 'tensor'), pairs)]
    ppermute x14 -> x2, waiting for transfers between devices: 35.7 us -> 1.6 us  [along_z(): return lax.ppermute(x, 'dp', pairs)]
    ppermute x14 -> x2, starting transfers between devices: 26.1 us -> 3.25 us  [along_z(): return lax.ppermute(x, 'dp', pairs)]
    ppermute x9, starting transfers between devices: 11.8 us -> 19.8 us  [along_x(): return lax.ppermute(x, 'tensor', pairs)]
    ppermute x3 -> x2, starting transfers between devices: 17.9 us -> 11.2 us  [exchange_xz(): return lax.ppermute(x, ('dp', 'tensor'), pairs)]
    ppermute x3 -> x2, waiting for transfers between devices: 15.5 us -> 11.8 us  [exchange_xz(): return lax.ppermute(x, ('dp', 'tensor'), pairs)]
  transfers between devices with their start and end apart: 39 -> 26, of which waited for: 17 -> 20; matrix products, arithmetic and copies ran while one was open for 2% -> 4% of each run, Pallas kernels for 34% -> 8%
where the time goes in v5:
time: 193 us; the launch traced here: 191 us
  waiting for transfers between devices  94.1 us (49%)
  starting transfers between devices  52.4 us (27%)
  Pallas kernels  25.2 us (13%)
  other arithmetic  5.59 us (3%)
  matrix products  5.11 us (3%)
  between operations  4.88 us (3%)
  local copies, waits for them, and re-layouts  4.05 us (2%)
    ppermute x12, waiting for transfers between devices, by_core(): return lax.ppermute(x, ('dp', 'tensor'), pairs)  54.1 us
    ppermute x9, waiting for transfers between devices, along_x(): return lax.ppermute(x, 'tensor', pairs)  26.5 us
    ppermute x9, starting transfers between devices, along_x(): return lax.ppermute(x, 'tensor', pairs)  19.8 us
    ppermute x12, starting transfers between devices, by_core(): return lax.ppermute(x, ('dp', 'tensor'), pairs)  18.1 us
    ppermute x2, waiting for transfers between devices, exchange_xz(): return lax.ppermute(x, ('dp', 'tensor'), pairs)  11.8 us
    ppermute x2, starting transfers between devices, exchange_xz(): return lax.ppermute(x, ('dp', 'tensor'), pairs)  11.2 us
    pallas_call x2, Pallas kernels, attend(): pl.pallas_call(functools.partial(attend_kernel, heads), grid_spec=pltpu.P...  10.6 us
    pallas_call x4, Pallas kernels, product(): pl.pallas_call(functools.partial(product_kernel, step), in_specs=[SMEM, V...  8.13 us
  transfers between devices with their start and end apart: 26, of which 20 were waited for; matrix products, arithmetic and copies ran while one was open for 4% of the time, Pallas kernels for 8%

profile of v5, /device:TPU:4, one launch (start us, length us, event | category | flops | bytes accessed | tf_op | source)
XLA Modules:
  0.0 191.3 jit_solution(6705396525358075808)
XLA Ops:
  1.9 5.7 %collective-permute-start = (bf16[512,256]{1,0:T(8,128)(2,1)S(1)}, bf16[512,256]{1,0:T(8,128)(2,1)S(1)}, u32[]{:S(2)}, u32[]{:S(2)}) collective-permute-start(bf16[512,256]{1,0:T(8,128)(2,1)S(1)} %pad_maximum_fusion), channel_id=1, source_target_pairs={{0,0},{1,1},{2,32},{3,33},{4,64},{5,65},{6,96},{7,97},{8,8},{9,9},... | collective-permute-start | bytes 786440 | tf_op jit(solution)/shard_map/ppermute | solution.py:59
  20.9 3.2 %collective-permute-start.3 = (bf16[512,256]{1,0:T(8,128)(2,1)S(1)}, bf16[512,256]{1,0:T(8,128)(2,1)S(1)}, u32[]{:S(2)}, u32[]{:S(2)}) collective-permute-start(bf16[512,256]{1,0:T(8,128)(2,1)S(1)} %collective-permute-done), channel_id=1, source_target_pairs={{0,64},{1,17},{2,66},{3,19},{4,68},{5,21},{6,70},{7,23},{8,72},{9,... | collective-permute-start | bytes 786440 | tf_op jit(solution)/shard_map/ppermute | solution.py:30
  24.2 4.3 %collective-permute-done.2 = bf16[512,256]{1,0:T(8,128)(2,1)S(1)} collective-permute-done((bf16[512,256]{1,0:T(8,128)(2,1)S(1)}, bf16[512,256]{1,0:T(8,128)(2,1)S(1)}, u32[]{:S(2)}, u32[]{:S(2)}) %collective-permute-start.2) | collective-permute-done | bytes 262176 | tf_op jit(solution)/shard_map/ppermute | solution.py:30
  28.4 2.8 %collective-permute-done.3 = bf16[512,256]{1,0:T(8,128)(2,1)S(1)} collective-permute-done((bf16[512,256]{1,0:T(8,128)(2,1)S(1)}, bf16[512,256]{1,0:T(8,128)(2,1)S(1)}, u32[]{:S(2)}, u32[]{:S(2)}) %collective-permute-start.3) | collective-permute-done | bytes 262176 | tf_op jit(solution)/shard_map/ppermute | solution.py:30
  32.2 3.1 %collective-permute-start.7 = (bf16[2048,256]{1,0:T(8,128)(2,1)S(1)}, bf16[2048,256]{1,0:T(8,128)(2,1)S(1)}, u32[]{:S(2)}, u32[]{:S(2)}) collective-permute-start(bf16[2048,256]{1,0:T(8,128)(2,1)S(1)} %constant_dynamic-update-slice_fusion.refs_0_), channel_id=1, source_target_pairs={{0,24},{1,97},{2,26},{3,99},{4,28},{5,101},{6,30},{7,103},{8,0},{9... | collective-permute-start | bytes 3145736 | tf_op jit(solution)/shard_map/ppermute | solution.py:30
  39.1 19.7 %collective-permute-done.7.refs_3_ = bf16[2048,256]{1,0:T(8,128)(2,1)S(1)} collective-permute-done((bf16[2048,256]{1,0:T(8,128)(2,1)S(1)}, bf16[2048,256]{1,0:T(8,128)(2,1)S(1)}, u32[]{:S(2)}, u32[]{:S(2)}) %collective-permute-start.7) | collective-permute-done | bytes 1048608 | tf_op jit(solution)/shard_map/ppermute | solution.py:30
  58.8 4.0 %collective-permute-done.5.refs_1_ = bf16[2048,256]{1,0:T(8,128)(2,1)S(1)} collective-permute-done((bf16[2048,256]{1,0:T(8,128)(2,1)S(1)}, bf16[2048,256]{1,0:T(8,128)(2,1)S(1)}, u32[]{:S(2)}, u32[]{:S(2)}) %collective-permute-start.5) | collective-permute-done | bytes 1048608 | tf_op jit(solution)/shard_map/ppermute | solution.py:30
  68.0 6.8 %collective-permute-start.8 = (bf16[1024,256]{1,0:T(8,128)(2,1)S(1)}, bf16[1024,256]{1,0:T(8,128)(2,1)S(1)}, u32[]{:S(2)}, u32[]{:S(2)}) collective-permute-start(bf16[1024,256]{1,0:T(8,128)(2,1)S(1)} %convolution_convert_fusion.2), channel_id=1, source_target_pairs={{0,4},{1,5},{2,6},{3,7},{4,0},{5,1},{6,2},{7,3},{8,12},{9,13},{10,... | collective-permute-start | bytes 1572872 | tf_op jit(solution)/shard_map/ppermute | solution.py:43
  78.1 7.7 %collective-permute-done.8.far_ref = bf16[1024,256]{1,0:T(8,128)(2,1)S(1)} collective-permute-done((bf16[1024,256]{1,0:T(8,128)(2,1)S(1)}, bf16[1024,256]{1,0:T(8,128)(2,1)S(1)}, u32[]{:S(2)}, u32[]{:S(2)}) %collective-permute-start.8) | collective-permute-done | bytes 524320 | tf_op jit(solution)/shard_map/ppermute | solution.py:43
  85.8 5.5 %collective-permute-done.9.left_ref = bf16[1024,256]{1,0:T(8,128)(2,1)S(1)} collective-permute-done((bf16[1024,256]{1,0:T(8,128)(2,1)S(1)}, bf16[1024,256]{1,0:T(8,128)(2,1)S(1)}, u32[]{:S(2)}, u32[]{:S(2)}) %collective-permute-start.9) | collective-permute-done | bytes 524320 | tf_op jit(solution)/shard_map/ppermute | solution.py:43
  92.5 5.3 %shard_map.132 = (bf16[2,128,1024]{2,1,0:T(8,128)(2,1)}, bf16[2,128,1024]{2,1,0:T(8,128)(2,1)}, bf16[512,256]{1,0:T(8,128)(2,1)S(1)}) custom-call(s32[3]{0:T(128)S(1)} %pad_add_fusion.index.flag, f32[1]{0:T(128)S(6)} %tanh.3.ratio_ref, bf16[2,128,1024]{2,1,0:T(8,128)(2,1)S(1)} %copy-done.2, bf16[2,128,1024]{2,1,0:T(8,128)(2,1)S(1)} %copy-done.3, ...), custom_call_target="tpu_custom_call" | custom-call | flops 939524096 | bytes 1441792 | tf_op jit(solution)/shard_map/pallas_call | solution.py:359
  99.8 5.3 %shard_map.134 = (bf16[2,128,1024]{2,1,0:T(8,128)(2,1)}, bf16[2,128,1024]{2,1,0:T(8,128)(2,1)}, bf16[512,256]{1,0:T(8,128)(2,1)S(1)}) custom-call(s32[3]{0:T(128)S(1)} %pad_add_fusion.1.index.flag, f32[1]{0:T(128)S(6)} %tanh.3.ratio_ref, bf16[2,128,1024]{2,1,0:T(8,128)(2,1)S(1)} %copy-done.2, ...), custom_call_target="tpu_custom_call", output_to_operand_aliasing={{0}: (7, {}), {1}: (8, {})} | custom-call | flops 939524096 | bytes 1441792 | tf_op jit(solution)/shard_map/pallas_call | solution.py:359
  107.5 3.2 %collective-permute-start.17 = (bf16[512,256]{1,0:T(8,128)(2,1)S(1)}, bf16[512,256]{1,0:T(8,128)(2,1)S(1)}, u32[]{:S(2)}, u32[]{:S(2)}) collective-permute-start(bf16[512,256]{1,0:T(8,128)(2,1)S(1)} %shard_map.133.refs_4_), channel_id=1, source_target_pairs={{0,4},{1,5},{2,6},{3,7},{4,0},{5,1},{6,2},{7,3},{8,12},{9,13},{10,... | collective-permute-start | bytes 786440 | tf_op jit(solution)/shard_map/ppermute | solution.py:43
  114.4 3.2 %collective-permute-start.14 = (bf16[512,256]{1,0:T(8,128)(2,1)S(1)}, bf16[512,256]{1,0:T(8,128)(2,1)S(1)}, u32[]{:S(2)}, u32[]{:S(2)}) collective-permute-start(bf16[512,256]{1,0:T(8,128)(2,1)S(1)} %shard_map.135.refs_0_), channel_id=1, source_target_pairs={{0,4},{1,5},{2,6},{3,7},{4,0},{5,1},{6,2},{7,3},{8,12},{9,13},{10,... | collective-permute-start | bytes 786440 | tf_op jit(solution)/shard_map/ppermute | solution.py:43
  119.6 5.8 %collective-permute-done.16.refs_5_ = bf16[512,256]{1,0:T(8,128)(2,1)S(1)} collective-permute-done((bf16[512,256]{1,0:T(8,128)(2,1)S(1)}, bf16[512,256]{1,0:T(8,128)(2,1)S(1)}, u32[]{:S(2)}, u32[]{:S(2)}) %collective-permute-start.16) | collective-permute-done | bytes 262176 | tf_op jit(solution)/shard_map/ppermute | solution.py:43
  129.6 3.4 %collective-permute-done.13.refs_1_ = bf16[512,256]{1,0:T(8,128)(2,1)S(1)} collective-permute-done((bf16[512,256]{1,0:T(8,128)(2,1)S(1)}, bf16[512,256]{1,0:T(8,128)(2,1)S(1)}, u32[]{:S(2)}, u32[]{:S(2)}) %collective-permute-start.13) | collective-permute-done | bytes 262176 | tf_op jit(solution)/shard_map/ppermute | solution.py:43
  135.9 3.2 %collective-permute-start.19 = (bf16[2048,256]{1,0:T(8,128)(2,1)S(1)}, bf16[2048,256]{1,0:T(8,128)(2,1)S(1)}, u32[]{:S(2)}, u32[]{:S(2)}) collective-permute-start(bf16[2048,256]{1,0:T(8,128)(2,1)S(1)} %shard_map.137), channel_id=1, source_target_pairs={{0,16},{1,65},{2,18},{3,67},{4,20},{5,69},{6,22},{7,71},{8,24},{9,... | collective-permute-start | bytes 3145736 | tf_op jit(solution)/shard_map/ppermute | solution.py:30
  143.4 3.2 %collective-permute-start.21 = (bf16[2048,256]{1,0:T(8,128)(2,1)S(1)}, bf16[2048,256]{1,0:T(8,128)(2,1)S(1)}, u32[]{:S(2)}, u32[]{:S(2)}) collective-permute-start(bf16[2048,256]{1,0:T(8,128)(2,1)S(1)} %shard_map.140), channel_id=1, source_target_pairs={{0,24},{1,97},{2,26},{3,99},{4,28},{5,101},{6,30},{7,103},{8,0},{9... | collective-permute-start | bytes 3145736 | tf_op jit(solution)/shard_map/ppermute | solution.py:30
  146.6 5.9 %collective-permute-done.19 = bf16[2048,256]{1,0:T(8,128)(2,1)S(1)} collective-permute-done((bf16[2048,256]{1,0:T(8,128)(2,1)S(1)}, bf16[2048,256]{1,0:T(8,128)(2,1)S(1)}, u32[]{:S(2)}, u32[]{:S(2)}) %collective-permute-start.19) | collective-permute-done | bytes 1048608 | tf_op jit(solution)/shard_map/ppermute | solution.py:30
  154.4 9.1 %collective-permute-done.20 = bf16[2048,256]{1,0:T(8,128)(2,1)S(1)} collective-permute-done((bf16[2048,256]{1,0:T(8,128)(2,1)S(1)}, bf16[2048,256]{1,0:T(8,128)(2,1)S(1)}, u32[]{:S(2)}, u32[]{:S(2)}) %collective-permute-start.20) | collective-permute-done | bytes 1048608 | tf_op jit(solution)/shard_map/ppermute | solution.py:30
  167.9 4.3 %collective-permute-done.22 = bf16[512,256]{1,0:T(8,128)(2,1)S(1)} collective-permute-done((bf16[512,256]{1,0:T(8,128)(2,1)S(1)}, bf16[512,256]{1,0:T(8,128)(2,1)S(1)}, u32[]{:S(2)}, u32[]{:S(2)}) %collective-permute-start.22) | collective-permute-done | bytes 262176 | tf_op jit(solution)/shard_map/ppermute | solution.py:30
  172.8 2.7 %collective-permute-done.23 = bf16[512,256]{1,0:T(8,128)(2,1)S(1)} collective-permute-done((bf16[512,256]{1,0:T(8,128)(2,1)S(1)}, bf16[512,256]{1,0:T(8,128)(2,1)S(1)}, u32[]{:S(2)}, u32[]{:S(2)}) %collective-permute-start.23) | collective-permute-done | bytes 262176 | tf_op jit(solution)/shard_map/ppermute | solution.py:30
  175.6 5.4 %collective-permute-start.25 = (bf16[512,256]{1,0:T(8,128)(2,1)S(1)}, bf16[512,256]{1,0:T(8,128)(2,1)S(1)}, u32[]{:S(2)}, u32[]{:S(2)}) collective-permute-start(bf16[512,256]{1,0:T(8,128)(2,1)S(1)} %fusion.6), channel_id=1, source_target_pairs={{0,0},{1,1},{2,32},{3,33},{4,64},{5,65},{6,96},{7,97},{8,8},{9,9},... | collective-permute-start | bytes 786440 | tf_op jit(solution)/shard_map/ppermute | solution.py:59
  181.0 9.4 %collective-permute-done.25 = bf16[512,256]{1,0:T(8,128)(2,1)S(1)} collective-permute-done((bf16[512,256]{1,0:T(8,128)(2,1)S(1)}, bf16[512,256]{1,0:T(8,128)(2,1)S(1)}, u32[]{:S(2)}, u32[]{:S(2)}) %collective-permute-start.25) | collective-permute-done | bytes 262176 | tf_op jit(solution)/shard_map/ppermute | solution.py:59
  (74 shorter events, 54.3 us)
Async XLA Ops:
  1.8 19.1 %collective-permute-start.1 = (bf16[2,512,1024]{2,1,0:T(8,128)(2,1)}, bf16[2,512,1024]{2,1,0:T(8,128)(2,1)}, u32[]{:S(2)}, u32[]{:S(2)}) collective-permute-start(bf16[2,512,1024]{2,1,0:T(8,128)(2,1)} %own_ref), channel_id=1, source_target_pairs={{0,1},{1,0},{2,3},{3,2},{4,5},{5,4},{6,7},{7,6},{8,9},{9,8},{10,11... | collective-permute-start | bytes 6291464 | tf_op jit(solution)/shard_map/ppermute | solution.py:47
  1.9 19.0 %collective-permute-start = (bf16[512,256]{1,0:T(8,128)(2,1)S(1)}, bf16[512,256]{1,0:T(8,128)(2,1)S(1)}, u32[]{:S(2)}, u32[]{:S(2)}) collective-permute-start(bf16[512,256]{1,0:T(8,128)(2,1)S(1)} %pad_maximum_fusion), channel_id=1, source_target_pairs={{0,0},{1,1},{2,32},{3,33},{4,64},{5,65},{6,96},{7,97},{8,8},{9,9},... | collective-permute-start | bytes 786440 | tf_op jit(solution)/shard_map/ppermute | solution.py:59
  20.8 7.6 %collective-permute-start.2 = (bf16[512,256]{1,0:T(8,128)(2,1)S(1)}, bf16[512,256]{1,0:T(8,128)(2,1)S(1)}, u32[]{:S(2)}, u32[]{:S(2)}) collective-permute-start(bf16[512,256]{1,0:T(8,128)(2,1)S(1)} %collective-permute-done), channel_id=1, source_target_pairs={{0,32},{1,9},{2,34},{3,11},{4,36},{5,13},{6,38},{7,15},{8,40},{9,1... | collective-permute-start | bytes 786440 | tf_op jit(solution)/shard_map/ppermute | solution.py:30
  20.9 10.4 %collective-permute-start.3 = (bf16[512,256]{1,0:T(8,128)(2,1)S(1)}, bf16[512,256]{1,0:T(8,128)(2,1)S(1)}, u32[]{:S(2)}, u32[]{:S(2)}) collective-permute-start(bf16[512,256]{1,0:T(8,128)(2,1)S(1)} %collective-permute-done), channel_id=1, source_target_pairs={{0,64},{1,17},{2,66},{3,19},{4,68},{5,21},{6,70},{7,23},{8,72},{9,... | collective-permute-start | bytes 786440 | tf_op jit(solution)/shard_map/ppermute | solution.py:30
  24.1 8.0 %collective-permute-start.4 = (bf16[512,256]{1,0:T(8,128)(2,1)S(1)}, bf16[512,256]{1,0:T(8,128)(2,1)S(1)}, u32[]{:S(2)}, u32[]{:S(2)}) collective-permute-start(bf16[512,256]{1,0:T(8,128)(2,1)S(1)} %collective-permute-done), channel_id=1, source_target_pairs={{0,96},{1,25},{2,98},{3,27},{4,100},{5,29},{6,102},{7,31},{8,104},... | collective-permute-start | bytes 786440 | tf_op jit(solution)/shard_map/ppermute | solution.py:30
  32.2 26.6 %collective-permute-start.7 = (bf16[2048,256]{1,0:T(8,128)(2,1)S(1)}, bf16[2048,256]{1,0:T(8,128)(2,1)S(1)}, u32[]{:S(2)}, u32[]{:S(2)}) collective-permute-start(bf16[2048,256]{1,0:T(8,128)(2,1)S(1)} %constant_dynamic-update-slice_fusion.refs_0_), channel_id=1, source_target_pairs={{0,24},{1,97},{2,26},{3,99},{4,28},{5,101},{6,30},{7,103},{8,0},{9... | collective-permute-start | bytes 3145736 | tf_op jit(solution)/shard_map/ppermute | solution.py:30
  35.2 23.6 %collective-permute-start.6 = (bf16[2048,256]{1,0:T(8,128)(2,1)S(1)}, bf16[2048,256]{1,0:T(8,128)(2,1)S(1)}, u32[]{:S(2)}, u32[]{:S(2)}) collective-permute-start(bf16[2048,256]{1,0:T(8,128)(2,1)S(1)} %constant_dynamic-update-slice_fusion.refs_0_), channel_id=1, source_target_pairs={{0,16},{1,65},{2,18},{3,67},{4,20},{5,69},{6,22},{7,71},{8,24},{9,... | collective-permute-start | bytes 3145736 | tf_op jit(solution)/shard_map/ppermute | solution.py:30
  35.9 26.9 %collective-permute-start.5 = (bf16[2048,256]{1,0:T(8,128)(2,1)S(1)}, bf16[2048,256]{1,0:T(8,128)(2,1)S(1)}, u32[]{:S(2)}, u32[]{:S(2)}) collective-permute-start(bf16[2048,256]{1,0:T(8,128)(2,1)S(1)} %constant_dynamic-update-slice_fusion.refs_0_), channel_id=1, source_target_pairs={{0,8},{1,33},{2,10},{3,35},{4,12},{5,37},{6,14},{7,39},{8,16},{9,4... | collective-permute-start | bytes 3145736 | tf_op jit(solution)/shard_map/ppermute | solution.py:30
  68.0 17.7 %collective-permute-start.8 = (bf16[1024,256]{1,0:T(8,128)(2,1)S(1)}, bf16[1024,256]{1,0:T(8,128)(2,1)S(1)}, u32[]{:S(2)}, u32[]{:S(2)}) collective-permute-start(bf16[1024,256]{1,0:T(8,128)(2,1)S(1)} %convolution_convert_fusion.2), channel_id=1, source_target_pairs={{0,4},{1,5},{2,6},{3,7},{4,0},{5,1},{6,2},{7,3},{8,12},{9,13},{10,... | collective-permute-start | bytes 1572872 | tf_op jit(solution)/shard_map/ppermute | solution.py:43
  74.8 16.5 %collective-permute-start.9 = (bf16[1024,256]{1,0:T(8,128)(2,1)S(1)}, bf16[1024,256]{1,0:T(8,128)(2,1)S(1)}, u32[]{:S(2)}, u32[]{:S(2)}) collective-permute-start(bf16[1024,256]{1,0:T(8,128)(2,1)S(1)} %convolution_convert_fusion.1), channel_id=1, source_target_pairs={{0,2},{1,3},{2,4},{3,5},{4,6},{5,7},{6,0},{7,1},{8,10},{9,11},{10,... | collective-permute-start | bytes 1572872 | tf_op jit(solution)/shard_map/ppermute | solution.py:43
  74.8 16.5 %collective-permute-start.10 = (bf16[1024,256]{1,0:T(8,128)(2,1)S(1)}, bf16[1024,256]{1,0:T(8,128)(2,1)S(1)}, u32[]{:S(2)}, u32[]{:S(2)}) collective-permute-start(bf16[1024,256]{1,0:T(8,128)(2,1)S(1)} %convolution_convert_fusion), channel_id=1, source_target_pairs={{0,6},{1,7},{2,0},{3,1},{4,2},{5,3},{6,4},{7,5},{8,14},{9,15},{10,... | collective-permute-start | bytes 1572872 | tf_op jit(solution)/shard_map/ppermute | solution.py:43
  91.7 8.1 %collective-permute-start.11 = (bf16[512,256]{1,0:T(8,128)(2,1)S(1)}, bf16[512,256]{1,0:T(8,128)(2,1)S(1)}, u32[]{:S(2)}, u32[]{:S(2)}) collective-permute-start(bf16[512,256]{1,0:T(8,128)(2,1)S(1)} %get-tuple-element.35.kv_ref), channel_id=1, source_target_pairs={{0,64},{8,72},{16,80},{24,88},{32,96},{40,104},{48,112},{56,120},{... | collective-permute-start | bytes 786440 | tf_op jit(solution)/shard_map/ppermute | solution.py:17
  105.1 8.2 %collective-permute-start.12 = (bf16[512,256]{1,0:T(8,128)(2,1)S(1)}, bf16[512,256]{1,0:T(8,128)(2,1)S(1)}, u32[]{:S(2)}, u32[]{:S(2)}) collective-permute-start(bf16[512,256]{1,0:T(8,128)(2,1)S(1)} %get-tuple-element.45.grad_ref), channel_id=1, source_target_pairs={{0,64},{8,72},{16,80},{24,88},{32,96},{40,104},{48,112},{56,120},{... | collective-permute-start | bytes 786440 | tf_op jit(solution)/shard_map/ppermute | solution.py:17
  107.5 10.2 %collective-permute-start.18 = (bf16[512,256]{1,0:T(8,128)(2,1)S(1)}, bf16[512,256]{1,0:T(8,128)(2,1)S(1)}, u32[]{:S(2)}, u32[]{:S(2)}) collective-permute-start(bf16[512,256]{1,0:T(8,128)(2,1)S(1)} %shard_map.133.refs_4_), channel_id=1, source_target_pairs={{0,6},{1,7},{2,0},{3,1},{4,2},{5,3},{6,4},{7,5},{8,14},{9,15},{10,... | collective-permute-start | bytes 786440 | tf_op jit(solution)/shard_map/ppermute | solution.py:43
  107.5 12.1 %collective-permute-start.17 = (bf16[512,256]{1,0:T(8,128)(2,1)S(1)}, bf16[512,256]{1,0:T(8,128)(2,1)S(1)}, u32[]{:S(2)}, u32[]{:S(2)}) collective-permute-start(bf16[512,256]{1,0:T(8,128)(2,1)S(1)} %shard_map.133.refs_4_), channel_id=1, source_target_pairs={{0,4},{1,5},{2,6},{3,7},{4,0},{5,1},{6,2},{7,3},{8,12},{9,13},{10,... | collective-permute-start | bytes 786440 | tf_op jit(solution)/shard_map/ppermute | solution.py:43
  110.7 14.7 %collective-permute-start.16 = (bf16[512,256]{1,0:T(8,128)(2,1)S(1)}, bf16[512,256]{1,0:T(8,128)(2,1)S(1)}, u32[]{:S(2)}, u32[]{:S(2)}) collective-permute-start(bf16[512,256]{1,0:T(8,128)(2,1)S(1)} %shard_map.133.refs_4_), channel_id=1, source_target_pairs={{0,2},{1,3},{2,4},{3,5},{4,6},{5,7},{6,0},{7,1},{8,10},{9,11},{10,... | collective-permute-start | bytes 786440 | tf_op jit(solution)/shard_map/ppermute | solution.py:43
  114.1 13.9 %collective-permute-start.15 = (bf16[512,256]{1,0:T(8,128)(2,1)S(1)}, bf16[512,256]{1,0:T(8,128)(2,1)S(1)}, u32[]{:S(2)}, u32[]{:S(2)}) collective-permute-start(bf16[512,256]{1,0:T(8,128)(2,1)S(1)} %shard_map.135.refs_0_), channel_id=1, source_target_pairs={{0,6},{1,7},{2,0},{3,1},{4,2},{5,3},{6,4},{7,5},{8,14},{9,15},{10,... | collective-permute-start | bytes 786440 | tf_op jit(solution)/shard_map/ppermute | solution.py:43
  114.4 15.1 %collective-permute-start.14 = (bf16[512,256]{1,0:T(8,128)(2,1)S(1)}, bf16[512,256]{1,0:T(8,128)(2,1)S(1)}, u32[]{:S(2)}, u32[]{:S(2)}) collective-permute-start(bf16[512,256]{1,0:T(8,128)(2,1)S(1)} %shard_map.135.refs_0_), channel_id=1, source_target_pairs={{0,4},{1,5},{2,6},{3,7},{4,0},{5,1},{6,2},{7,3},{8,12},{9,13},{10,... | collective-permute-start | bytes 786440 | tf_op jit(solution)/shard_map/ppermute | solution.py:43
  117.7 15.3 %collective-permute-start.13 = (bf16[512,256]{1,0:T(8,128)(2,1)S(1)}, bf16[512,256]{1,0:T(8,128)(2,1)S(1)}, u32[]{:S(2)}, u32[]{:S(2)}) collective-permute-start(bf16[512,256]{1,0:T(8,128)(2,1)S(1)} %shard_map.135.refs_0_), channel_id=1, source_target_pairs={{0,2},{1,3},{2,4},{3,5},{4,6},{5,7},{6,0},{7,1},{8,10},{9,11},{10,... | collective-permute-start | bytes 786440 | tf_op jit(solution)/shard_map/ppermute | solution.py:43
  135.9 16.5 %collective-permute-start.19 = (bf16[2048,256]{1,0:T(8,128)(2,1)S(1)}, bf16[2048,256]{1,0:T(8,128)(2,1)S(1)}, u32[]{:S(2)}, u32[]{:S(2)}) collective-permute-start(bf16[2048,256]{1,0:T(8,128)(2,1)S(1)} %shard_map.137), channel_id=1, source_target_pairs={{0,16},{1,65},{2,18},{3,67},{4,20},{5,69},{6,22},{7,71},{8,24},{9,... | collective-permute-start | bytes 3145736 | tf_op jit(solution)/shard_map/ppermute | solution.py:30
  143.3 20.3 %collective-permute-start.20 = (bf16[2048,256]{1,0:T(8,128)(2,1)S(1)}, bf16[2048,256]{1,0:T(8,128)(2,1)S(1)}, u32[]{:S(2)}, u32[]{:S(2)}) collective-permute-start(bf16[2048,256]{1,0:T(8,128)(2,1)S(1)} %shard_map.139), channel_id=1, source_target_pairs={{0,8},{1,33},{2,10},{3,35},{4,12},{5,37},{6,14},{7,39},{8,16},{9,4... | collective-permute-start | bytes 3145736 | tf_op jit(solution)/shard_map/ppermute | solution.py:30
  143.4 20.2 %collective-permute-start.21 = (bf16[2048,256]{1,0:T(8,128)(2,1)S(1)}, bf16[2048,256]{1,0:T(8,128)(2,1)S(1)}, u32[]{:S(2)}, u32[]{:S(2)}) collective-permute-start(bf16[2048,256]{1,0:T(8,128)(2,1)S(1)} %shard_map.140), channel_id=1, source_target_pairs={{0,24},{1,97},{2,26},{3,99},{4,28},{5,101},{6,30},{7,103},{8,0},{9... | collective-permute-start | bytes 3145736 | tf_op jit(solution)/shard_map/ppermute | solution.py:30
  164.2 8.0 %collective-permute-start.22 = (bf16[512,256]{1,0:T(8,128)(2,1)S(1)}, bf16[512,256]{1,0:T(8,128)(2,1)S(1)}, u32[]{:S(2)}, u32[]{:S(2)}) collective-permute-start(bf16[512,256]{1,0:T(8,128)(2,1)S(1)} %get-tuple-element.56), channel_id=1, source_target_pairs={{0,64},{1,17},{2,66},{3,19},{4,68},{5,21},{6,70},{7,23},{8,72},{9,... | collective-permute-start | bytes 786440 | tf_op jit(solution)/shard_map/ppermute | solution.py:30
  175.6 14.9 %collective-permute-start.25 = (bf16[512,256]{1,0:T(8,128)(2,1)S(1)}, bf16[512,256]{1,0:T(8,128)(2,1)S(1)}, u32[]{:S(2)}, u32[]{:S(2)}) collective-permute-start(bf16[512,256]{1,0:T(8,128)(2,1)S(1)} %fusion.6), channel_id=1, source_target_pairs={{0,0},{1,1},{2,32},{3,33},{4,64},{5,65},{6,96},{7,97},{8,8},{9,9},... | collective-permute-start | bytes 786440 | tf_op jit(solution)/shard_map/ppermute | solution.py:59
  (7 other events, 147.7 us)
